TPU v7x, 32 devices: a whole 2x2x4 slice. The times are simulated.
32 devices in a mesh: clip: 4 (over z), ha: 4 (over y, x), wa: 2 (over core).
Axes of the slice: x: 2, y: 2, z: 4, core: 2. Of those that a mesh axis runs over, the one named last changes fastest.
Arguments:
- slow_in: float32 [4, 8, 16, 16, 1024], P('clip', None, 'ha', 'wa'), may hold values from -6 to 6
- fast_in: float32 [4, 32, 16, 16, 128], P('clip', None, 'ha', 'wa'), may hold values from -6 to 6
- valid_frames: int32 [4], replicated, may hold values from 1 to 8, as said below
- lateral_w: bfloat16 [2, 5, 128, 256], replicated, may hold values from -0.25 to 0.25
- slow_temporal_w: bfloat16 [2, 3, 1280, 256], replicated, may hold values from -0.09375 to 0.09375
- slow_spatial_w: bfloat16 [2, 3, 3, 256, 256], replicated, may hold values from -0.125 to 0.125
- slow_expand_w: bfloat16 [2, 256, 1024], replicated, may hold values from -0.375 to 0.375
- slow_skip_w: bfloat16 [2, 1280, 1024], replicated, may hold values from -0.15625 to 0.15625
- fast_temporal_w: bfloat16 [2, 3, 128, 32], replicated, may hold values from -0.3125 to 0.3125
- fast_spatial_w: bfloat16 [2, 3, 3, 32, 32], replicated, may hold values from -0.375 to 0.375
- fast_expand_w: bfloat16 [2, 32, 128], replicated, may hold values from -1 to 1
- fast_skip_w: bfloat16 [2, 128, 128], replicated, may hold values from -0.5 to 0.5
- gains: float32 [2, 3136], replicated, may hold values from 0.25 to 1.75
- biases: float32 [2, 3136], replicated, may hold values from -1.5 to 1.5
- slow_cot: float32 [4, 8, 16, 16, 1024], P('clip', None, 'ha', 'wa'), may hold values from -6 to 6
- fast_cot: float32 [4, 32, 16, 16, 128], P('clip', None, 'ha', 'wa'), may hold values from -6 to 6
Outputs:
- out_slow: float32 [4, 8, 16, 16, 1024], P('clip', None, 'ha', 'wa')
- out_fast: float32 [4, 32, 16, 16, 128], P('clip', None, 'ha', 'wa')
- grad_slow_in: float32 [4, 8, 16, 16, 1024], P('clip', None, 'ha', 'wa')
- grad_fast_in: float32 [4, 32, 16, 16, 128], P('clip', None, 'ha', 'wa')
- grad_lateral_w: float32 [2, 5, 128, 256], P(None, None, ('ha', 'wa'), 'clip')
- grad_slow_temporal_w: float32 [2, 3, 1280, 256], P(None, None, ('ha', 'wa'), 'clip')
- grad_slow_spatial_w: float32 [2, 3, 3, 256, 256], P(None, None, None, ('ha', 'wa'), 'clip')
- grad_slow_expand_w: float32 [2, 256, 1024], P(None, ('ha', 'wa'), 'clip')
- grad_slow_skip_w: float32 [2, 1280, 1024], P(None, ('ha', 'wa'), 'clip')
- grad_fast_temporal_w: float32 [2, 3, 128, 32], P(None, None, ('ha', 'wa'), 'clip')
- grad_fast_spatial_w: float32 [2, 3, 3, 32, 32], P(None, None, None, ('ha', 'wa'), 'clip')
- grad_fast_expand_w: float32 [2, 32, 128], P(None, ('ha', 'wa'), 'clip')
- grad_fast_skip_w: float32 [2, 128, 128], P(None, ('ha', 'wa'), 'clip')
- grad_gains: float32 [2, 3136], replicated
- grad_biases: float32 [2, 3136], replicated
Inputs may be any that keep to these rules, and one draw needn't show every extreme that they name: valid_frames[c] sets the masks and counts of the steps for clip c; the last clip has all 8.
All inputs are finite; a program needn't handle non-finite values.
Results may differ from a plain program's by a relative error of at most 0.024.
Values may be sent and summed in bfloat16 or wider, within the bound.
No kernel may reach another device: no remote copies, remote signals or barrier semaphores. Data moves between devices by JAX's collectives and lax.ppermute only.
A program may use at most 256 MiB of HBM per device.

v0:
```python
import functools

import jax
import jax.numpy as jnp
from jax import lax
from jax.experimental import pallas as pl
from jax.experimental.pallas import tpu as pltpu
from jax.sharding import PartitionSpec as P

DS = 1024
DL = 256
BS = 256
DF = 128
BF = 32
ST = 8
ALPHA = 4
HT = 16
WD = 16
LAYERS = 2
CC = DS + DL
EPSILON = 1e-05
LANES = 128
CLIP, HA, WA = "clip", "ha", "wa"
ALL_AXES = (CLIP, HA, WA)


LAT, STM, SSP, SEX, SSK, FTM, FSP, FEX, FSK = 0, 2, 4, 6, 14, 22, 23, 24, 25
GB_ROWS = 32

F32 = jnp.float32
BF16 = jnp.bfloat16


def dot(a, b):
    return jnp.dot(a, b, preferred_element_type=F32)


def dot_nt(a, b):
    return lax.dot_general(a, b, (((1,), (1,)), ((), ())), preferred_element_type=F32)


def dot_tn(a, b):
    return lax.dot_general(a, b, (((0,), (0,)), ((), ())), preferred_element_type=F32)


def sigmoid(v):
    return 0.5 * jnp.tanh(0.5 * v) + 0.5


def silu(v):
    return v * sigmoid(v)


def slope(v):
    s = sigmoid(v)
    return s + v * s * (1.0 - s)


def silu_and_slope(v):
    s = sigmoid(v)
    act = v * s
    return act, s + act * (1.0 - s)


def wide(tile, row, count):
    if count == 1:
        return tile[row : row + 1, :]
    return jnp.concatenate([tile[row + i : row + i + 1, :] for i in range(count)], axis=1)


def fold_phases(tile):
    return tile + pltpu.roll(tile, 32, 1) + pltpu.roll(tile, 64, 1) + pltpu.roll(tile, 96, 1)


def down(x, frame):
    return jnp.concatenate([jnp.zeros_like(x[:frame]), x[:-frame]], axis=0)


def up(x, frame):
    return jnp.concatenate([x[frame:], jnp.zeros_like(x[:frame])], axis=0)


def col_sum(x):
    return jnp.sum(x, axis=0, keepdims=True)


class Norm:
    def __init__(self, total, row, gb, gb_row, count, inv_count):
        mean = wide(total, row, count) * inv_count
        square = wide(total, row + count, count) * inv_count
        self.mean = mean
        self.rstd = lax.rsqrt(square - mean * mean + EPSILON)
        self.gain = wide(gb[0], gb_row, count)
        self.bias = wide(gb[1], gb_row, count)
        self.scale = self.gain * self.rstd
        self.shift = self.bias - mean * self.scale

    def columns(self, start, size):
        other = object.__new__(Norm)
        for name in ("mean", "rstd", "gain", "bias", "scale", "shift"):
            setattr(other, name, getattr(self, name)[:, start : start + size])
        return other

    def out(self, z):
        return z * self.scale + self.shift

    def hat(self, z):
        return (z - self.mean) * self.rstd

    def back(self, dy, hat, inside, a_sum, b_sum, inv_count):
        return self.scale * (dy - jnp.where(inside, a_sum * inv_count + hat * (b_sum * inv_count), 0.0))


def inside_rows(rows, columns, limit):
    return lax.broadcasted_iota(jnp.int32, (rows, columns), 0) < limit


def moments(z, inside):
    masked = jnp.where(inside, z, 0.0)
    return col_sum(masked), col_sum(masked * z)


def put_rows(ref, row, vector):
    for i in range(vector.shape[1] // LANES):
        ref[row + i : row + i + 1, :] = vector[:, i * LANES : (i + 1) * LANES]


def spread(tile, ref):
    def body(i, carry):
        ref[i] = tile[...]
        return carry

    lax.fori_loop(0, ref.shape[0], body, 0)


def gathered(ref):
    return jnp.sum(ref[...], axis=0)


def phase(ref, p):
    return ref[:, p].reshape(ref.shape[0] * ref.shape[2], ref.shape[3])


def send_halo(z, shape, si, whole, one, two):
    t, h, w = shape
    columns = z.shape[1]
    four = z.reshape(t, h, w, columns)
    whole[...] = z.astype(BF16)
    top, bottom = (four[:, i].reshape(t * w, columns) for i in (0, h - 1))
    if one.dtype == BF16:
        one[...] = top.astype(BF16)
        two[...] = bottom.astype(BF16)
        return
    even = jnp.full((t * w, columns), si[1] % 2, jnp.int32) == 0
    base = one.shape[0] - t * w * columns // LANES
    for ref, value in ((one, jnp.where(even, bottom, top)), (two, jnp.where(even, top, bottom))):
        for i in range(columns // LANES):
            ref[base + i * t * w : base + (i + 1) * t * w, :] = value[:, i * LANES : (i + 1) * LANES]


def send_sums(pay, one, two):
    if one.dtype == F32:
        for ref in (one, two):
            ref[: pay.shape[0], :] = pay[...]


def halo_values(si, edge, refs):
    one, two, other, o_one, o_two = refs
    if one.dtype == BF16:
        return [ref[...].astype(F32) for ref in (one, two, o_one, other, o_two)]
    columns = other.shape[1]
    base = one.shape[0] - edge * columns // LANES

    def rows(ref):
        parts = [ref[base + i * edge : base + (i + 1) * edge, :] for i in range(columns // LANES)]
        return jnp.concatenate(parts, axis=1) if len(parts) > 1 else parts[0]

    even = jnp.full((edge, columns), si[1] % 2, jnp.int32) == 0
    one, two, o_one, o_two = (rows(ref) for ref in (one, two, o_one, o_two))
    return [
        jnp.where(even, two, one), jnp.where(even, one, two),
        jnp.where(even, o_two, o_one), other[...].astype(F32), jnp.where(even, o_one, o_two),
    ]


def fill_padded(pad, shape, own, above, below, others, has_left, has_right):
    t, h, w = shape
    c = own.shape[1]
    pad[:, 1 : h + 1, w : 2 * w, :] = own.reshape(t, h, w, c)
    pad[:, 0, w : 2 * w, :] = above.reshape(t, w, c)
    pad[:, h + 1, w : 2 * w, :] = below.reshape(t, w, c)
    o_above, o_own, o_below = others
    for start, has in ((0, has_left), (2 * w, has_right)):
        pad[:, 1 : h + 1, start : start + w, :] = (o_own * has).reshape(t, h, w, c)
        pad[:, 0, start : start + w, :] = (o_above * has).reshape(t, w, c)
        pad[:, h + 1, start : start + w, :] = (o_below * has).reshape(t, w, c)


def tap(pad, shape, a, b):
    t, h, w = shape
    part = pad[:, a : a + h, w - 1 + b : 2 * w - 1 + b, :]
    return part.reshape(t * h * w, part.shape[-1]).astype(BF16)


def activate_padded(pad, shape, norm, own, halo_refs, si, sf):
    def act(z):
        return silu(norm.out(z.astype(F32))).astype(BF16).astype(F32)

    edge = shape[0] * shape[2]
    above, below, o_above, o_own, o_below = (act(x) for x in halo_values(si, edge, halo_refs))
    has_up, has_down = sf[2], sf[3]
    others = (o_above * has_up, o_own, o_below * has_down)
    fill_padded(pad, shape, act(own), above * has_up, below * has_down, others, sf[4], sf[5])


def fast_head(phases, shape, si, inside, lat_w, ft_band, fk_w, fb_out, zlat_out, zft_out, halo_out, zfk_out, pay, row):
    frame = shape[1] * shape[2]
    low = [v.astype(BF16) for v in phases]
    for p in range(ALPHA):
        fb_out[:, p * DF : (p + 1) * DF] = low[p]
    before2, before3, after0 = down(low[2], frame), down(low[3], frame), up(low[0], frame)
    z = (
        dot(before2, lat_w[0, 0])
        + dot(before3, lat_w[0, 1])
        + dot(low[0], lat_w[0, 2])
        + dot(low[1], lat_w[0, 3])
        + dot(low[2], lat_w[0, 4])
    )
    zlat_out[...] = z
    total, square = moments(z, inside[:, :DL])
    put_rows(pay, row, total)
    put_rows(pay, row + 2, square)
    six = [before3] + low + [after0]
    z = dot(six[0], ft_band[0])
    for j in range(1, 6):
        z = z + dot(six[j], ft_band[j])
    zft_out[...] = z
    send_halo(z, shape, si, *halo_out)
    total, square = moments(z, inside[:, :LANES])
    put_rows(pay, row + 4, total)
    put_rows(pay, row + 5, square)
    total, square = 0.0, 0.0
    for p in range(ALPHA):
        z = dot(low[p], fk_w[0])
        zfk_out[:, p * DF : (p + 1) * DF] = z
        one, two = moments(z, inside[:, :LANES])
        total, square = total + one, square + two
    put_rows(pay, row + 6, total)
    put_rows(pay, row + 7, square)


def place_columns(p):
    row = lax.broadcasted_iota(jnp.int32, (BF, LANES), 0)
    column = lax.broadcasted_iota(jnp.int32, (BF, LANES), 1)
    return jnp.where(column == row + BF * p, 1.0, 0.0).astype(BF16)


def kernel_start(shape, si, sf, fast, lat_w, ft_w, fk_w, fb, zlat, zft, z16, top, bottom, zfk, pay, ft_band):
    t, h, w = shape
    inside = inside_rows(t * h * w, DL, si[0])
    places = [place_columns(p) for p in range(ALPHA)]
    for l in range(LAYERS):
        for j in range(6):
            part = 0.0
            for p in range(ALPHA):
                if 0 <= j - p <= 2:
                    part = part + dot_tn(ft_w[l, j - p], places[p])
            ft_band[l, j] = part.astype(BF16)
    fast_head(
        [phase(fast, p) for p in range(ALPHA)],
        shape, si, inside, lat_w, ft_band.at[0], fk_w, fb, zlat, zft, (z16, top, bottom), zfk, pay, 0,
    )
    send_sums(pay, top, bottom)


def lane(shape):
    return lax.broadcasted_iota(jnp.int32, shape, len(shape) - 1)


def kernel_prepare(gains, biases, fs_w, fe_w, gb, fs_bd, fe_bd):
    for i, source in enumerate((gains, biases)):
        for l in range(LAYERS):
            for r in range(22):
                gb[l, i, r : r + 1, :] = source[l : l + 1, r * LANES : (r + 1) * LANES]
            v = source[l : l + 1, 22 * LANES : 23 * LANES]
            v2 = source[l : l + 1, 23 * LANES : 24 * LANES]
            v3 = jnp.concatenate([source[l : l + 1, 24 * LANES :], jnp.zeros((1, 64), F32)], axis=1)
            place = lane((1, LANES))
            gb[l, i, FTM : FTM + 1, :] = fold_phases(jnp.where(place < 32, v, 0.0))
            gb[l, i, FSP : FSP + 1, :] = fold_phases(jnp.where((place >= 32) & (place < 64), v, 0.0))
            v, v2, v3 = (pltpu.roll(x, 64, 1) for x in (v, v2, v3))
            gb[l, i, FEX : FEX + 1, :] = jnp.where(place < 64, v, v2)
            gb[l, i, FSK : FSK + 1, :] = jnp.where(place < 64, v2, v3)
            gb[l, i, 26:32, :] = jnp.zeros((6, LANES), F32)
    row = lax.broadcasted_iota(jnp.int32, (LANES, LANES), 0)
    column = lane((LANES, LANES))
    same = (row // BF) == (column // BF)
    spread_columns = 0.0
    for p in range(ALPHA):
        spread_columns = spread_columns + place_columns(p).astype(F32)
    spread_columns = spread_columns.astype(BF16)
    for l in range(LAYERS):
        for a in range(3):
            for b in range(3):
                part = dot(fs_w[l, a, b], spread_columns).astype(BF16)
                fs_bd[l, a, b] = jnp.where(same, dot_tn(spread_columns, part), 0.0).astype(BF16)
        fe_bd[l] = jnp.zeros((LANES, ALPHA * DF), BF16)
        for p in range(ALPHA):
            fe_bd[l, p * BF : (p + 1) * BF, p * DF : (p + 1) * DF] = fe_w[l]


def kernel_temporal(first, shape, si, sf, *refs):
    t, h, w = shape
    rows, frame = t * h * w, h * w
    if first:
        (recv, slow, gb, zlat, zft, h1, h2, h3, h4, h5, st_w, sk_w, fs_bd,
         low_out, zst, z16, top, bottom, zsk, af9, zfs, pay, pad) = refs
        row = 0
        total = recv[...]
    else:
        (recv, gb_before, tot_sk, zse_in, zsk_in, gb, zlat, zft, h1, h2, h3, h4, h5, st_w, sk_w, fs_bd,
         low_out, zst, z16, top, bottom, zsk, af9, zfs, pay, pad) = refs
        row = 16
        total = recv[...]
        inside = inside_rows(rows, 256, si[0])
        one = Norm(total, 0, gb_before, SEX, 8, sf[0])
        two = Norm(tot_sk[...], 8, gb_before, SSK, 8, sf[0])
        for c in range(0, DS, 256):
            u = one.columns(c, 256).out(zse_in[:, c : c + 256]) + two.columns(c, 256).out(zsk_in[:, c : c + 256])
            low_out[:, c : c + 256] = jnp.where(inside, silu(u), 0.0).astype(BF16)
    inside = inside_rows(rows, 256, si[0])
    lat = Norm(total, row, gb, LAT, 2, sf[0])
    ft = Norm(fold_phases(total), row + 4, gb, FTM, 1, sf[1])
    if first:
        low_out[:, :DS] = slow[...].astype(BF16)
    low_out[:, DS:] = silu(lat.out(zlat[...])).astype(BF16)
    activate_padded(pad, shape, ft, zft[...], (h1, h2, h3, h4, h5), si, sf)
    low = low_out[...]
    z = dot(low, st_w[0, 1])
    z = z + down(dot(low, st_w[0, 0]), frame)
    z = z + up(dot(low, st_w[0, 2]), frame)
    zst[...] = z
    send_halo(z, shape, si, z16, top, bottom)
    one, two = moments(z, inside)
    put_rows(pay, 0, one)
    put_rows(pay, 2, two)
    for a in range(3):
        for b in range(3):
            k = 3 * a + b
            af9[:, k * LANES : (k + 1) * LANES] = tap(pad, shape, a, b)
    z = dot(af9[...], fs_bd[...].reshape(9 * LANES, LANES))
    zfs[...] = z
    one, two = moments(z, inside[:, :LANES])
    put_rows(pay, 4, one)
    put_rows(pay, 5, two)
    pay[6:8, :] = jnp.zeros((2, LANES), F32)
    for c in range(0, DS, 256):
        z = dot(low, sk_w[0, :, c : c + 256])
        zsk[:, c : c + 256] = z
        one, two = moments(z, inside)
        put_rows(pay, 8 + c // LANES, one)
        put_rows(pay, 16 + c // LANES, two)
    send_sums(pay, top, bottom)


def kernel_spatial(shape, si, sf, recv, gb, zst, h1, h2, h3, h4, h5, zfs, ss_w, fe_bd,
                   a9, zss, bf, zfe, pays, pay, pad):
    t, h, w = shape
    inside = inside_rows(t * h * w, 256, si[0])
    total = recv[...]
    st = Norm(total, 0, gb, STM, 2, sf[0])
    fs = Norm(fold_phases(total), 4, gb, FSP, 1, sf[1])
    activate_padded(pad, shape, st, zst[...], (h1, h2, h3, h4, h5), si, sf)
    for a in range(3):
        for b in range(3):
            k = 3 * a + b
            a9[:, k * BS : (k + 1) * BS] = tap(pad, shape, a, b)
    z = dot(a9[...], ss_w[...].reshape(9 * BS, BS))
    zss[...] = z
    one, two = moments(z, inside)
    put_rows(pay, 0, one)
    put_rows(pay, 2, two)
    low = silu(fs.out(zfs[...])).astype(BF16)
    bf[...] = low
    total, square = 0.0, 0.0
    for p in range(ALPHA):
        z = dot(low, fe_bd[:, p * DF : (p + 1) * DF])
        zfe[:, p * DF : (p + 1) * DF] = z
        one, two = moments(z, inside[:, :LANES])
        total, square = total + one, square + two
    put_rows(pay, 4, total)
    put_rows(pay, 5, square)
    pay[6:8, :] = jnp.zeros((2, LANES), F32)
    spread(pay, pays)


def kernel_expand(last, shape, si, sf, *refs):
    t, h, w = shape
    inside = inside_rows(t * h * w, 256, si[0])
    if last:
        recv, gb, zss, se_w, bt, zse, pays, tot_out, pay = refs
    else:
        (recv, gb, zss, se_w, tot_fk, zfe, zfk, lat_w, ft_band, fk_w,
         bt, zse, pay, tot_out, fb, zlat, zft, z16, top, bottom, zfk_out) = refs
    total = gathered(recv)
    tot_out[...] = total
    ss = Norm(total, 0, gb, SSP, 2, sf[0])
    low = silu(ss.out(zss[...])).astype(BF16)
    bt[...] = low
    for c in range(0, DS, 256):
        z = dot(low, se_w[0, :, c : c + 256])
        zse[:, c : c + 256] = z
        one, two = moments(z, inside)
        put_rows(pay, c // LANES, one)
        put_rows(pay, 8 + c // LANES, two)
    if not last:
        fe = Norm(total, 4, gb, FEX, 1, sf[1])
        fk = Norm(tot_fk[...], tot_fk.shape[0] - 2, gb, FSK, 1, sf[1])
        phases = []
        for p in range(ALPHA):
            cols = slice(p * DF, (p + 1) * DF)
            u = fe.out(zfe[:, cols]) + fk.out(zfk[:, cols])
            phases.append(jnp.where(inside[:, :LANES], silu(u), 0.0))
        fast_head(
            phases, shape, si, inside, lat_w, ft_band, fk_w, fb, zlat, zft, (z16, top, bottom), zfk_out, pay, 16
        )
        send_sums(pay, top, bottom)
    else:
        spread(pay, pays)


class Refs:
    def __init__(self, names, refs):
        self.__dict__.update(zip(names, refs))

    def layer(self, prefix):
        own = {k[len(prefix) :]: v for k, v in self.__dict__.items() if k.startswith(prefix)}
        return Refs(own.keys(), own.values())


def norms_of(L, sf, *names):
    def make(name):
        if name == "se":
            return Norm(L.tot_se[...], 0, L.gb, SEX, 8, sf[0])
        if name == "sk":
            return Norm(L.tot_sk[...], 8, L.gb, SSK, 8, sf[0])
        if name == "ss":
            return Norm(L.tot_ss[...], 0, L.gb, SSP, 2, sf[0])
        if name == "st":
            return Norm(L.tot_sk[...], 0, L.gb, STM, 2, sf[0])
        if name == "lat":
            return Norm(L.tot_lat[...], L.tot_lat.shape[0] - 8, L.gb, LAT, 2, sf[0])
        if name == "ft":
            return Norm(fold_phases(L.tot_lat[...]), L.tot_lat.shape[0] - 4, L.gb, FTM, 1, sf[1])
        if name == "fk":
            return Norm(L.tot_lat[...], L.tot_lat.shape[0] - 2, L.gb, FSK, 1, sf[1])
        if name == "fs":
            return Norm(fold_phases(L.tot_sk[...]), 4, L.gb, FSP, 1, sf[1])
        return Norm(L.tot_ss[...], 4, L.gb, FEX, 1, sf[1])

    return [make(name) for name in names]


def fill_rows(pay, start, end):
    pay[start:end, :] = jnp.zeros((end - start, LANES), F32)


def top_slow(L, inside, sf, grad, du_out, pay, row, out=None):
    se, sk = norms_of(L, sf, "se", "sk")
    for c in range(0, DS, 256):
        cols = slice(c, c + 256)
        one, two = se.columns(c, 256), sk.columns(c, 256)
        hat1, hat2 = one.hat(L.zse[:, cols]), two.hat(L.zsk[:, cols])
        u = one.gain * hat1 + one.bias + (two.gain * hat2 + two.bias)
        act, rate = silu_and_slope(u)
        if out is not None:
            out[:, cols] = jnp.where(inside, act, 0.0)
        du = jnp.where(inside, grad(cols) * rate, 0.0)
        du_out[:, cols] = du
        put_rows(pay, row + c // LANES, col_sum(du))
        put_rows(pay, row + 8 + c // LANES, col_sum(du * hat1))
        put_rows(pay, row + 16 + c // LANES, col_sum(du * hat2))


def top_fast(L, inside, sf, grad, du_out, pay, row, out=None):
    fe, fk = norms_of(L, sf, "fe", "fk")
    inside = inside[:, :LANES]
    sums = [0.0, 0.0, 0.0]
    for p in range(ALPHA):
        cols = slice(p * DF, (p + 1) * DF)
        hat1, hat2 = fe.hat(L.zfe[:, cols]), fk.hat(L.zfk[:, cols])
        u = fe.gain * hat1 + fe.bias + (fk.gain * hat2 + fk.bias)
        act, rate = silu_and_slope(u)
        if out is not None:
            out[:, p] = jnp.where(inside, act, 0.0).reshape(out.shape[0], out.shape[2], DF)
        du = jnp.where(inside, grad(p) * rate, 0.0)
        du_out[:, cols] = du
        sums = [sums[0] + col_sum(du), sums[1] + col_sum(du * hat1), sums[2] + col_sum(du * hat2)]
    for i in range(3):
        put_rows(pay, row + i, sums[i])


def expand_slow(L, inside, sf, total, row, du_in, se_w, dz_se, dz_sk, pay, out_row):
    se, sk, ss = norms_of(L, sf, "se", "sk", "ss")
    back = 0.0
    for c in range(0, DS, 256):
        cols = slice(c, c + 256)
        r = row + c // LANES
        du = du_in[:, cols]
        a_sum = wide(total, r, 2)
        one, two = se.columns(c, 256), sk.columns(c, 256)
        dz = one.back(du, one.hat(L.zse[:, cols]), inside, a_sum, wide(total, 8 + r, 2), sf[0]).astype(BF16)
        dz_se[:, cols] = dz
        back = back + dot_nt(dz, se_w[0, :, cols])
        dz = two.back(du, two.hat(L.zsk[:, cols]), inside, a_sum, wide(total, 16 + r, 2), sf[0])
        dz_sk[:, cols] = dz.astype(BF16)
    z = L.zss[...]
    dy = back * slope(ss.out(z))
    put_rows(pay, out_row, col_sum(dy))
    put_rows(pay, out_row + 2, col_sum(dy * ss.hat(z)))
    return dy, z


def expand_fast(L, inside, sf, total, row, du_in, fe_bd, dz_fe, dz_fk, pay, out_row):
    fe, fk, fs = norms_of(L, sf, "fe", "fk", "fs")
    inside = inside[:, :LANES]
    back = 0.0
    a_sum = wide(total, row, 1)
    for p in range(ALPHA):
        cols = slice(p * DF, (p + 1) * DF)
        du = du_in[:, cols]
        dz = fe.back(du, fe.hat(L.zfe[:, cols]), inside, a_sum, wide(total, row + 1, 1), sf[1]).astype(BF16)
        dz_fe[:, cols] = dz
        back = back + dot_nt(dz, fe_bd[:, cols])
        dz = fk.back(du, fk.hat(L.zfk[:, cols]), inside, a_sum, wide(total, row + 2, 1), sf[1])
        dz_fk[:, cols] = dz.astype(BF16)
    z = L.zfs[...]
    dy = back * slope(fs.out(z))
    put_rows(pay, out_row, col_sum(dy))
    put_rows(pay, out_row + 1, col_sum(dy * fs.hat(z)))
    return dy, z


def pack_halo(pairs, shape, si, dy_out, halo_out):
    dy = jnp.concatenate([one for one, _ in pairs], axis=1) if len(pairs) > 1 else pairs[0][0]
    dy_out[...] = dy
    send_halo(jnp.concatenate([dy] + [z for _, z in pairs], axis=1), shape, si, *halo_out)


def spatial_gradient(parts, shape, si, sf, dy_in, halo_refs, pad, dz_out):
    t, h, w = shape
    width = dy_in.shape[1]

    def dz(dy, z, frame):
        inside = inside_rows(dy.shape[0], width, si[0] // (h * w) * frame)
        pieces, column = [], 0
        for norm, _, a_sum, b_sum, inv in parts:
            cols = slice(column, column + norm.mean.shape[1])
            pieces.append(norm.back(dy[:, cols], norm.hat(z[:, cols]), inside[:, cols], a_sum, b_sum, inv))
            column = cols.stop
        value = jnp.concatenate(pieces, axis=1) if len(pieces) > 1 else pieces[0]
        return value.astype(BF16)

    def arrived(value, frame):
        return dz(value[:, :width], value[:, width:], frame).astype(F32)

    z = jnp.concatenate([part[1] for part in parts], axis=1) if len(parts) > 1 else parts[0][1]
    own = dz(dy_in[...], z, h * w)
    dz_out[...] = own
    above, below, o_above, o_own, o_below = (
        arrived(x, h * w if i == 3 else w) for i, x in enumerate(halo_values(si, t * w, halo_refs))
    )
    others = (o_above * sf[2], o_own, o_below * sf[3])
    fill_padded(pad, shape, own.astype(F32), above * sf[2], below * sf[3], others, sf[4], sf[5])


def spatial_part(norm, z, total, row, columns, inv):
    count = columns // LANES
    if columns == LANES:
        total = fold_phases(total)
    return norm, z, wide(total, row, count), wide(total, row + count, count), inv


def spatial_back(pad, shape, slow_w, fast_w):
    back, back_f = 0.0, 0.0
    for a in range(3):
        for b in range(3):
            part = tap(pad, shape, 2 - a, 2 - b)
            if slow_w is not None:
                back = back + dot_nt(part[:, :BS], slow_w[0, a, b])
            if fast_w is not None:
                back_f = back_f + dot_nt(part[:, part.shape[1] - LANES :], fast_w[a, b])
    return back, back_f


def finish_spatial(norm, z, back, dy_out, pay, row):
    dy = back * slope(norm.out(z))
    dy_out[...] = dy
    put_rows(pay, row, col_sum(dy))
    put_rows(pay, row + dy.shape[1] // LANES, col_sum(dy * norm.hat(z)))


def temporal_slow(L, frame, inside, sf, total, row, dy_in, dlow, st_w, dz_st, dy_lat, pay, out_row):
    st, lat = norms_of(L, sf, "st", "lat")
    dz = st.back(
        dy_in[...], st.hat(L.zst[...]), inside, wide(total, row, 2), wide(total, row + 2, 2), sf[0]
    ).astype(BF16)
    dz_st[:, :BS] = up(dz, frame)
    dz_st[:, BS : 2 * BS] = dz
    dz_st[:, 2 * BS :] = down(dz, frame)

    def back(cols):
        part = dlow[:, cols]
        for j in range(3):
            part = part + dot_nt(dz_st[:, j * BS : (j + 1) * BS], st_w[0, j, cols, :])
        return part

    z = L.zlat[...]
    dy = back(slice(DS, CC)) * slope(lat.out(z))
    dy_lat[...] = dy
    put_rows(pay, out_row, col_sum(dy))
    put_rows(pay, out_row + 2, col_sum(dy * lat.hat(z)))
    return back


def temporal_fast(L, frame, inside, sf, total, row, dy_in, dz_ft, dz_fk, fk_w, ft_band):
    (ft,) = norms_of(L, sf, "ft")
    folded = fold_phases(total)
    dz = ft.back(
        dy_in[...], ft.hat(L.zft[...]), inside[:, :LANES], wide(folded, row, 1), wide(folded, row + 1, 1), sf[1]
    ).astype(BF16)
    dz_ft[...] = dz

    def grad(p):
        part = dot_nt(dz_fk[:, p * DF : (p + 1) * DF], fk_w[0]) + dot_nt(dz, ft_band[p + 1])
        if p == ALPHA - 1:
            part = part + up(dot_nt(dz, ft_band[0]), frame)
        if p == 0:
            part = part + down(dot_nt(dz, ft_band[5]), frame)
        return part

    return grad


def lateral_back(L, frame, inside, sf, total, row, dy_in, lat_w, dz_lat, grad):
    (lat,) = norms_of(L, sf, "lat")
    dz = lat.back(
        dy_in[...], lat.hat(L.zlat[...]), inside, wide(total, row, 2), wide(total, row + 2, 2), sf[0]
    ).astype(BF16)
    dz_lat[...] = dz

    def whole(p):
        part = grad(p)
        if p < 3:
            part = part + dot_nt(dz, lat_w[0, p + 2])
        if p >= 2:
            part = part + up(dot_nt(dz, lat_w[0, p - 2]), frame)
        return part

    return whole


def back_turn(shape, R, inside, si, sf):
    L = R.layer("a_")
    L.tot_se = R.tot
    R.tot[...] = gathered(R.recv)
    top_slow(L, inside, sf, lambda cols: R.slow_cot[:, cols], R.du_s, R.pay, 0, R.out_slow)
    top_fast(L, inside, sf, lambda p: phase(R.fast_cot, p), R.du_f, R.pay, 24, R.out_fast)
    fill_rows(R.pay, 27, 32)


def back_expand(shape, R, inside, si, sf):
    L = R.layer("a_")
    total = R.recv[...]
    slow = expand_slow(L, inside, sf, total, 0, R.du_s, R.se_w, R.dz_se, R.dz_sk, R.pay, 0)
    fast = expand_fast(L, inside, sf, total, 24, R.du_f, R.fe_bd, R.dz_fe, R.dz_fk, R.pay, 4)
    fill_rows(R.pay, 6, 8)
    pack_halo([slow, fast], shape, si, R.dy, (R.whole, R.top, R.bottom))
    send_sums(R.pay, R.top, R.bottom)


def back_spatial(shape, R, inside, si, sf):
    L = R.layer("a_")
    total = R.recv[...]
    ss, fs, st, ft = norms_of(L, sf, "ss", "fs", "st", "ft")
    parts = [
        spatial_part(ss, L.zss[...], total, 0, BS, sf[0]),
        spatial_part(fs, L.zfs[...], total, 4, LANES, sf[1]),
    ]
    spatial_gradient(parts, shape, si, sf, R.dy, (R.h0, R.h1, R.h2, R.h3, R.h4), R.pad, R.dz)
    back, back_f = spatial_back(R.pad, shape, R.ss_w, R.fs_bd)
    finish_spatial(st, L.zst[...], back, R.dy_st, R.pay, 0)
    finish_spatial(ft, L.zft[...], back_f, R.dy_ft, R.pay, 4)
    fill_rows(R.pay, 6, 8)


def back_temporal(shape, R, inside, si, sf):
    L, below = R.layer("a_"), R.layer("b_")
    frame = shape[1] * shape[2]
    total = R.recv[...]
    back = temporal_slow(L, frame, inside, sf, total, 0, R.dy_st, R.dlow, R.st_w, R.dz_st, R.dy_lat, R.pay, 0)
    top_slow(below, inside, sf, back, R.du_s, R.pay, 8)
    fill_rows(R.pay, 4, 8)
    grad = temporal_fast(L, frame, inside, sf, total, 4, R.dy_ft, R.dz_ft, R.dz_fk, R.fk_w, R.ft_band)
    for p in range(ALPHA):
        R.dfast[:, p * DF : (p + 1) * DF] = grad(p)


def back_lateral(shape, R, inside, si, sf):
    L, below = R.layer("a_"), R.layer("b_")
    frame = shape[1] * shape[2]
    total = R.recv[...]
    slow = expand_slow(below, inside, sf, total, 8, R.du_s, R.se_w, R.dz_se, R.dz_sk, R.pay, 0)
    pack_halo([slow], shape, si, R.dy, (R.whole, R.top, R.bottom))
    grad = lateral_back(
        L, frame, inside, sf, total, 0, R.dy_lat, R.lat_w, R.dz_lat, lambda p: R.dfast[:, p * DF : (p + 1) * DF]
    )
    top_fast(below, inside, sf, grad, R.du_f, R.pay, 4)
    fill_rows(R.pay, 7, 8)
    send_sums(R.pay, R.top, R.bottom)


def back_low_spatial(shape, R, inside, si, sf):
    L = R.layer("b_")
    total = R.recv[...]
    fast = expand_fast(L, inside, sf, total, 4, R.du_f, R.fe_bd, R.dz_fe, R.dz_fk, R.pay, 4)
    pack_halo([fast], shape, si, R.dy_fs, (R.whole, R.top, R.bottom))
    ss, st = norms_of(L, sf, "ss", "st")
    parts = [spatial_part(ss, L.zss[...], total, 0, BS, sf[0])]
    spatial_gradient(parts, shape, si, sf, R.dy, (R.h0, R.h1, R.h2, R.h3, R.h4), R.pad, R.dz)
    back, _ = spatial_back(R.pad, shape, R.ss_w, None)
    finish_spatial(st, L.zst[...], back, R.dy_st, R.pay, 0)
    fill_rows(R.pay, 6, 8)
    send_sums(R.pay, R.top, R.bottom)


def back_low_temporal(shape, R, inside, si, sf):
    L = R.layer("b_")
    frame = shape[1] * shape[2]
    total = R.recv[...]
    fs, ft = norms_of(L, sf, "fs", "ft")
    parts = [spatial_part(fs, L.zfs[...], total, 4, LANES, sf[1])]
    spatial_gradient(parts, shape, si, sf, R.dy_fs, (R.h0, R.h1, R.h2, R.h3, R.h4), R.pad, R.dz_f)
    _, back_f = spatial_back(R.pad, shape, None, R.fs_bd)
    finish_spatial(ft, L.zft[...], back_f, R.dy_ft, R.pay, 4)
    back = temporal_slow(L, frame, inside, sf, total, 0, R.dy_st, R.dlow, R.st_w, R.dz_st, R.dy_lat, R.pay, 0)
    fill_rows(R.pay, 6, 8)
    for c in range(0, DS, 256):
        R.dslow[:, c : c + 256] = back(slice(c, c + 256))


def back_low_lateral(shape, R, inside, si, sf):
    L = R.layer("b_")
    frame = shape[1] * shape[2]
    total = R.recv[...]
    grad = temporal_fast(L, frame, inside, sf, total, 4, R.dy_ft, R.dz_ft, R.dz_fk, R.fk_w, R.ft_band)
    grad = lateral_back(L, frame, inside, sf, total, 0, R.dy_lat, R.lat_w, R.dz_lat, grad)
    for p in range(ALPHA):
        R.dfast[:, p] = grad(p).reshape(shape[0], frame, DF)


def kernel_back_skip(dz_sk, sk_w, dlow):
    for k in range(0, CC, 256):
        dlow[:, k : k + 256] = dot_nt(dz_sk[...], sk_w[0, k : k + 256, :])


def part_tiles(si, tiles, ref, keep, send):
    side = si[2]
    for i in range(tiles // 2):
        keep[i] = ref[2 * i + side]
        send[i] = ref[2 * i + 1 - side]


def pick_phases(parts):
    place = lane(parts[0].shape) // BF
    return fold_phases(sum(jnp.where(place == p, part, 0.0) for p, part in enumerate(parts)))


SMALL_ROWS = 64
ROW_JOBS = {"pl": 4, "st": 2, "ss": 2, "lat": 2, "sm": 7}


def job_rows(job, tiles):
    rows = {"pl": 4 * (CC + BS), "st": 3 * CC, "ss": 9 * BS, "lat": 5 * DF, "sm": SMALL_ROWS * tiles}
    return rows[job] // tiles


def bundle_rows(jobs, tiles):
    planes = job_rows("pl", tiles) if "pl" in jobs else 0
    small = SMALL_ROWS if "sm" in jobs else 0
    rows = sum(job_rows(job, tiles) for job in jobs if job not in ("pl", "sm"))
    return planes + -(-rows // 32) * 32 + small, planes, small


def share_rows(jobs, tiles):
    count, planes, small = bundle_rows(jobs, tiles)
    return planes // 2 + (count - planes - small) // 2 + 2 * small


def kernel_weights_rows(tiles, frame, jobs, si, *refs):
    kst, kss, kla, ksm = CC // tiles, BS // tiles, DF // tiles, BF // tiles
    count = sum(ROW_JOBS[job] for job in jobs)
    keep, send, blocks, small = refs[count:]
    rows, _, small_rows = bundle_rows(jobs, tiles)
    base = 0
    operands = list(refs[:count])
    for job in jobs:
        own = [operands.pop(0) for _ in range(ROW_JOBS[job])]
        if job == "pl":
            low, bt, dz_sk, dz_se = own
            ksk, kse = kst, kss
            for j in range(4):
                cols, start = slice(j * 256, (j + 1) * 256), base + j * (ksk + kse)
                d = dot_tn(low[...], dz_sk[:, cols]).astype(BF16)
                blocks[:, start : start + ksk, :] = d.reshape(tiles, ksk, 256)
                d = dot_tn(bt[...], dz_se[:, cols]).astype(BF16)
                blocks[:, start + ksk : start + ksk + kse, :] = d.reshape(tiles, kse, 256)
        elif job == "st":
            low, dz = own
            for j in range(3):
                d = dot_tn(low[...], dz[:, j * BS : (j + 1) * BS]).astype(BF16)
                blocks[:, base + j * kst : base + (j + 1) * kst, :] = d.reshape(tiles, kst, BS)
        elif job == "ss":
            a9, dz = own
            for k in range(9):
                d = dot_tn(a9[:, k * BS : (k + 1) * BS], dz[:, :BS]).astype(BF16)
                blocks[:, base + k * kss : base + (k + 1) * kss, :] = d.reshape(tiles, kss, BS)
        elif job == "lat":
            fb, dz = own
            f = [fb[:, p * DF : (p + 1) * DF] for p in range(3)] + [fb[:, 3 * DF :]]
            for k, x in enumerate([down(f[2], frame), down(f[3], frame), f[0], f[1], f[2]]):
                d = dot_tn(x, dz[...]).astype(BF16)
                blocks[:, base + k * kla : base + (k + 1) * kla, :] = d.reshape(tiles, kla, DL)
        else:
            af9, fb, bf, dz_f, dz_ft, dz_fe, dz_fk = own
            small[...] = jnp.zeros(small.shape, F32)
            last = dz_f.shape[1] - LANES
            for k in range(9):
                d = dot_tn(af9[:, k * LANES : (k + 1) * LANES], dz_f[:, last:])
                d = pick_phases([d[p * BF : (p + 1) * BF] for p in range(ALPHA)])
                for i in range(tiles):
                    small[i, k * ksm : (k + 1) * ksm, LANES:] = d[i * ksm : (i + 1) * ksm]
            f = [fb[:, p * DF : (p + 1) * DF] for p in range(ALPHA)]
            six = [dot_tn(x, dz_ft[...]) for x in [down(f[3], frame)] + f + [up(f[0], frame)]]
            for k in range(3):
                d = pick_phases([six[k + p] for p in range(ALPHA)])
                small[:, k * kla : (k + 1) * kla, :LANES] = d.reshape(tiles, kla, LANES)
            fe, fk = 0.0, 0.0
            for p in range(ALPHA):
                cols = slice(p * DF, (p + 1) * DF)
                fk = fk + dot_tn(fb[:, cols], dz_fk[:, cols])
                fe = fe + dot_tn(bf[...], dz_fe[:, cols])[p * BF : (p + 1) * BF, :]
            for i in range(tiles):
                small[i, 9 * ksm : 10 * ksm, LANES:] = fe[i * ksm : (i + 1) * ksm]
                small[i, 10 * ksm : 10 * ksm + kla, LANES:] = fk[i * kla : (i + 1) * kla]
            blocks[:, rows - small_rows :, :] = small[...].astype(BF16)
            continue
        base += job_rows(job, tiles)
    if rows - small_rows > base:
        blocks[:, base : rows - small_rows, :] = jnp.zeros((tiles, rows - small_rows - base, 256), BF16)
    part_tiles(si, tiles, blocks, keep, send)


def add(one, two):
    return (one.astype(F32) + two.astype(F32)).astype(BF16)


def kernel_halve_first(split, si, kept, got, keep_a, send_a, keep_b, send_b):
    low, high = si[1] % 2, si[1] // 2
    for i in range(2):
        for ref, side in ((keep_a, low), (send_a, 1 - low)):
            place = 2 * i + side
            ref[i] = add(kept[place, :split], got[place, :split])
        for ref, side in ((keep_b, high), (send_b, 1 - high)):
            place = 2 * side + i
            ref[i] = add(kept[place, split:], got[place, split:])


def kernel_halve_second(si, kept_a, got_a, kept_b, got_b, keep_a, send_a, keep_b, send_b):
    low, high = si[1] % 2, si[1] // 2
    for ref, place in ((keep_a, high), (send_a, 1 - high)):
        ref[...] = add(kept_a[place], got_a[place])
    for ref, place in ((keep_b, low), (send_b, 1 - low)):
        ref[...] = add(kept_b[place], got_b[place])


def kernel_halve_last(si, kept, got, keep, send):
    bit = si[3] // 2
    for ref, place in ((keep, bit), (send, 1 - bit)):
        ref[...] = add(kept[place], got[place])


def kernel_pick_places(si, kept, got, *outs):
    for i, ref in enumerate(outs):
        place = si[1] ^ i
        ref[...] = add(kept[place], got[place])


def whole_sum(parts):
    total = parts[0][...].astype(F32)
    for part in parts[1:]:
        total = total + part[...].astype(F32)
    return total


def columns_of(x, j):
    half = x.shape[0] // 2
    base = (j // 2) * LANES
    a, b = x[:half, base : base + LANES], x[half:, base : base + LANES]
    left = lane(a.shape) < 64
    if j % 2 == 0:
        return jnp.where(left, a, pltpu.roll(b, 64, 1))
    return jnp.where(left, pltpu.roll(a, 64, 1), b)


def column_blocks(jobs, tiles, total, blocks):
    count, planes, small_rows = bundle_rows(jobs, tiles)
    big = count - small_rows
    packed = (big - planes) // 2
    each = planes // 4
    for j in range(4):
        if planes:
            plane = total[j * each : (j + 1) * each].astype(BF16)
            blocks[j, :each, :] = plane[:, :LANES]
            blocks[j, each : 2 * each, :] = plane[:, LANES:]
        base = 2 * each
        if packed:
            blocks[j, base : base + packed, :] = columns_of(total[planes:big], j).astype(BF16)
        base += packed
        if small_rows:
            small = total[big:].astype(BF16)
            blocks[j, base : base + small_rows, :] = small[:, :LANES]
            blocks[j, base + small_rows :, :] = small[:, LANES:]


def kernel_pick_columns(jobs, tiles, si, a, b, c, d, out0, out1, out2, out3, blocks):
    column_blocks(jobs, tiles, whole_sum((a, b, c, d)), blocks)
    for i, ref in enumerate((out0, out1, out2, out3)):
        ref[...] = blocks[si[3] ^ i]


def kernel_join_columns(jobs, tiles, si, kept_a, got_a, kept_b, got_b, keep, send, blocks):
    total = jnp.concatenate([whole_sum((kept_a, got_a)), whole_sum((kept_b, got_b))], axis=0)
    column_blocks(jobs, tiles, total, blocks)
    bit = si[3] % 2
    for ref, side in ((keep, bit), (send, 1 - bit)):
        for i in range(2):
            ref[i] = blocks[2 * i + side]


def kernel_finish(tiles, plan, si, *refs):
    kst, kss, kla, ksm = CC // tiles, BS // tiles, DF // tiles, BF // tiles
    refs = list(refs)
    g_lat, g_st, g_ss, g_se, g_sk, g_ft, g_fs, g_fe, g_fk = refs[-9:]
    for jobs, layers, count in plan:
        total, refs = whole_sum(refs[:count]), refs[count:]
        rows, planes, small_rows = bundle_rows(jobs, tiles)
        start = planes // 2
        if planes:
            plane = jnp.concatenate([total[: start // 2], total[start // 2 : start]], axis=1)
            g_sk[layers[0]] = plane[:kst]
            g_se[layers[0]] = plane[kst:]
        packed = (rows - planes - small_rows) // 2
        big = total[start : start + packed]
        rows = [big[:, :64], pltpu.roll(big, 64, 1)[:, :64]] if packed else []
        tail = total[start + packed :]

        def part(start, size):
            end = start + size
            if end <= packed:
                return rows[0][start:end]
            if start >= packed:
                return rows[1][start - packed : end - packed]
            return jnp.concatenate([rows[0][start:], rows[1][: end - packed]], axis=0)

        base = 0
        for job, l in zip(jobs, layers):
            if job == "pl":
                continue
            if job == "st":
                for k in range(3):
                    g_st[l, k] = part(base + k * kst, kst).T
            elif job == "ss":
                for k in range(9):
                    g_ss[l, k // 3, k % 3] = part(base + k * kss, kss)
            elif job == "lat":
                for k in range(5):
                    g_lat[l, k] = part(base + k * kla, kla)
            else:
                small = tail[:SMALL_ROWS]
                eight = pltpu.roll(small, (LANES - 8 * si[3]) % LANES, 1)[:, :8]
                for k in range(3):
                    g_ft[l, k] = eight[k * kla : (k + 1) * kla].T
                small = tail[SMALL_ROWS:]
                eight = pltpu.roll(small, (LANES - 8 * si[3]) % LANES, 1)[:, :8]
                for k in range(9):
                    g_fs[l, k // 3, k % 3] = eight[k * ksm : (k + 1) * ksm]
                part32 = pltpu.roll(small, (LANES - 32 * si[3]) % LANES, 1)[:, :32]
                g_fe[l] = part32[9 * ksm : 10 * ksm]
                g_fk[l] = part32[10 * ksm : 10 * ksm + kla]
                continue
            base += job_rows(job, tiles)


def kernel_norm_sums(places, *refs):
    d_gains, d_biases = refs[-2:]
    for l in range(LAYERS):
        for i, out in ((0, d_biases), (1, d_gains)):
            column = 0
            for n, row, second, count in places[l][:5]:
                row += i * second
                for r in range(row, row + count):
                    out[l : l + 1, column : column + LANES] = refs[n][r : r + 1, :]
                    column += LANES
            ft, fs, fe, fk = (
                refs[n][row + i * second : row + i * second + 1, :] for n, row, second, _ in places[l][5:]
            )
            ft, fs = fold_phases(ft), fold_phases(fs)
            fe, fk = pltpu.roll(fe, 64, 1), pltpu.roll(fk, 64, 1)
            place = lane((1, LANES))
            out[l : l + 1, column : column + LANES] = jnp.where(place < 32, ft, jnp.where(place < 64, fs, fe))
            out[l : l + 1, column + LANES : column + 2 * LANES] = jnp.where(place < 64, fe, fk)
            out[l : l + 1, column + 2 * LANES :] = fk[:, :64]


SMEM = pltpu.MemorySpace.SMEM
VMEM = pltpu.MemorySpace.VMEM


class Weight:
    def __init__(self, array, layer):
        self.array = array
        self.layer = layer


class Layer:
    def __init__(self, array, layer):
        self.array = array
        self.layer = layer


class Load:
    def __init__(self, array):
        self.array = array


class Arriving:
    def __init__(self, copy, ref, layered):
        self.copy = copy
        self.ref = ref
        self.layered = layered
        self.shape = ref.shape

    def __getitem__(self, place):
        if self.copy is not None:
            self.copy.wait()
            self.copy = None
        if not self.layered:
            return self.ref[place]
        return self.ref[place[1:]] if isinstance(place, tuple) else self.ref[...]


class Out:
    def __init__(self, shape, kind):
        self.shape = shape
        self.kind = kind


def scalar_values(place, valid, frame, tiles):
    ha, wa, clip = place[0], place[1], place[2]
    total = valid[0]
    for i in range(1, valid.shape[0]):
        total = total + valid[i]
    count = jnp.full((1, LANES), total * (HT * WD), jnp.int32).astype(F32)
    inverse = 1.0 / count
    flags = [ha > 0, ha < tiles[0] - 1, wa > 0, wa < tiles[1] - 1]
    vectors = [jnp.where(jnp.full((1, LANES), jnp.where(f, 1, 0), jnp.int32) > 0, 1.0, 0.0) for f in flags]
    vectors = [inverse, inverse * (1.0 / ALPHA)] + vectors
    return (valid[clip] * frame, ha, wa, clip), [v[:, :1] for v in vectors]


def call(body, scalars, operands, outs, scratch=(), limit=16, pinned=False):
    mode, scalars = (None, ()) if not scalars else (scalars[0], scalars[1:3])
    count, first = len(operands), len(scalars)
    weights = [i for i, x in enumerate(operands) if isinstance(x, (Weight, Load))]
    results = [i for i, x in enumerate(outs) if isinstance(x, Out)]
    arrays = [x.array if isinstance(x, (Weight, Layer, Load)) else x for x in operands]
    if pinned:
        for i in weights:
            arrays[i] = pltpu.with_memory_space_constraint(arrays[i], pltpu.HBM)
    layered = [isinstance(x, Weight) for x in operands]
    shapes = [(x.shape, x.kind) if isinstance(x, Out) else x for x in outs]
    buffers = [pltpu.VMEM(arrays[i].shape[1:] if layered[i] else arrays[i].shape, arrays[i].dtype) for i in weights]
    buffers += [pltpu.VMEM(*shapes[i]) for i in results]
    own = first + count + len(outs)

    def wrapped(*refs):
        refs = list(refs)
        inner, rest = refs[own : own + len(buffers)], refs[own + len(buffers) :]
        arriving, leaving = [], []
        for n, i in enumerate(weights):
            source = refs[first + i].at[operands[i].layer] if layered[i] else refs[first + i]
            copy = pltpu.make_async_copy(source, inner[n], rest[-1].at[n])
            copy.start()
            refs[first + i] = Arriving(copy, inner[n], layered[i])
            arriving.append(refs[first + i])
        for i, x in enumerate(operands):
            if isinstance(x, Layer):
                refs[first + i] = refs[first + i].at[x.layer]
        for n, i in enumerate(results):
            n += len(weights)
            leaving.append(pltpu.make_async_copy(inner[n], refs[first + count + i], rest[-1].at[n]))
            refs[first + count + i] = inner[n]
        given = ()
        if mode is not None:
            t_frame, tiles = mode[1], mode[2]
            ints, vectors = scalar_values(refs[0], refs[1], t_frame, tiles) if mode[0] == "all" else (
                (None, refs[0][0], refs[0][1], refs[0][2]), None)
            given = (ints, vectors) if mode[0] == "all" else (ints,)
        body(*given, *refs[first:own], *(rest[:-1] if buffers else rest))
        for copy in leaving:
            copy.start()
        for one in arriving:
            if one.copy is not None:
                one.copy.wait()
        for copy in leaving:
            copy.wait()

    def space(i, some):
        return pl.BlockSpec(memory_space=pltpu.HBM if i in some else VMEM)

    return pl.pallas_call(
        wrapped,
        out_shape=[jax.ShapeDtypeStruct(shape, kind) for shape, kind in shapes],
        in_specs=[pl.BlockSpec(memory_space=SMEM) for _ in scalars] + [space(i, weights) for i in range(count)],
        out_specs=[space(i, results) for i in range(len(outs))],
        scratch_shapes=buffers
        + [pltpu.VMEM(shape, kind) for shape, kind in scratch]
        + ([pltpu.SemaphoreType.DMA((len(buffers),))] if buffers else []),
        cost_estimate=pl.CostEstimate(flops=2000000000, bytes_accessed=4000000, transcendentals=0),
        compiler_params=pltpu.CompilerParams(vmem_limit_bytes=limit << 20),
    )(*scalars, *arrays)


def sum_over(x, axis):
    step, count = 1, lax.axis_size(axis)
    while step < count:
        pair = x + flip(x, axis, step)
        if 4 * step <= count:
            pair = pair + (flip(x, axis, 2 * step) + flip(x, axis, 3 * step))
            step *= 2
        x = pair
        step *= 2
    return x


def sum_all(x):
    for axis in (WA, HA, CLIP):
        x = sum_over(x, axis)
    return x


def exchange(block):
    return lax.all_to_all(block, ALL_AXES, 0, 0)


def swap(x):
    return lax.ppermute(x, WA, [(0, 1), (1, 0)])


def halo(z, top, bottom):
    count = lax.axis_size(HA)
    above = lax.ppermute(bottom, HA, [(i, i + 1) for i in range(count - 1)])
    below = lax.ppermute(top, HA, [(i + 1, i) for i in range(count - 1)])
    return [above, below, swap(z), swap(above), swap(below)]


def sum_with_halo(x, one, two, z):
    n = x.shape[0]
    one, two, across = flip(one, HA, 1), flip(two, HA, 3), flip(x, HA, 2)
    both = x + across
    o_one, o_two, o_both = swap(one), swap(two), swap(both)
    total = (both + (one[:n] + two[:n])) + (o_both + (o_one[:n] + o_two[:n]))
    return total, [one, two, swap(z), o_one, o_two]


def after(first, *rest):
    return lax.optimization_barrier((first,) + rest)


def flip(x, axis, step):
    return lax.ppermute(x, axis, [(i, i ^ step) for i in range(lax.axis_size(axis))])


ORDERS = ((WA, HA, CLIP), (WA, HA, CLIP), (WA, CLIP, HA), (WA, HA, CLIP), (WA, CLIP, HA), (WA, HA, CLIP), (WA, CLIP, HA))
LAUNCH = {(1, 'wa'): ('A1',), (3, 'wa'): ('ST1',), (5, 'wa'): ('A0',), (6, 'wa'): ('T0',), (3, 'ha'): ('A1',), (5, 'ha'): ('ST1',)}
LAND = {(1, 'clip'): ('A1',), (2, 'ha'): ('A1',), (3, 'clip'): ('ST1',), (4, 'ha'): ('A1', 'ST1'), (5, 'clip'): ('A1', 'A0'), (6, 'ha'): ('ST1', 'A0', 'T0')}
BUNDLES = {1: [('A1', False, [('pl', 1)])], 3: [('ST1', False, [('ss', 1), ('st', 1)])], 5: [('A0', False, [('pl', 0), ('ss', 0), ('lat', 1), ('sm', 1)])], 6: [('T0', False, [('st', 0)])], 7: [('L0', True, [('lat', 0), ('sm', 0)])]}
WAIT = {(2, HA, "A1"), (6, HA, "T0"), (6, HA, "ST1"), (4, HA, "ST1")}


def local(
    slow_in,
    fast_in,
    valid_frames,
    lateral_w,
    slow_temporal_w,
    slow_spatial_w,
    slow_expand_w,
    slow_skip_w,
    fast_temporal_w,
    fast_spatial_w,
    fast_expand_w,
    fast_skip_w,
    gains,
    biases,
    slow_cot,
    fast_cot,
):
    devices = lax.axis_size(ALL_AXES)
    clips, n_ha, n_wa = (lax.axis_size(a) for a in ALL_AXES)
    tiles = n_ha * n_wa
    _, t, h, w, _ = slow_in.shape
    shape = (t, h, w)
    frame = h * w
    rows = t * frame

    place = jnp.stack([lax.axis_index(a) for a in (HA, WA, CLIP)]).astype(jnp.int32)
    scalars = (("all", frame, (n_ha, n_wa)), place, valid_frames)
    places = (("place", frame, (n_ha, n_wa)), place, valid_frames)

    slow2 = slow_in.reshape(rows, DS)
    fast4 = fast_in.reshape(t, ALPHA, frame, DF)
    slow_cot2 = slow_cot.reshape(rows, DS)
    fast_cot4 = fast_cot.reshape(t, ALPHA, frame, DF)

    def act(columns, kind=F32):
        return ((rows, columns), kind)

    def edges(columns, sums=None):
        if sums is None:
            return [act(columns, BF16), ((t * w, columns), BF16), ((t * w, columns), BF16)]
        return [act(columns, BF16)] + [((sums + t * w * columns // LANES, LANES), F32)] * 2

    def pay(count):
        return ((count, LANES), F32)

    def bind(body, *static):
        return functools.partial(body, *static)

    pad_slow = ((t, h + 2, 3 * w, BS), F32)
    pad_fast = ((t, h + 2, 3 * w, LANES), F32)
    pad_both = ((t, h + 2, 3 * w, BS + LANES), F32)
    saved = []
    fb, zlat, zft, z16, top, bottom, zfk, sent, band = call(
        bind(kernel_start, shape),
        scalars,
        [Load(fast4), Weight(lateral_w, 0), Load(jnp.swapaxes(fast_temporal_w, 2, 3)), Weight(fast_skip_w, 0)],
        [act(512, BF16), act(DL), act(LANES), *edges(LANES, 8), act(512), pay(8), ((LAYERS, 6, LANES, LANES), BF16)],
        pinned=True,
    )
    recv, around = sum_with_halo(sent, top, bottom, z16)
    recv = sum_over(recv, CLIP)
    gb_all, fs_bd, fe_bd = call(
        kernel_prepare,
        (),
        [Load(gains), Load(biases), Load(fast_spatial_w), Load(fast_expand_w)],
        [((LAYERS, 2, GB_ROWS, LANES), F32), ((LAYERS, 3, 3, LANES, LANES), BF16), ((LAYERS, LANES, ALPHA * DF), BF16)],
        pinned=True,
    )
    gb = [Layer(gb_all, l) for l in range(LAYERS)]
    before = None
    for l in range(LAYERS):
        last = l == LAYERS - 1
        start = [recv, Load(slow2), gb[l]] if l == 0 else [recv, gb[l - 1], before["tot_sk"], before["zse"], before["zsk"], gb[l]]
        low, zst, z16, top, bottom, zsk, af9, zfs, sent = call(
            bind(kernel_temporal, l == 0, shape),
            scalars,
            start + [zlat, zft, *around, Weight(slow_temporal_w, l), Weight(slow_skip_w, l), Layer(fs_bd, l)],
            [act(CC, BF16), act(BS), *edges(BS, 24), act(DS), act(9 * LANES, BF16), act(LANES), pay(24)],
            [pad_fast],
            pinned=l == 0,
        )
        tot_lat = recv
        if l > 0:
            before["tot_se"] = tot_lat
        recv, around = sum_with_halo(sent, top, bottom, z16)
        recv = sum_over(recv, CLIP)
        a9, zss, bf, zfe, sent = call(
            bind(kernel_spatial, shape),
            scalars,
            [recv, gb[l], zst, *around, zfs, Weight(slow_spatial_w, l), Layer(fe_bd, l)],
            [act(9 * BS, BF16), act(BS), act(LANES, BF16), act(512), ((devices, 8, LANES), F32)],
            [pay(8), pad_slow],
        )
        tot_st = recv
        recv = exchange(sent)
        keep = dict(
            fb=fb, zlat=zlat, zft=zft, zfk=zfk, low=low, zst=zst, zsk=zsk, af9=af9, zfs=zfs, a9=a9, zss=zss, bf=bf,
            zfe=zfe, tot_lat=tot_lat, tot_fk=tot_lat, tot_st=tot_st, tot_sk=tot_st,
        )
        if last:
            bt, zse, sent, tot_ss = call(
                bind(kernel_expand, True, shape),
                scalars,
                [recv, gb[l], zss, Weight(slow_expand_w, l)],
                [act(BS, BF16), act(DS), ((devices, 16, LANES), F32), pay(8)],
                [pay(16)],
            )
        else:
            bt, zse, sent, tot_ss, fb, zlat, zft, z16, top, bottom, zfk = call(
                bind(kernel_expand, False, shape),
                scalars,
                [recv, gb[l], zss, Weight(slow_expand_w, l), tot_lat, zfe, zfk,
                 Weight(lateral_w, l + 1), Layer(band, l + 1), Weight(fast_skip_w, l + 1)],
                [act(BS, BF16), act(DS), pay(24), pay(8),
                 act(512, BF16), act(DL), act(LANES), *edges(LANES, 24), act(512)],
            )
        if last:
            recv = exchange(sent)
        else:
            recv, around = sum_with_halo(sent, top, bottom, z16)
            recv = sum_over(recv, CLIP)
        keep.update(bt=bt, zse=zse, tot_ss=tot_ss, tot_fe=tot_ss)
        saved.append(keep)
        before = keep

    for l in range(LAYERS):
        saved[l]["gb"] = gb[l]

    def stage(body, ins, outs, scratch=(), limit=16):
        names = list(ins) + list(outs) + [name for name, _ in scratch]

        def named(ints, vectors, *refs):
            body(shape, Refs(names, refs), inside_rows(rows, 256, ints[0]), ints, vectors)

        results = call(
            named, scalars, list(ins.values()), list(outs.values()), [kind for _, kind in scratch], limit
        )
        return dict(zip(outs, results))

    def layer(prefix, l, *names):
        return {prefix + name: saved[l][name] for name in names}

    def edge(columns, sums=None):
        return dict(zip(("whole", "top", "bottom"), edges(columns, sums)))

    def around_of(values):
        return {f"h{i}": x for i, x in enumerate(values)}

    narrow = clips == 4

    def halves_chain(keep, send, jobs):
        count = bundle_rows(jobs, tiles)[0]
        (got,) = yield [keep], [(send, WA, 1)]
        split = count // 32 * 16
        a, b = (split, 256), (count - split, 256)
        keep_a, send_a, keep_b, send_b = call(
            bind(kernel_halve_first, split), places, [keep, got], [((2,) + x, BF16) for x in (a, a, b, b)]
        )
        got_a, got_b = yield [keep_a, keep_b], [(send_a, HA, 1), (send_b, HA, 2)]
        keep_a, send_a, keep_b, send_b = call(
            kernel_halve_second, places, [keep_a, got_a, keep_b, got_b], [(x, BF16) for x in (a, a, b, b)]
        )
        got_a, got_b = yield [keep_a, keep_b], [(send_a, HA, 2), (send_b, HA, 1)]
        parts = [keep_a, got_a, keep_b, got_b]
        if narrow:
            block = (share_rows(jobs, tiles), LANES)
            keep, send = call(
                bind(kernel_join_columns, jobs, tiles), places, parts, [((2,) + block, BF16)] * 2, [((4,) + block, BF16)]
            )
            (got,) = yield [keep], [(send, CLIP, 1)]
            keep, send = call(kernel_halve_last, places, [keep, got], [(block, BF16)] * 2)
            (got,) = yield [keep], [(send, CLIP, 2)]
            parts = [keep, got]
        yield parts, None

    def direct_chain(keep, send, jobs):
        count = bundle_rows(jobs, tiles)[0]
        (got,) = yield [keep], [(send, WA, 1)]
        mine, *others = call(kernel_pick_places, places, [keep, got], [((count, 256), BF16)] * 4)
        got = yield [mine], [(x, HA, i + 1) for i, x in enumerate(others)]
        parts = [mine, *got]
        if narrow:
            block = (share_rows(jobs, tiles), LANES)
            mine, *others = call(
                bind(kernel_pick_columns, jobs, tiles), places, parts, [(block, BF16)] * 4, [((4,) + block, BF16)]
            )
            got = yield [mine], [(x, CLIP, i + 1) for i, x in enumerate(others)]
            parts = [mine, *got]
        yield parts, None

    class Running:
        def __init__(self, chain, jobs, layers):
            self.chain = chain
            self.jobs = jobs
            self.layers = layers
            self.got = None
            self.state = next(chain)

        def done(self):
            return self.state[1] is None

        def launch(self, x=None):
            if self.done() or self.got is not None:
                return
            sends = [send for send, _, _ in self.state[1]]
            if x is not None:
                _, *sends = after(x, *sends)
            self.got = [flip(send, axis, step) for send, (_, axis, step) in zip(sends, self.state[1])]

        def land(self, x):
            if self.got is None:
                return x
            x, *got = after(x, *self.got)
            self.got = None
            self.state = self.chain.send(got)
            return x

        def finish(self):
            while not self.done():
                self.launch()
                got, self.got = self.got, None
                self.state = self.chain.send(got)
                yield

    running = {}

    def bundle(name, chain, *parts):
        jobs, layers = tuple(p[0] for p in parts), tuple(p[1] for p in parts)
        operands = []
        for job, l, r in parts:
            k = saved[l]
            operands += {
                "pl": lambda: [k["low"], k["bt"], r["dz_sk"], r["dz_se"]],
                "st": lambda: [k["low"], r["dz_st"]],
                "ss": lambda: [k["a9"], r["dz"]],
                "lat": lambda: [k["fb"], r["dz_lat"]],
                "sm": lambda: [k["af9"], k["fb"], k["bf"], r["dz_f"], r["dz_ft"], r["dz_fe"], r["dz_fk"]],
            }[job]()
        count = bundle_rows(jobs, tiles)[0]
        pair = call(
            bind(kernel_weights_rows, tiles, frame, jobs),
            places,
            operands,
            [((tiles // 2, count, 256), BF16)] * 2,
            [((tiles, count, 256), BF16), ((tiles, SMALL_ROWS, 256), F32)],
            limit=24,
        )
        running[name] = Running(chain(*pair, jobs), jobs, layers)

    def skip_back(l, r):
        (r["dlow"],) = call(kernel_back_skip, (), [r["dz_sk"], Weight(slow_skip_w, l)], [act(CC)])

    totals = []

    around = []

    def total_of(x, edge_rows=None):
        n = len(totals)
        for axis in ORDERS[n]:
            for name in LAND.get((n, axis), ()):
                x = running[name].land(x)
                if (n, axis, name) not in WAIT:
                    running[name].launch()
            if edge_rows is None:
                x = sum_over(x, axis)
            elif axis == HA:
                x, around[:] = sum_with_halo(x, edge_rows["top"], edge_rows["bottom"], edge_rows["whole"])
            elif axis == CLIP:
                x = sum_over(x, axis)
            for name in LAUNCH.get((n, axis), ()) + tuple(w[2] for w in WAIT if w[:2] == (n, axis)):
                running[name].launch(x)
        totals.append(x)
        return x

    one, two = LAYERS - 1, LAYERS - 2
    r1, r0 = {}, {}

    def start_bundles():
        for name, direct, parts in BUNDLES.get(len(totals), ()):
            chain = direct_chain if direct else halves_chain
            bundle(name, chain, *[(job, l, (r0, r1)[l]) for job, l in parts])

    slow_names, fast_names = ("gb", "tot_se", "tot_sk", "zse", "zsk"), ("tot_ss", "tot_lat", "zfe", "zfk")
    r1.update(stage(
        back_turn,
        dict(recv=recv, **layer("a_", one, *slow_names[:1], *slow_names[2:], *fast_names), slow_cot=Load(slow_cot2), fast_cot=Load(fast_cot4)),
        dict(out_slow=Out((rows, DS), F32), out_fast=Out((t, ALPHA, frame, DF), F32), du_s=act(DS), du_f=act(512), pay=pay(32), tot=pay(16)),
    ))
    saved[-1]["tot_se"] = r1["tot"]
    recv = total_of(r1["pay"])
    r1.update(stage(
        back_expand,
        dict(recv=recv, **layer("a_", one, *slow_names, *fast_names, "zss", "zfs"), du_s=r1["du_s"], du_f=r1["du_f"],
             se_w=Weight(slow_expand_w, one), fe_bd=Layer(fe_bd, one)),
        dict(dz_se=act(DS, BF16), dz_sk=act(DS, BF16), dz_fe=act(512, BF16), dz_fk=act(512, BF16), dy=act(BS + LANES),
             **edge(2 * (BS + LANES)), pay=pay(8)),
    ))
    skip_back(one, r1)
    start_bundles()
    recv = total_of(r1["pay"])
    r1.update(stage(
        back_spatial,
        dict(recv=recv, **layer("a_", one, "gb", "tot_sk", "tot_ss", "tot_lat", "zss", "zfs", "zst", "zft"), dy=r1["dy"],
             **around_of(halo(r1["whole"], r1["top"], r1["bottom"])), ss_w=Weight(slow_spatial_w, one), fs_bd=Layer(fs_bd, one)),
        dict(dz=act(BS + LANES, BF16), dy_st=act(BS), dy_ft=act(LANES), pay=pay(8)),
        [("pad", pad_both)],
    ))
    r1["dz_f"] = r1["dz"]
    start_bundles()
    recv = total_of(r1["pay"])
    r1.update(stage(
        back_temporal,
        dict(recv=recv, **layer("a_", one, "gb", "tot_sk", "tot_lat", "zst", "zft", "zlat"),
             **layer("b_", two, *slow_names), dy_st=r1["dy_st"], dy_ft=r1["dy_ft"], dlow=r1["dlow"], dz_fk=r1["dz_fk"],
             st_w=Weight(slow_temporal_w, one), ft_band=Layer(band, one), fk_w=Weight(fast_skip_w, one)),
        dict(dz_st=act(3 * BS, BF16), dz_ft=act(LANES, BF16), dfast=act(512), dy_lat=act(DL), du_s=act(DS), pay=pay(32)),
    ))
    start_bundles()
    recv = total_of(r1["pay"])
    r0.update(stage(
        back_lateral,
        dict(recv=recv, **layer("a_", one, "gb", "tot_lat", "zlat"),
             **layer("b_", two, *slow_names, *fast_names, "zss"), dy_lat=r1["dy_lat"], dfast=r1["dfast"], du_s=r1["du_s"],
             lat_w=Weight(lateral_w, one), se_w=Weight(slow_expand_w, two)),
        dict(dz_lat=act(DL, BF16), du_f=act(512), dz_se=act(DS, BF16), dz_sk=act(DS, BF16), dy=act(BS), **edge(2 * BS), pay=pay(8)),
    ))
    r1["dz_lat"] = r0["dz_lat"]
    start_bundles()
    skip_back(two, r0)
    recv = total_of(r0["pay"])
    fast = stage(
        back_low_spatial,
        dict(recv=recv, **layer("b_", two, "gb", "tot_sk", "tot_ss", "tot_lat", "zss", "zst", "zfe", "zfk", "zfs"),
             du_f=r0["du_f"], dy=r0["dy"], **around_of(halo(r0["whole"], r0["top"], r0["bottom"])), ss_w=Weight(slow_spatial_w, two), fe_bd=Layer(fe_bd, two)),
        dict(dz_fe=act(512, BF16), dz_fk=act(512, BF16), dy_fs=act(LANES), **edge(2 * LANES), dz=act(BS, BF16), dy_st=act(BS),
             pay=pay(8)),
        [("pad", pad_slow)],
    )
    r0.update(fast)
    start_bundles()
    recv = total_of(r0["pay"])
    r0.update(stage(
        back_low_temporal,
        dict(recv=recv, **layer("b_", two, "gb", "tot_sk", "tot_lat", "zst", "zft", "zlat", "zfs"), dy_fs=r0["dy_fs"],
             **around_of(halo(r0["whole"], r0["top"], r0["bottom"])), dy_st=r0["dy_st"], dlow=r0["dlow"], st_w=Weight(slow_temporal_w, two), fs_bd=Layer(fs_bd, two)),
        dict(dz_f=act(LANES, BF16), dy_ft=act(LANES), dz_st=act(3 * BS, BF16), dy_lat=act(DL), dslow=Out((rows, DS), F32),
             pay=pay(8)),
        [("pad", pad_fast)],
    ))
    start_bundles()
    recv = total_of(r0["pay"])
    r0.update(stage(
        back_low_lateral,
        dict(recv=recv, **layer("b_", two, "gb", "tot_lat", "zft", "zlat"), dy_ft=r0["dy_ft"], dy_lat=r0["dy_lat"],
             dz_fk=r0["dz_fk"], lat_w=Weight(lateral_w, two), ft_band=Layer(band, two), fk_w=Weight(fast_skip_w, two)),
        dict(dz_ft=act(LANES, BF16), dz_lat=act(DL, BF16), dfast=Out((t, ALPHA, frame, DF), F32)),
    ))
    start_bundles()
    ways = [chain.finish() for chain in running.values()]
    while ways:
        ways = [way for way in ways if next(way, 0) is None]
    out_slow, out_fast, grad_slow, grad_fast = r1["out_slow"], r1["out_fast"], r0["dslow"], r0["dfast"]
    where = [
        [(6, 0, 2, 2), (5, 0, 2, 2), (4, 0, 2, 2), (3, 8, 8, 8), (3, 8, 16, 8), (6, 4, 1, 1), (5, 4, 1, 1), (4, 4, 1, 1),
         (4, 4, 2, 1)],
        [(3, 0, 2, 2), (2, 0, 2, 2), (1, 0, 2, 2), (0, 0, 8, 8), (0, 0, 16, 8), (2, 4, 1, 1), (1, 4, 1, 1), (0, 24, 1, 1),
         (0, 24, 2, 1)],
    ]
    nst, nss, nla, nsm = CC // tiles, BS // tiles, DF // tiles, BF // tiles
    n, f, g = BS // clips, BF // clips, DF // clips
    sums = call(bind(kernel_norm_sums, where), (), totals, [Out(gains.shape, F32), Out(biases.shape, F32)])
    weights = [(LAYERS,) + dims for dims in (
        (5, nla, n), (3, nst, n), (3, 3, nss, n), (nss, DS // clips), (nst, DS // clips),
        (3, nla, f), (3, 3, nsm, f), (nsm, g), (nla, g),
    )]
    chains = list(running.values())
    if narrow:
        plan = [(chain.jobs, chain.layers, len(chain.state[0])) for chain in chains]
        parts = [x for chain in chains for x in chain.state[0]]
        turned = (1, 5)
        weights = [dims[:-2] + dims[:-3:-1] if i in turned else dims for i, dims in enumerate(weights)]
        weights = call(bind(kernel_finish, tiles, plan), places, parts, [Out(dims, F32) for dims in weights])
        weights = [jnp.swapaxes(x, -1, -2) if i in turned else x for i, x in enumerate(weights)]
    else:
        found = {}
        for chain in chains:
            got = [x.astype(F32) for x in chain.state[0]]
            if chain.jobs != ("lat", "sm"):
                total = jnp.concatenate([got[0] + got[1], got[2] + got[3]], axis=0).astype(BF16)
            else:
                total = sum(got).astype(BF16)
            count, planes, small_rows = bundle_rows(chain.jobs, tiles)
            if planes:
                plane = jnp.transpose(total[:planes].reshape(4, -1, 256), (1, 0, 2)).reshape(planes // 4, clips, DS // clips)
                plane = lax.psum_scatter(plane, CLIP, scatter_dimension=1)
                found["sk", chain.layers[0]], found["se", chain.layers[0]] = plane[:nst], plane[nst:]
            small = lax.psum(total[count - small_rows :], CLIP) if small_rows else None
            if count - small_rows > planes:
                total = lax.psum_scatter(
                    total[planes : count - small_rows].reshape(-1, clips, n), CLIP, scatter_dimension=1
                )
            base = 0
            for job, l in zip(chain.jobs, chain.layers):
                if job == "sm":
                    left = lax.dynamic_slice_in_dim(small[:, :LANES], place[2] * f, f, 1)
                    right = lax.dynamic_slice_in_dim(small[:, LANES:], place[2] * f, f, 1)
                    last = lax.dynamic_slice_in_dim(small[:, LANES:], place[2] * g, g, 1)
                    found["ft", l], found["fs", l] = left[: 3 * nla], right[: 9 * nsm]
                    found["fe", l], found["fk", l] = last[9 * nsm : 10 * nsm], last[10 * nsm : 10 * nsm + nla]
                elif job != "pl":
                    found[job, l] = total[base : base + job_rows(job, tiles)]
                    base += job_rows(job, tiles)
        names = ("lat", "st", "ss", "se", "sk", "ft", "fs", "fe", "fk")
        weights = [
            jnp.stack([found[name, l] for l in range(LAYERS)]).astype(F32).reshape(dims)
            for name, dims in zip(names, weights)
        ]
    return (
        out_slow.reshape(slow_in.shape),
        out_fast.reshape(fast_in.shape),
        grad_slow.reshape(slow_in.shape),
        grad_fast.reshape(fast_in.shape),
        *weights,
        *sums,
    )


def solution(mesh):
    pixels = P(CLIP, None, HA, WA, None)
    tile = (HA, WA)
    return jax.shard_map(
        local,
        mesh=mesh,
        in_specs=(pixels, pixels) + (P(),) * 12 + (pixels, pixels),
        out_specs=(
            (pixels,) * 4
            + (P(None, None, tile, CLIP),) * 2
            + (P(None, None, None, tile, CLIP),)
            + (P(None, tile, CLIP),) * 2
            + (P(None, None, tile, CLIP),)
            + (P(None, None, None, tile, CLIP),)
            + (P(None, tile, CLIP),) * 2
            + (P(),) * 2
        ),
        check_vma=False,
    )
```

profile of v0, /device:TPU:0, one launch (start us, length us, event | category | flops | bytes accessed | tf_op | source)
XLA Modules:
  0.0 341.2 jit_solution(10164507555116238689)
XLA Ops:
  1.4 2.9 shard_map.271
  4.2 4.0 %collective-permute-start.2 = (f32[72,128]{1,0:T(8,128)S(1)}, f32[72,128]{1,0:T(8,128)S(1)}, u32[]{:S(2)}, u32[]{:S(2)}) collective-permute-start(f32[72,128]{1,0:T(8,128)S(1)} %get-tuple-element.237), channel_id=1, source_target_pairs={{0,6},{2,4},{4,2},{6,0},{1,7},{3,5},{5,3},{7,1},{8,14},{10,12},{12... | collective-permute-start | bytes 110600 | tf_op jit(solution)/shard_map/ppermute | solution.py:1192
  10.2 2.0 collective-permute-done.1.refs_7_
  13.0 2.8 collective-permute-done
  17.0 2.6 collective-permute-start.7
  21.2 2.6 shard_map.272
  25.1 5.2 %shard_map.273 = (bf16[256,1280]{1,0:T(8,128)(2,1)S(1)}, f32[256,256]{1,0:T(8,128)S(1)}, bf16[256,256]{1,0:T(8,128)(2,1)S(1)}, f32[152,128]{1,0:T(8,128)S(1)}, f...) custom-call(s32[3]{0:T(128)S(1)} %pad_add_fusion.refs_0_, ...), custom_call_target="tpu_custom_call" | custom-call | flops 2000000000 | bytes 4000000 | tf_op jit(solution)/shard_map/pallas_call | solution.py:1132
  32.6 3.0 collective-permute-done.12.refs_6_
  37.1 2.8 collective-permute-done.10
  45.8 2.5 collective-permute-done.18
  48.4 2.3 shard_map.274
  50.7 11.5 %all_to_all.15.refs_2_ = f32[32,8,128]{2,1,0:T(8,128)S(1)} all-to-all(f32[32,8,128]{2,1,0:T(8,128)S(1)} %get-tuple-element.250), channel_id=1, replica_groups=mesh['clip'=4,'ha'=4,'wa'=2] {'clip','ha','wa'}, dimensions={0} | all-to-all | bytes 262144 | tf_op jit(solution)/shard_map/all_to_all | solution.py:1164
  62.2 2.3 shard_map.275
  66.7 3.0 collective-permute-done.22.refs_11_
  70.8 3.2 collective-permute-done.20
  75.8 2.2 collective-permute-start.28
  81.8 4.4 %shard_map.276 = (bf16[256,1280]{1,0:T(8,128)(2,1)S(1)}, f32[256,256]{1,0:T(8,128)S(1)}, bf16[256,256]{1,0:T(8,128)(2,1)S(1)}, f32[152,128]{1,0:T(8,128)S(1)}, f...) custom-call(s32[3]{0:T(128)S(1)} %pad_add_fusion.refs_0_, ...), custom_call_target="tpu_custom_call" | custom-call | flops 2000000000 | bytes 4000000 | tf_op jit(solution)/shard_map/pallas_call | solution.py:1132
  88.4 3.2 collective-permute-done.32.refs_6_
  93.0 2.9 collective-permute-done.30
  97.6 2.5 collective-permute-start.38
  103.8 2.3 shard_map.277
  106.0 11.2 %all_to_all.16.refs_2_ = f32[32,8,128]{2,1,0:T(8,128)S(1)} all-to-all(f32[32,8,128]{2,1,0:T(8,128)S(1)} %get-tuple-element.269), channel_id=1, replica_groups=mesh['clip'=4,'ha'=4,'wa'=2] {'clip','ha','wa'}, dimensions={0} | all-to-all | bytes 262144 | tf_op jit(solution)/shard_map/all_to_all | solution.py:1164
  118.4 12.6 %all_to_all.17.refs_2_ = f32[32,16,128]{2,1,0:T(8,128)S(1)} all-to-all(f32[32,16,128]{2,1,0:T(8,128)S(1)} %get-tuple-element.271), channel_id=1, replica_groups=mesh['clip'=4,'ha'=4,'wa'=2] {'clip','ha','wa'}, dimensions={0} | all-to-all | bytes 524288 | tf_op jit(solution)/shard_map/all_to_all | solution.py:1164
  131.0 3.0 shard_map.279
  141.9 2.1 collective-permute-start.46
  155.6 3.7 %collective-permute-start.55 = (bf16[64,768]{1,0:T(8,128)(2,1)S(1)}, bf16[64,768]{1,0:T(8,128)(2,1)S(1)}, u32[]{:S(2)}, u32[]{:S(2)}) collective-permute-start(bf16[64,768]{1,0:T(8,128)(2,1)S(1)} %get-tuple-element.292), channel_id=1, source_target_pairs={{0,2},{2,4},{4,6},{1,3},{3,5},{5,7},{8,10},{10,12},{12,14},{9,11},... | collective-permute-start | bytes 294920 | tf_op jit(solution)/shard_map/ppermute | solution.py:1173
  161.2 2.5 collective-permute-start.54
  166.6 2.6 collective-permute-start.64
  170.6 2.3 shard_map.282
  175.2 2.0 collective-permute-start.63
  181.6 2.1 collective-permute-start.68
  187.3 3.0 shard_map.285
  206.7 2.4 shard_map.287
  214.8 3.5 %collective-permute-start.88 = (bf16[64,512]{1,0:T(8,128)(2,1)S(1)}, bf16[64,512]{1,0:T(8,128)(2,1)S(1)}, u32[]{:S(2)}, u32[]{:S(2)}) collective-permute-start(bf16[64,512]{1,0:T(8,128)(2,1)S(1)} %get-tuple-element.332), channel_id=1, source_target_pairs={{0,2},{2,4},{4,6},{1,3},{3,5},{5,7},{8,10},{10,12},{12,14},{9,11},... | collective-permute-start | bytes 196616 | tf_op jit(solution)/shard_map/ppermute | solution.py:1173
  218.3 12.4 %collective-permute-start.89 = (bf16[64,512]{1,0:T(8,128)(2,1)S(1)}, bf16[64,512]{1,0:T(8,128)(2,1)S(1)}, u32[]{:S(2)}, u32[]{:S(2)}) collective-permute-start(bf16[64,512]{1,0:T(8,128)(2,1)S(1)} %get-tuple-element.333), channel_id=1, source_target_pairs={{2,0},{4,2},{6,4},{3,1},{5,3},{7,5},{10,8},{12,10},{14,12},{11,9},... | collective-permute-start | bytes 196616 | tf_op jit(solution)/shard_map/ppermute | solution.py:1174
  230.8 3.1 collective-permute-start.86
  236.0 2.4 collective-permute-done.87
  238.6 2.3 shard_map.290
  241.0 2.9 shard_map.292
  250.1 2.5 collective-permute-start.102
  265.8 3.4 shard_map.294
  272.6 2.4 collective-permute-start.110
  280.1 3.7 %collective-permute-done.111.refs_3_ = bf16[384,256]{1,0:T(8,128)(2,1)S(1)} collective-permute-done((bf16[384,256]{1,0:T(8,128)(2,1)S(1)}, bf16[384,256]{1,0:T(8,128)(2,1)S(1)}, u32[]{:S(2)}, u32[]{:S(2)}) %collective-permute-start.111) | collective-permute-done | bytes 196640 | tf_op jit(solution)/shard_map/ppermute | solution.py:1192
  294.4 2.6 collective-permute-start.124
  297.4 2.5 collective-permute-start.118
  305.2 2.5 shard_map.298
  326.0 2.7 collective-permute-done.130.refs_3_
  331.3 2.5 collective-permute-start.138
  (333 shorter events, 168.2 us)
Async XLA Ops:
  4.2 5.9 %collective-permute-start.2 = (f32[72,128]{1,0:T(8,128)S(1)}, f32[72,128]{1,0:T(8,128)S(1)}, u32[]{:S(2)}, u32[]{:S(2)}) collective-permute-start(f32[72,128]{1,0:T(8,128)S(1)} %get-tuple-element.237), channel_id=1, source_target_pairs={{0,6},{2,4},{4,2},{6,0},{1,7},{3,5},{5,3},{7,1},{8,14},{10,12},{12... | collective-permute-start | bytes 110600 | tf_op jit(solution)/shard_map/ppermute | solution.py:1192
  10.2 6.8 %collective-permute-start.5 = (f32[72,128]{1,0:T(8,128)S(1)}, f32[72,128]{1,0:T(8,128)S(1)}, u32[]{:S(2)}, u32[]{:S(2)}) collective-permute-start(f32[72,128]{1,0:T(8,128)S(1)} %collective-permute-done.2.refs_8_), channel_id=1, source_target_pairs={{0,1},{1,0},{2,3},{3,2},{4,5},{5,4},{6,7},{7,6},{8,9},{9,8},{10,11... | collective-permute-start | bytes 110600 | tf_op jit(solution)/shard_map/ppermute | solution.py:1168
  15.8 9.2 %collective-permute-start.9 = (bf16[256,128]{1,0:T(8,128)(2,1)S(1)}, bf16[256,128]{1,0:T(8,128)(2,1)S(1)}, u32[]{:S(2)}, u32[]{:S(2)}) collective-permute-start(bf16[256,128]{1,0:T(8,128)(2,1)S(1)} %get-tuple-element.241), channel_id=1, source_target_pairs={{0,1},{1,0},{2,3},{3,2},{4,5},{5,4},{6,7},{7,6},{8,9},{9,8},{10,11... | collective-permute-start | bytes 196616 | tf_op jit(solution)/shard_map/ppermute | solution.py:1168
  17.0 6.9 %collective-permute-start.7 = (f32[8,128]{1,0:T(8,128)S(1)}, f32[8,128]{1,0:T(8,128)S(1)}, u32[]{:S(2)}, u32[]{:S(2)}) collective-permute-start(f32[8,128]{1,0:T(8,128)S(1)} %fusion.10), channel_id=1, source_target_pairs={{0,16},{8,24},{16,0},{24,8},{1,17},{9,25},{17,1},{25,9},{2,18},{10... | collective-permute-start | bytes 12296 | tf_op jit(solution)/shard_map/ppermute | solution.py:1192
  151.6 9.5 %collective-permute-start.51 = (bf16[4,768,256]{2,1,0:T(8,128)(2,1)S(1)}, bf16[4,768,256]{2,1,0:T(8,128)(2,1)S(1)}, u32[]{:S(2)}, u32[]{:S(2)}) collective-permute-start(bf16[4,768,256]{2,1,0:T(8,128)(2,1)S(1)} %get-tuple-element.289), channel_id=1, source_target_pairs={{0,1},{1,0},{2,3},{3,2},{4,5},{5,4},{6,7},{7,6},{8,9},{9,8},{10,11... | collective-permute-start | bytes 4718600 | tf_op jit(solution)/shard_map/ppermute | solution.py:1192
  152.1 7.2 %collective-permute-start.49 = (f32[8,128]{1,0:T(8,128)S(1)}, f32[8,128]{1,0:T(8,128)S(1)}, u32[]{:S(2)}, u32[]{:S(2)}) collective-permute-start(f32[8,128]{1,0:T(8,128)S(1)} %add.298), channel_id=1, source_target_pairs={{0,4},{2,6},{4,0},{6,2},{1,5},{3,7},{5,1},{7,3},{8,12},{10,14},{12... | collective-permute-start | bytes 12296 | tf_op jit(solution)/shard_map/ppermute | solution.py:1192
  153.4 7.6 %collective-permute-start.50 = (f32[8,128]{1,0:T(8,128)S(1)}, f32[8,128]{1,0:T(8,128)S(1)}, u32[]{:S(2)}, u32[]{:S(2)}) collective-permute-start(f32[8,128]{1,0:T(8,128)S(1)} %add.298), channel_id=1, source_target_pairs={{0,6},{2,4},{4,2},{6,0},{1,7},{3,5},{5,3},{7,1},{8,14},{10,12},{12... | collective-permute-start | bytes 12296 | tf_op jit(solution)/shard_map/ppermute | solution.py:1192
  155.4 5.7 %collective-permute-start.48 = (f32[8,128]{1,0:T(8,128)S(1)}, f32[8,128]{1,0:T(8,128)S(1)}, u32[]{:S(2)}, u32[]{:S(2)}) collective-permute-start(f32[8,128]{1,0:T(8,128)S(1)} %add.298), channel_id=1, source_target_pairs={{0,2},{2,0},{4,6},{6,4},{1,3},{3,1},{5,7},{7,5},{8,10},{10,8},{12,... | collective-permute-start | bytes 12296 | tf_op jit(solution)/shard_map/ppermute | solution.py:1192
  155.6 8.1 %collective-permute-start.55 = (bf16[64,768]{1,0:T(8,128)(2,1)S(1)}, bf16[64,768]{1,0:T(8,128)(2,1)S(1)}, u32[]{:S(2)}, u32[]{:S(2)}) collective-permute-start(bf16[64,768]{1,0:T(8,128)(2,1)S(1)} %get-tuple-element.292), channel_id=1, source_target_pairs={{0,2},{2,4},{4,6},{1,3},{3,5},{5,7},{8,10},{10,12},{12,14},{9,11},... | collective-permute-start | bytes 294920 | tf_op jit(solution)/shard_map/ppermute | solution.py:1173
  159.3 6.5 %collective-permute-start.56 = (bf16[64,768]{1,0:T(8,128)(2,1)S(1)}, bf16[64,768]{1,0:T(8,128)(2,1)S(1)}, u32[]{:S(2)}, u32[]{:S(2)}) collective-permute-start(bf16[64,768]{1,0:T(8,128)(2,1)S(1)} %get-tuple-element.293), channel_id=1, source_target_pairs={{2,0},{4,2},{6,4},{3,1},{5,3},{7,5},{10,8},{12,10},{14,12},{11,9},... | collective-permute-start | bytes 294920 | tf_op jit(solution)/shard_map/ppermute | solution.py:1174
  161.0 9.6 %collective-permute-start.57 = (bf16[256,768]{1,0:T(8,128)(2,1)S(1)}, bf16[256,768]{1,0:T(8,128)(2,1)S(1)}, u32[]{:S(2)}, u32[]{:S(2)}) collective-permute-start(bf16[256,768]{1,0:T(8,128)(2,1)S(1)} %get-tuple-element.294), channel_id=1, source_target_pairs={{0,1},{1,0},{2,3},{3,2},{4,5},{5,4},{6,7},{7,6},{8,9},{9,8},{10,11... | collective-permute-start | bytes 1179656 | tf_op jit(solution)/shard_map/ppermute | solution.py:1168
  163.7 5.6 %collective-permute-start.52 = (f32[8,128]{1,0:T(8,128)S(1)}, f32[8,128]{1,0:T(8,128)S(1)}, u32[]{:S(2)}, u32[]{:S(2)}) collective-permute-start(f32[8,128]{1,0:T(8,128)S(1)} %add_add_fusion.16), channel_id=1, source_target_pairs={{0,8},{8,0},{16,24},{24,16},{1,9},{9,1},{17,25},{25,17},{2,10},{10... | collective-permute-start | bytes 12296 | tf_op jit(solution)/shard_map/ppermute | solution.py:1192
  166.6 14.2 %collective-permute-start.64 = (bf16[2,384,256]{2,1,0:T(8,128)(2,1)S(1)}, bf16[2,384,256]{2,1,0:T(8,128)(2,1)S(1)}, u32[]{:S(2)}, u32[]{:S(2)}) collective-permute-start(bf16[2,384,256]{2,1,0:T(8,128)(2,1)S(1)} %get-tuple-element.298), channel_id=1, source_target_pairs={{0,2},{2,0},{4,6},{6,4},{1,3},{3,1},{5,7},{7,5},{8,10},{10,8},{12,... | collective-permute-start | bytes 1179656 | tf_op jit(solution)/shard_map/ppermute | solution.py:1192
  169.3 11.5 %collective-permute-start.65 = (bf16[2,384,256]{2,1,0:T(8,128)(2,1)S(1)}, bf16[2,384,256]{2,1,0:T(8,128)(2,1)S(1)}, u32[]{:S(2)}, u32[]{:S(2)}) collective-permute-start(bf16[2,384,256]{2,1,0:T(8,128)(2,1)S(1)} %get-tuple-element.299), channel_id=1, source_target_pairs={{0,4},{2,6},{4,0},{6,2},{1,5},{3,7},{5,1},{7,3},{8,12},{10,14},{12... | collective-permute-start | bytes 1179656 | tf_op jit(solution)/shard_map/ppermute | solution.py:1192
  192.2 6.5 %collective-permute-start.73 = (bf16[4,768,256]{2,1,0:T(8,128)(2,1)S(1)}, bf16[4,768,256]{2,1,0:T(8,128)(2,1)S(1)}, u32[]{:S(2)}, u32[]{:S(2)}) collective-permute-start(bf16[4,768,256]{2,1,0:T(8,128)(2,1)S(1)} %get-tuple-element.309), channel_id=1, source_target_pairs={{0,1},{1,0},{2,3},{3,2},{4,5},{5,4},{6,7},{7,6},{8,9},{9,8},{10,11... | collective-permute-start | bytes 4718600 | tf_op jit(solution)/shard_map/ppermute | solution.py:1192
  197.0 14.8 %collective-permute-start.81 = (bf16[384,256]{1,0:T(8,128)(2,1)S(1)}, bf16[384,256]{1,0:T(8,128)(2,1)S(1)}, u32[]{:S(2)}, u32[]{:S(2)}) collective-permute-start(bf16[384,256]{1,0:T(8,128)(2,1)S(1)} %get-tuple-element.322), channel_id=1, source_target_pairs={{0,4},{2,6},{4,0},{6,2},{1,5},{3,7},{5,1},{7,3},{8,12},{10,14},{12... | collective-permute-start | bytes 589832 | tf_op jit(solution)/shard_map/ppermute | solution.py:1192
  197.4 15.8 %collective-permute-start.82 = (bf16[384,256]{1,0:T(8,128)(2,1)S(1)}, bf16[384,256]{1,0:T(8,128)(2,1)S(1)}, u32[]{:S(2)}, u32[]{:S(2)}) collective-permute-start(bf16[384,256]{1,0:T(8,128)(2,1)S(1)} %get-tuple-element.323), channel_id=1, source_target_pairs={{0,2},{2,0},{4,6},{6,4},{1,3},{3,1},{5,7},{7,5},{8,10},{10,8},{12,... | collective-permute-start | bytes 589832 | tf_op jit(solution)/shard_map/ppermute | solution.py:1192
  203.5 27.3 %collective-permute-start.83 = (bf16[2,384,256]{2,1,0:T(8,128)(2,1)S(1)}, bf16[2,384,256]{2,1,0:T(8,128)(2,1)S(1)}, u32[]{:S(2)}, u32[]{:S(2)}) collective-permute-start(bf16[2,384,256]{2,1,0:T(8,128)(2,1)S(1)} %get-tuple-element.327), channel_id=1, source_target_pairs={{0,2},{2,0},{4,6},{6,4},{1,3},{3,1},{5,7},{7,5},{8,10},{10,8},{12,... | collective-permute-start | bytes 1179656 | tf_op jit(solution)/shard_map/ppermute | solution.py:1192
  205.7 25.1 %collective-permute-start.84 = (bf16[2,384,256]{2,1,0:T(8,128)(2,1)S(1)}, bf16[2,384,256]{2,1,0:T(8,128)(2,1)S(1)}, u32[]{:S(2)}, u32[]{:S(2)}) collective-permute-start(bf16[2,384,256]{2,1,0:T(8,128)(2,1)S(1)} %get-tuple-element.328), channel_id=1, source_target_pairs={{0,4},{2,6},{4,0},{6,2},{1,5},{3,7},{5,1},{7,3},{8,12},{10,14},{12... | collective-permute-start | bytes 1179656 | tf_op jit(solution)/shard_map/ppermute | solution.py:1192
  211.8 6.6 %collective-permute-start.80 = (f32[8,128]{1,0:T(8,128)S(1)}, f32[8,128]{1,0:T(8,128)S(1)}, u32[]{:S(2)}, u32[]{:S(2)}) collective-permute-start(f32[8,128]{1,0:T(8,128)S(1)} %add.319), channel_id=1, source_target_pairs={{0,24},{8,16},{16,8},{24,0},{1,25},{9,17},{17,9},{25,1},{2,26},{10... | collective-permute-start | bytes 12296 | tf_op jit(solution)/shard_map/ppermute | solution.py:1192
  213.2 17.5 %collective-permute-start.78 = (f32[8,128]{1,0:T(8,128)S(1)}, f32[8,128]{1,0:T(8,128)S(1)}, u32[]{:S(2)}, u32[]{:S(2)}) collective-permute-start(f32[8,128]{1,0:T(8,128)S(1)} %add.319), channel_id=1, source_target_pairs={{0,8},{8,0},{16,24},{24,16},{1,9},{9,1},{17,25},{25,17},{2,10},{10... | collective-permute-start | bytes 12296 | tf_op jit(solution)/shard_map/ppermute | solution.py:1192
  214.8 20.2 %collective-permute-start.88 = (bf16[64,512]{1,0:T(8,128)(2,1)S(1)}, bf16[64,512]{1,0:T(8,128)(2,1)S(1)}, u32[]{:S(2)}, u32[]{:S(2)}) collective-permute-start(bf16[64,512]{1,0:T(8,128)(2,1)S(1)} %get-tuple-element.332), channel_id=1, source_target_pairs={{0,2},{2,4},{4,6},{1,3},{3,5},{5,7},{8,10},{10,12},{12,14},{9,11},... | collective-permute-start | bytes 196616 | tf_op jit(solution)/shard_map/ppermute | solution.py:1173
  218.3 17.1 %collective-permute-start.89 = (bf16[64,512]{1,0:T(8,128)(2,1)S(1)}, bf16[64,512]{1,0:T(8,128)(2,1)S(1)}, u32[]{:S(2)}, u32[]{:S(2)}) collective-permute-start(bf16[64,512]{1,0:T(8,128)(2,1)S(1)} %get-tuple-element.333), channel_id=1, source_target_pairs={{2,0},{4,2},{6,4},{3,1},{5,3},{7,5},{10,8},{12,10},{14,12},{11,9},... | collective-permute-start | bytes 196616 | tf_op jit(solution)/shard_map/ppermute | solution.py:1174
  230.7 7.9 %collective-permute-start.90 = (bf16[256,512]{1,0:T(8,128)(2,1)S(1)}, bf16[256,512]{1,0:T(8,128)(2,1)S(1)}, u32[]{:S(2)}, u32[]{:S(2)}) collective-permute-start(bf16[256,512]{1,0:T(8,128)(2,1)S(1)} %get-tuple-element.334), channel_id=1, source_target_pairs={{0,1},{1,0},{2,3},{3,2},{4,5},{5,4},{6,7},{7,6},{8,9},{9,8},{10,11... | collective-permute-start | bytes 786440 | tf_op jit(solution)/shard_map/ppermute | solution.py:1168
  244.0 12.0 %collective-permute-start.98 = (bf16[4,1216,256]{2,1,0:T(8,128)(2,1)S(1)}, bf16[4,1216,256]{2,1,0:T(8,128)(2,1)S(1)}, u32[]{:S(2)}, u32[]{:S(2)}) collective-permute-start(bf16[4,1216,256]{2,1,0:T(8,128)(2,1)S(1)} %get-tuple-element.355), channel_id=1, source_target_pairs={{0,1},{1,0},{2,3},{3,2},{4,5},{5,4},{6,7},{7,6},{8,9},{9,8},{10,11... | collective-permute-start | bytes 7471112 | tf_op jit(solution)/shard_map/ppermute | solution.py:1192
  246.6 6.1 %collective-permute-start.96 = (f32[8,128]{1,0:T(8,128)S(1)}, f32[8,128]{1,0:T(8,128)S(1)}, u32[]{:S(2)}, u32[]{:S(2)}) collective-permute-start(f32[8,128]{1,0:T(8,128)S(1)} %add.326), channel_id=1, source_target_pairs={{0,6},{2,4},{4,2},{6,0},{1,7},{3,5},{5,3},{7,1},{8,14},{10,12},{12... | collective-permute-start | bytes 12296 | tf_op jit(solution)/shard_map/ppermute | solution.py:1192
  247.6 6.4 %collective-permute-start.94 = (f32[8,128]{1,0:T(8,128)S(1)}, f32[8,128]{1,0:T(8,128)S(1)}, u32[]{:S(2)}, u32[]{:S(2)}) collective-permute-start(f32[8,128]{1,0:T(8,128)S(1)} %add.326), channel_id=1, source_target_pairs={{0,2},{2,0},{4,6},{6,4},{1,3},{3,1},{5,7},{7,5},{8,10},{10,8},{12,... | collective-permute-start | bytes 12296 | tf_op jit(solution)/shard_map/ppermute | solution.py:1192
  249.9 6.1 %collective-permute-start.97 = (bf16[2,384,128]{2,1,0:T(8,128)(2,1)S(1)}, bf16[2,384,128]{2,1,0:T(8,128)(2,1)S(1)}, u32[]{:S(2)}, u32[]{:S(2)}) collective-permute-start(bf16[2,384,128]{2,1,0:T(8,128)(2,1)S(1)} %get-tuple-element.340), channel_id=1, source_target_pairs={{0,8},{8,0},{16,24},{24,16},{1,9},{9,1},{17,25},{25,17},{2,10},{10... | collective-permute-start | bytes 589832 | tf_op jit(solution)/shard_map/ppermute | solution.py:1192
  250.1 10.4 %collective-permute-start.102 = (bf16[64,256]{1,0:T(8,128)(2,1)S(1)}, bf16[64,256]{1,0:T(8,128)(2,1)S(1)}, u32[]{:S(2)}, u32[]{:S(2)}) collective-permute-start(bf16[64,256]{1,0:T(8,128)(2,1)S(1)} %get-tuple-element.358), channel_id=1, source_target_pairs={{0,2},{2,4},{4,6},{1,3},{3,5},{5,7},{8,10},{10,12},{12,14},{9,11},... | collective-permute-start | bytes 98312 | tf_op jit(solution)/shard_map/ppermute | solution.py:1173
  252.7 8.0 %collective-permute-start.103 = (bf16[64,256]{1,0:T(8,128)(2,1)S(1)}, bf16[64,256]{1,0:T(8,128)(2,1)S(1)}, u32[]{:S(2)}, u32[]{:S(2)}) collective-permute-start(bf16[64,256]{1,0:T(8,128)(2,1)S(1)} %get-tuple-element.359), channel_id=1, source_target_pairs={{2,0},{4,2},{6,4},{3,1},{5,3},{7,5},{10,8},{12,10},{14,12},{11,9},... | collective-permute-start | bytes 98312 | tf_op jit(solution)/shard_map/ppermute | solution.py:1174
  262.4 21.9 %collective-permute-start.113 = (bf16[2,608,256]{2,1,0:T(8,128)(2,1)S(1)}, bf16[2,608,256]{2,1,0:T(8,128)(2,1)S(1)}, u32[]{:S(2)}, u32[]{:S(2)}) collective-permute-start(bf16[2,608,256]{2,1,0:T(8,128)(2,1)S(1)} %get-tuple-element.375), channel_id=1, source_target_pairs={{0,2},{2,0},{4,6},{6,4},{1,3},{3,1},{5,7},{7,5},{8,10},{10,8},{12,... | collective-permute-start | bytes 1867784 | tf_op jit(solution)/shard_map/ppermute | solution.py:1192
  263.8 20.5 %collective-permute-start.114 = (bf16[2,608,256]{2,1,0:T(8,128)(2,1)S(1)}, bf16[2,608,256]{2,1,0:T(8,128)(2,1)S(1)}, u32[]{:S(2)}, u32[]{:S(2)}) collective-permute-start(bf16[2,608,256]{2,1,0:T(8,128)(2,1)S(1)} %get-tuple-element.376), channel_id=1, source_target_pairs={{0,4},{2,6},{4,0},{6,2},{1,5},{3,7},{5,1},{7,3},{8,12},{10,14},{12... | collective-permute-start | bytes 1867784 | tf_op jit(solution)/shard_map/ppermute | solution.py:1192
  275.3 21.7 %collective-permute-start.115 = (bf16[4,480,256]{2,1,0:T(8,128)(2,1)S(1)}, bf16[4,480,256]{2,1,0:T(8,128)(2,1)S(1)}, u32[]{:S(2)}, u32[]{:S(2)}) collective-permute-start(bf16[4,480,256]{2,1,0:T(8,128)(2,1)S(1)} %get-tuple-element.380), channel_id=1, source_target_pairs={{0,1},{1,0},{2,3},{3,2},{4,5},{5,4},{6,7},{7,6},{8,9},{9,8},{10,11... | collective-permute-start | bytes 2949128 | tf_op jit(solution)/shard_map/ppermute | solution.py:1192
  278.0 5.7 %collective-permute-start.111 = (bf16[384,256]{1,0:T(8,128)(2,1)S(1)}, bf16[384,256]{1,0:T(8,128)(2,1)S(1)}, u32[]{:S(2)}, u32[]{:S(2)}) collective-permute-start(bf16[384,256]{1,0:T(8,128)(2,1)S(1)} %get-tuple-element.370), channel_id=1, source_target_pairs={{0,4},{2,6},{4,0},{6,2},{1,5},{3,7},{5,1},{7,3},{8,12},{10,14},{12... | collective-permute-start | bytes 589832 | tf_op jit(solution)/shard_map/ppermute | solution.py:1192
  278.6 5.7 %collective-permute-start.112 = (bf16[384,256]{1,0:T(8,128)(2,1)S(1)}, bf16[384,256]{1,0:T(8,128)(2,1)S(1)}, u32[]{:S(2)}, u32[]{:S(2)}) collective-permute-start(bf16[384,256]{1,0:T(8,128)(2,1)S(1)} %get-tuple-element.371), channel_id=1, source_target_pairs={{0,2},{2,0},{4,6},{6,4},{1,3},{3,1},{5,7},{7,5},{8,10},{10,8},{12,... | collective-permute-start | bytes 589832 | tf_op jit(solution)/shard_map/ppermute | solution.py:1192
  285.1 7.2 %collective-permute-start.122 = (bf16[608,256]{1,0:T(8,128)(2,1)S(1)}, bf16[608,256]{1,0:T(8,128)(2,1)S(1)}, u32[]{:S(2)}, u32[]{:S(2)}) collective-permute-start(bf16[608,256]{1,0:T(8,128)(2,1)S(1)} %get-tuple-element.404), channel_id=1, source_target_pairs={{0,4},{2,6},{4,0},{6,2},{1,5},{3,7},{5,1},{7,3},{8,12},{10,14},{12... | collective-permute-start | bytes 933896 | tf_op jit(solution)/shard_map/ppermute | solution.py:1192
  286.7 6.9 %collective-permute-start.123 = (bf16[608,256]{1,0:T(8,128)(2,1)S(1)}, bf16[608,256]{1,0:T(8,128)(2,1)S(1)}, u32[]{:S(2)}, u32[]{:S(2)}) collective-permute-start(bf16[608,256]{1,0:T(8,128)(2,1)S(1)} %get-tuple-element.406), channel_id=1, source_target_pairs={{0,2},{2,0},{4,6},{6,4},{1,3},{3,1},{5,7},{7,5},{8,10},{10,8},{12,... | collective-permute-start | bytes 933896 | tf_op jit(solution)/shard_map/ppermute | solution.py:1192
  288.7 42.6 %collective-permute-start.119 = (bf16[384,128]{1,0:T(8,128)(2,1)S(1)}, bf16[384,128]{1,0:T(8,128)(2,1)S(1)}, u32[]{:S(2)}, u32[]{:S(2)}) collective-permute-start(bf16[384,128]{1,0:T(8,128)(2,1)S(1)} %get-tuple-element.389), channel_id=1, source_target_pairs={{0,16},{8,24},{16,0},{24,8},{1,17},{9,25},{17,1},{25,9},{2,18},{10... | collective-permute-start | bytes 294920 | tf_op jit(solution)/shard_map/ppermute | solution.py:1192
  294.4 19.2 %collective-permute-start.124 = (bf16[2,704,128]{2,1,0:T(8,128)(2,1)S(1)}, bf16[2,704,128]{2,1,0:T(8,128)(2,1)S(1)}, u32[]{:S(2)}, u32[]{:S(2)}) collective-permute-start(bf16[2,704,128]{2,1,0:T(8,128)(2,1)S(1)} %get-tuple-element.408), channel_id=1, source_target_pairs={{0,8},{8,0},{16,24},{24,16},{1,9},{9,1},{17,25},{25,17},{2,10},{10... | collective-permute-start | bytes 1081352 | tf_op jit(solution)/shard_map/ppermute | solution.py:1192
  303.5 5.7 %collective-permute-start.120 = (bf16[2,384,128]{2,1,0:T(8,128)(2,1)S(1)}, bf16[2,384,128]{2,1,0:T(8,128)(2,1)S(1)}, u32[]{:S(2)}, u32[]{:S(2)}) collective-permute-start(bf16[2,384,128]{2,1,0:T(8,128)(2,1)S(1)} %get-tuple-element.396), channel_id=1, source_target_pairs={{0,8},{8,0},{16,24},{24,16},{1,9},{9,1},{17,25},{25,17},{2,10},{10... | collective-permute-start | bytes 589832 | tf_op jit(solution)/shard_map/ppermute | solution.py:1192
  303.6 6.2 %collective-permute-start.126 = (bf16[2,240,256]{2,1,0:T(8,128)(2,1)S(1)}, bf16[2,240,256]{2,1,0:T(8,128)(2,1)S(1)}, u32[]{:S(2)}, u32[]{:S(2)}) collective-permute-start(bf16[2,240,256]{2,1,0:T(8,128)(2,1)S(1)} %get-tuple-element.416), channel_id=1, source_target_pairs={{0,2},{2,0},{4,6},{6,4},{1,3},{3,1},{5,7},{7,5},{8,10},{10,8},{12,... | collective-permute-start | bytes 737288 | tf_op jit(solution)/shard_map/ppermute | solution.py:1192
  304.2 7.6 %collective-permute-start.127 = (bf16[2,240,256]{2,1,0:T(8,128)(2,1)S(1)}, bf16[2,240,256]{2,1,0:T(8,128)(2,1)S(1)}, u32[]{:S(2)}, u32[]{:S(2)}) collective-permute-start(bf16[2,240,256]{2,1,0:T(8,128)(2,1)S(1)} %get-tuple-element.418), channel_id=1, source_target_pairs={{0,4},{2,6},{4,0},{6,2},{1,5},{3,7},{5,1},{7,3},{8,12},{10,14},{12... | collective-permute-start | bytes 737288 | tf_op jit(solution)/shard_map/ppermute | solution.py:1192
  309.2 6.4 %collective-permute-start.132 = (bf16[4,160,256]{2,1,0:T(8,128)(2,1)S(1)}, bf16[4,160,256]{2,1,0:T(8,128)(2,1)S(1)}, u32[]{:S(2)}, u32[]{:S(2)}) collective-permute-start(bf16[4,160,256]{2,1,0:T(8,128)(2,1)S(1)} %get-tuple-element.435), channel_id=1, source_target_pairs={{0,1},{1,0},{2,3},{3,2},{4,5},{5,4},{6,7},{7,6},{8,9},{9,8},{10,11... | collective-permute-start | bytes 983048 | tf_op jit(solution)/shard_map/ppermute | solution.py:1192
  309.8 24.0 %collective-permute-start.121 = (bf16[384,128]{1,0:T(8,128)(2,1)S(1)}, bf16[384,128]{1,0:T(8,128)(2,1)S(1)}, u32[]{:S(2)}, u32[]{:S(2)}) collective-permute-start(bf16[384,128]{1,0:T(8,128)(2,1)S(1)} %get-tuple-element.398), channel_id=1, source_target_pairs={{0,16},{8,24},{16,0},{24,8},{1,17},{9,25},{17,1},{25,9},{2,18},{10... | collective-permute-start | bytes 294920 | tf_op jit(solution)/shard_map/ppermute | solution.py:1192
  321.0 16.3 %collective-permute-start.125 = (bf16[704,128]{1,0:T(8,128)(2,1)S(1)}, bf16[704,128]{1,0:T(8,128)(2,1)S(1)}, u32[]{:S(2)}, u32[]{:S(2)}) collective-permute-start(bf16[704,128]{1,0:T(8,128)(2,1)S(1)} %get-tuple-element.410), channel_id=1, source_target_pairs={{0,16},{8,24},{16,0},{24,8},{1,17},{9,25},{17,1},{25,9},{2,18},{10... | collective-permute-start | bytes 540680 | tf_op jit(solution)/shard_map/ppermute | solution.py:1192
  325.0 10.4 %collective-permute-start.136 = (bf16[176,128]{1,0:T(8,128)(2,1)S(1)}, bf16[176,128]{1,0:T(8,128)(2,1)S(1)}, u32[]{:S(2)}, u32[]{:S(2)}) collective-permute-start(bf16[176,128]{1,0:T(8,128)(2,1)S(1)} %get-tuple-element.441), channel_id=1, source_target_pairs={{0,8},{8,0},{16,24},{24,16},{1,9},{9,1},{17,25},{25,17},{2,10},{10... | collective-permute-start | bytes 135176 | tf_op jit(solution)/shard_map/ppermute | solution.py:1192
  328.8 6.7 %collective-permute-start.137 = (bf16[176,128]{1,0:T(8,128)(2,1)S(1)}, bf16[176,128]{1,0:T(8,128)(2,1)S(1)}, u32[]{:S(2)}, u32[]{:S(2)}) collective-permute-start(bf16[176,128]{1,0:T(8,128)(2,1)S(1)} %get-tuple-element.442), channel_id=1, source_target_pairs={{0,16},{8,24},{16,0},{24,8},{1,17},{9,25},{17,1},{25,9},{2,18},{10... | collective-permute-start | bytes 135176 | tf_op jit(solution)/shard_map/ppermute | solution.py:1192
  331.3 5.9 %collective-permute-start.138 = (bf16[176,128]{1,0:T(8,128)(2,1)S(1)}, bf16[176,128]{1,0:T(8,128)(2,1)S(1)}, u32[]{:S(2)}, u32[]{:S(2)}) collective-permute-start(bf16[176,128]{1,0:T(8,128)(2,1)S(1)} %get-tuple-element.443), channel_id=1, source_target_pairs={{0,24},{8,16},{16,8},{24,0},{1,25},{9,17},{17,9},{25,1},{2,26},{10... | collective-permute-start | bytes 135176 | tf_op jit(solution)/shard_map/ppermute | solution.py:1192
  (102 other events, 590.0 us)
where the time goes:
time: 341 us
  starting transfers between devices  147 us (43%)
  waiting for transfers between devices  85 us (25%)
  Pallas kernels  71.5 us (21%)
  blocking collectives  35.2 us (10%)
    ppermute x108, starting transfers between devices, flip(): lax.ppermute(x, axis, [(i, i ^ step) for i in range(lax.axis_size(axis))])  119 us
    ppermute x108, waiting for transfers between devices, flip(): lax.ppermute(x, axis, [(i, i ^ step) for i in range(lax.axis_size(axis))])  80.4 us
    pallas_call x43, Pallas kernels, call(): pl.pallas_call(wrapped, out_shape=[jax.ShapeDtypeStruct(shape, kind) for...  71.5 us
    all_to_all x3, blocking collectives, exchange(): return lax.all_to_all(block, ALL_AXES, 0, 0)  35.2 us
    ppermute x3, starting transfers between devices, halo(): below = lax.ppermute(top, HA, [(i + 1, i) for i in range(count - 1)])  15.3 us
    ppermute x3, starting transfers between devices, halo(): above = lax.ppermute(bottom, HA, [(i, i + 1) for i in range(count - 1)])  9.73 us
  transfers between devices with their start and end apart: 139, of which 64 were waited for; matrix products, arithmetic and copies ran while one was open for 0% of the time, Pallas kernels for 11%

commit v1 on v0

--- a/solution.py
+++ b/solution.py
@@ -743,20 +743,44 @@
     spatial_gradient(parts, shape, si, sf, R.dy_fs, (R.h0, R.h1, R.h2, R.h3, R.h4), R.pad, R.dz_f)
     _, back_f = spatial_back(R.pad, shape, None, R.fs_bd)
     finish_spatial(ft, L.zft[...], back_f, R.dy_ft, R.pay, 4)
-    back = temporal_slow(L, frame, inside, sf, total, 0, R.dy_st, R.dlow, R.st_w, R.dz_st, R.dy_lat, R.pay, 0)
+    temporal_slow(L, frame, inside, sf, total, 0, R.dy_st, R.dlow, R.st_w, R.dz_st, R.dy_lat, R.pay, 0)
     fill_rows(R.pay, 6, 8)
+
+
+def kernel_low_input(dz_st, dlow, st_w, dslow):
     for c in range(0, DS, 256):
-        R.dslow[:, c : c + 256] = back(slice(c, c + 256))
+        cols = slice(c, c + 256)
+        part = dlow[:, cols]
+        for j in range(3):
+            part = part + dot_nt(dz_st[:, j * BS : (j + 1) * BS], st_w[0, j, cols, :])
+        dslow[:, cols] = part
 
 
 def back_low_lateral(shape, R, inside, si, sf):
     L = R.layer("b_")
-    frame = shape[1] * shape[2]
+    lat, ft = norms_of(L, sf, "lat", "ft")
     total = R.recv[...]
-    grad = temporal_fast(L, frame, inside, sf, total, 4, R.dy_ft, R.dz_ft, R.dz_fk, R.fk_w, R.ft_band)
-    grad = lateral_back(L, frame, inside, sf, total, 0, R.dy_lat, R.lat_w, R.dz_lat, grad)
+    folded = fold_phases(total)
+    R.dz_lat[...] = lat.back(
+        R.dy_lat[...], lat.hat(L.zlat[...]), inside, wide(total, 0, 2), wide(total, 2, 2), sf[0]
+    ).astype(BF16)
+    R.dz_ft[...] = ft.back(
+        R.dy_ft[...], ft.hat(L.zft[...]), inside[:, :LANES], wide(folded, 4, 1), wide(folded, 5, 1), sf[1]
+    ).astype(BF16)
+
+
+def kernel_low_fast_input(frame, dz_lat, dz_ft, dz_fk, lat_w, fk_w, ft_band, dfast):
     for p in range(ALPHA):
-        R.dfast[:, p] = grad(p).reshape(shape[0], frame, DF)
+        part = dot_nt(dz_fk[:, p * DF : (p + 1) * DF], fk_w[0]) + dot_nt(dz_ft[...], ft_band[p + 1])
+        if p == ALPHA - 1:
+            part = part + up(dot_nt(dz_ft[...], ft_band[0]), frame)
+        if p == 0:
+            part = part + down(dot_nt(dz_ft[...], ft_band[5]), frame)
+        if p < 3:
+            part = part + dot_nt(dz_lat[...], lat_w[0, p + 2])
+        if p >= 2:
+            part = part + up(dot_nt(dz_lat[...], lat_w[0, p - 2]), frame)
+        dfast[:, p] = part.reshape(dfast.shape[0], frame, DF)
 
 
 def kernel_back_skip(dz_sk, sk_w, dlow):
@@ -1039,6 +1063,11 @@
         self.layer = layer
 
 
+class Ready:
+    def __init__(self, array):
+        self.array = array
+
+
 class Load:
     def __init__(self, array):
         self.array = array
@@ -1079,26 +1108,31 @@
     return (valid[clip] * frame, ha, wa, clip), [v[:, :1] for v in vectors]
 
 
-def call(body, scalars, operands, outs, scratch=(), limit=16, pinned=False):
+def call(body, scalars, operands, outs, scratch=(), limit=16, pinned=False, ahead=()):
     mode, scalars = (None, ()) if not scalars else (scalars[0], scalars[1:3])
+    operands = list(operands) + list(ahead)
     count, first = len(operands), len(scalars)
+    kept = len(outs)
+    outs = list(outs) + [(x.array.shape[1:], x.array.dtype) for x in ahead]
     weights = [i for i, x in enumerate(operands) if isinstance(x, (Weight, Load))]
     results = [i for i, x in enumerate(outs) if isinstance(x, Out)]
-    arrays = [x.array if isinstance(x, (Weight, Layer, Load)) else x for x in operands]
+    arrays = [x.array if isinstance(x, (Weight, Layer, Load, Ready)) else x for x in operands]
     if pinned:
         for i in weights:
             arrays[i] = pltpu.with_memory_space_constraint(arrays[i], pltpu.HBM)
     layered = [isinstance(x, Weight) for x in operands]
     shapes = [(x.shape, x.kind) if isinstance(x, Out) else x for x in outs]
-    buffers = [pltpu.VMEM(arrays[i].shape[1:] if layered[i] else arrays[i].shape, arrays[i].dtype) for i in weights]
+    inward = weights[: len(weights) - len(ahead)]
+    buffers = [pltpu.VMEM(arrays[i].shape[1:] if layered[i] else arrays[i].shape, arrays[i].dtype) for i in inward]
     buffers += [pltpu.VMEM(*shapes[i]) for i in results]
     own = first + count + len(outs)
+    copies = len(buffers) + len(ahead)
 
     def wrapped(*refs):
         refs = list(refs)
         inner, rest = refs[own : own + len(buffers)], refs[own + len(buffers) :]
         arriving, leaving = [], []
-        for n, i in enumerate(weights):
+        for n, i in enumerate(inward):
             source = refs[first + i].at[operands[i].layer] if layered[i] else refs[first + i]
             copy = pltpu.make_async_copy(source, inner[n], rest[-1].at[n])
             copy.start()
@@ -1107,8 +1141,15 @@
         for i, x in enumerate(operands):
             if isinstance(x, Layer):
                 refs[first + i] = refs[first + i].at[x.layer]
+            if isinstance(x, Ready):
+                refs[first + i] = Arriving(None, refs[first + i], True)
+        later = []
+        for n, x in enumerate(ahead):
+            source = refs[first + count - len(ahead) + n].at[x.layer]
+            later.append(pltpu.make_async_copy(source, refs[first + count + kept + n], rest[-1].at[len(buffers) + n]))
+            later[-1].start()
         for n, i in enumerate(results):
-            n += len(weights)
+            n += len(inward)
             leaving.append(pltpu.make_async_copy(inner[n], refs[first + count + i], rest[-1].at[n]))
             refs[first + count + i] = inner[n]
         given = ()
@@ -1117,13 +1158,14 @@
             ints, vectors = scalar_values(refs[0], refs[1], t_frame, tiles) if mode[0] == "all" else (
                 (None, refs[0][0], refs[0][1], refs[0][2]), None)
             given = (ints, vectors) if mode[0] == "all" else (ints,)
-        body(*given, *refs[first:own], *(rest[:-1] if buffers else rest))
+        given_refs = refs[first : first + count - len(ahead)] + refs[first + count : first + count + kept]
+        body(*given, *given_refs, *(rest[:-1] if copies else rest))
         for copy in leaving:
             copy.start()
         for one in arriving:
             if one.copy is not None:
                 one.copy.wait()
-        for copy in leaving:
+        for copy in leaving + later:
             copy.wait()
 
     def space(i, some):
@@ -1136,8 +1178,8 @@
         out_specs=[space(i, results) for i in range(len(outs))],
         scratch_shapes=buffers
         + [pltpu.VMEM(shape, kind) for shape, kind in scratch]
-        + ([pltpu.SemaphoreType.DMA((len(buffers),))] if buffers else []),
-        cost_estimate=pl.CostEstimate(flops=2000000000, bytes_accessed=4000000, transcendentals=0),
+        + ([pltpu.SemaphoreType.DMA((copies,))] if copies else []),
+        cost_estimate=pl.CostEstimate(flops=3000000000, bytes_accessed=6000000, transcendentals=0),
         compiler_params=pltpu.CompilerParams(vmem_limit_bytes=limit << 20),
     )(*scalars, *arrays)
 
@@ -1193,10 +1235,10 @@
 
 
 ORDERS = ((WA, HA, CLIP), (WA, HA, CLIP), (WA, CLIP, HA), (WA, HA, CLIP), (WA, CLIP, HA), (WA, HA, CLIP), (WA, CLIP, HA))
-LAUNCH = {(1, 'wa'): ('A1',), (3, 'wa'): ('ST1',), (5, 'wa'): ('A0',), (6, 'wa'): ('T0',), (3, 'ha'): ('A1',), (5, 'ha'): ('ST1',)}
-LAND = {(1, 'clip'): ('A1',), (2, 'ha'): ('A1',), (3, 'clip'): ('ST1',), (4, 'ha'): ('A1', 'ST1'), (5, 'clip'): ('A1', 'A0'), (6, 'ha'): ('ST1', 'A0', 'T0')}
-BUNDLES = {1: [('A1', False, [('pl', 1)])], 3: [('ST1', False, [('ss', 1), ('st', 1)])], 5: [('A0', False, [('pl', 0), ('ss', 0), ('lat', 1), ('sm', 1)])], 6: [('T0', False, [('st', 0)])], 7: [('L0', True, [('lat', 0), ('sm', 0)])]}
-WAIT = {(2, HA, "A1"), (6, HA, "T0"), (6, HA, "ST1"), (4, HA, "ST1")}
+LAUNCH = {(1, 'wa'): ('A1',), (3, 'wa'): ('ST1',), (5, 'wa'): ('A0',), (3, 'ha'): ('A1',), (5, 'ha'): ('ST1',), (6, 'ha'): ('A0',)}
+LAND = {(1, 'clip'): ('A1',), (2, 'ha'): ('A1',), (3, 'clip'): ('ST1',), (4, 'ha'): ('A1', 'ST1'), (5, 'clip'): ('A1', 'A0'), (6, 'ha'): ('ST1',)}
+BUNDLES = {1: [('A1', False, [('pl', 1)])], 3: [('ST1', False, [('ss', 1), ('st', 1)])], 5: [('A0', False, [('pl', 0), ('ss', 0), ('lat', 1), ('sm', 1)])], 7: [('L0', True, [('st', 0), ('lat', 0), ('sm', 0)])]}
+WAIT = {(5, CLIP, "A0"), (2, HA, "A1"), (6, HA, "ST1"), (4, HA, "ST1")}
 
 
 def local(
@@ -1261,12 +1303,13 @@
     )
     recv, around = sum_with_halo(sent, top, bottom, z16)
     recv = sum_over(recv, CLIP)
-    gb_all, fs_bd, fe_bd = call(
+    gb_all, fs_bd, fe_bd, *ahead = call(
         kernel_prepare,
         (),
         [Load(gains), Load(biases), Load(fast_spatial_w), Load(fast_expand_w)],
         [((LAYERS, 2, GB_ROWS, LANES), F32), ((LAYERS, 3, 3, LANES, LANES), BF16), ((LAYERS, LANES, ALPHA * DF), BF16)],
         pinned=True,
+        ahead=[Weight(slow_temporal_w, 0), Weight(slow_skip_w, 0)],
     )
     gb = [Layer(gb_all, l) for l in range(LAYERS)]
     before = None
@@ -1276,10 +1319,9 @@
         low, zst, z16, top, bottom, zsk, af9, zfs, sent = call(
             bind(kernel_temporal, l == 0, shape),
             scalars,
-            start + [zlat, zft, *around, Weight(slow_temporal_w, l), Weight(slow_skip_w, l), Layer(fs_bd, l)],
+            start + [zlat, zft, *around, Ready(ahead[0]), Ready(ahead[1]), Layer(fs_bd, l)],
             [act(CC, BF16), act(BS), *edges(BS, 24), act(DS), act(9 * LANES, BF16), act(LANES), pay(24)],
             [pad_fast],
-            pinned=l == 0,
         )
         tot_lat = recv
         if l > 0:
@@ -1308,13 +1350,14 @@
                 [pay(16)],
             )
         else:
-            bt, zse, sent, tot_ss, fb, zlat, zft, z16, top, bottom, zfk = call(
+            bt, zse, sent, tot_ss, fb, zlat, zft, z16, top, bottom, zfk, *ahead = call(
                 bind(kernel_expand, False, shape),
                 scalars,
                 [recv, gb[l], zss, Weight(slow_expand_w, l), tot_lat, zfe, zfk,
                  Weight(lateral_w, l + 1), Layer(band, l + 1), Weight(fast_skip_w, l + 1)],
                 [act(BS, BF16), act(DS), pay(24), pay(8),
                  act(512, BF16), act(DL), act(LANES), *edges(LANES, 24), act(512)],
+                ahead=[Weight(slow_temporal_w, l + 1), Weight(slow_skip_w, l + 1)],
             )
         if last:
             recv = exchange(sent)
@@ -1328,16 +1371,17 @@
     for l in range(LAYERS):
         saved[l]["gb"] = gb[l]
 
-    def stage(body, ins, outs, scratch=(), limit=16):
+    def stage(body, ins, outs, scratch=(), limit=16, ahead=()):
         names = list(ins) + list(outs) + [name for name, _ in scratch]
 
         def named(ints, vectors, *refs):
             body(shape, Refs(names, refs), inside_rows(rows, 256, ints[0]), ints, vectors)
 
         results = call(
-            named, scalars, list(ins.values()), list(outs.values()), [kind for _, kind in scratch], limit
+            named, scalars, list(ins.values()), list(outs.values()), [kind for _, kind in scratch], limit,
+            ahead=list(ahead),
         )
-        return dict(zip(outs, results))
+        return dict(zip(outs, results[: len(outs)]), ahead=results[len(outs) :])
 
     def layer(prefix, l, *names):
         return {prefix + name: saved[l][name] for name in names}
@@ -1448,6 +1492,7 @@
             limit=24,
         )
         running[name] = Running(chain(*pair, jobs), jobs, layers)
+        running[name].direct = chain is direct_chain
 
     def skip_back(l, r):
         (r["dlow"],) = call(kernel_back_skip, (), [r["dz_sk"], Weight(slow_skip_w, l)], [act(CC)])
@@ -1469,7 +1514,7 @@
                 x, around[:] = sum_with_halo(x, edge_rows["top"], edge_rows["bottom"], edge_rows["whole"])
             elif axis == CLIP:
                 x = sum_over(x, axis)
-            for name in LAUNCH.get((n, axis), ()) + tuple(w[2] for w in WAIT if w[:2] == (n, axis)):
+            for name in LAUNCH.get((n, axis), ()) + tuple(w[2] for w in WAIT if w[:2] == (n, axis) and w != (5, CLIP, "A0")):
                 running[name].launch(x)
         totals.append(x)
         return x
@@ -1506,6 +1551,7 @@
              **around_of(halo(r1["whole"], r1["top"], r1["bottom"])), ss_w=Weight(slow_spatial_w, one), fs_bd=Layer(fs_bd, one)),
         dict(dz=act(BS + LANES, BF16), dy_st=act(BS), dy_ft=act(LANES), pay=pay(8)),
         [("pad", pad_both)],
+        ahead=[Weight(slow_temporal_w, one)],
     ))
     r1["dz_f"] = r1["dz"]
     start_bundles()
@@ -1514,7 +1560,7 @@
         back_temporal,
         dict(recv=recv, **layer("a_", one, "gb", "tot_sk", "tot_lat", "zst", "zft", "zlat"),
              **layer("b_", two, *slow_names), dy_st=r1["dy_st"], dy_ft=r1["dy_ft"], dlow=r1["dlow"], dz_fk=r1["dz_fk"],
-             st_w=Weight(slow_temporal_w, one), ft_band=Layer(band, one), fk_w=Weight(fast_skip_w, one)),
+             st_w=Ready(r1["ahead"][0]), ft_band=Layer(band, one), fk_w=Weight(fast_skip_w, one)),
         dict(dz_st=act(3 * BS, BF16), dz_ft=act(LANES, BF16), dfast=act(512), dy_lat=act(DL), du_s=act(DS), pay=pay(32)),
     ))
     start_bundles()
@@ -1537,6 +1583,7 @@
         dict(dz_fe=act(512, BF16), dz_fk=act(512, BF16), dy_fs=act(LANES), **edge(2 * LANES), dz=act(BS, BF16), dy_st=act(BS),
              pay=pay(8)),
         [("pad", pad_slow)],
+        ahead=[Weight(slow_temporal_w, two)],
     )
     r0.update(fast)
     start_bundles()
@@ -1544,24 +1591,32 @@
     r0.update(stage(
         back_low_temporal,
         dict(recv=recv, **layer("b_", two, "gb", "tot_sk", "tot_lat", "zst", "zft", "zlat", "zfs"), dy_fs=r0["dy_fs"],
-             **around_of(halo(r0["whole"], r0["top"], r0["bottom"])), dy_st=r0["dy_st"], dlow=r0["dlow"], st_w=Weight(slow_temporal_w, two), fs_bd=Layer(fs_bd, two)),
-        dict(dz_f=act(LANES, BF16), dy_ft=act(LANES), dz_st=act(3 * BS, BF16), dy_lat=act(DL), dslow=Out((rows, DS), F32),
-             pay=pay(8)),
+             **around_of(halo(r0["whole"], r0["top"], r0["bottom"])), dy_st=r0["dy_st"], dlow=r0["dlow"], st_w=Ready(r0["ahead"][0]), fs_bd=Layer(fs_bd, two)),
+        dict(dz_f=act(LANES, BF16), dy_ft=act(LANES), dz_st=act(3 * BS, BF16), dy_lat=act(DL), pay=pay(8)),
         [("pad", pad_fast)],
     ))
     start_bundles()
     recv = total_of(r0["pay"])
     r0.update(stage(
         back_low_lateral,
-        dict(recv=recv, **layer("b_", two, "gb", "tot_lat", "zft", "zlat"), dy_ft=r0["dy_ft"], dy_lat=r0["dy_lat"],
-             dz_fk=r0["dz_fk"], lat_w=Weight(lateral_w, two), ft_band=Layer(band, two), fk_w=Weight(fast_skip_w, two)),
-        dict(dz_ft=act(LANES, BF16), dz_lat=act(DL, BF16), dfast=Out((t, ALPHA, frame, DF), F32)),
+        dict(recv=recv, **layer("b_", two, "gb", "tot_lat", "zft", "zlat"), dy_ft=r0["dy_ft"], dy_lat=r0["dy_lat"]),
+        dict(dz_ft=act(LANES, BF16), dz_lat=act(DL, BF16)),
     ))
     start_bundles()
     ways = [chain.finish() for chain in running.values()]
+    _, late_lat, late_st = after(running["L0"].state[1][0][0], r0["dz_lat"], r0["dz_st"])
     while ways:
         ways = [way for way in ways if next(way, 0) is None]
-    out_slow, out_fast, grad_slow, grad_fast = r1["out_slow"], r1["out_fast"], r0["dslow"], r0["dfast"]
+    out_slow, out_fast = r1["out_slow"], r1["out_fast"]
+    (grad_slow,) = call(
+        kernel_low_input, (), [late_st, r0["dlow"], Weight(slow_temporal_w, two)], [Out((rows, DS), F32)]
+    )
+    (grad_fast,) = call(
+        bind(kernel_low_fast_input, frame),
+        (),
+        [late_lat, r0["dz_ft"], r0["dz_fk"], Weight(lateral_w, two), Weight(fast_skip_w, two), Layer(band, two)],
+        [Out((t, ALPHA, frame, DF), F32)],
+    )
     where = [
         [(6, 0, 2, 2), (5, 0, 2, 2), (4, 0, 2, 2), (3, 8, 8, 8), (3, 8, 16, 8), (6, 4, 1, 1), (5, 4, 1, 1), (4, 4, 1, 1),
          (4, 4, 2, 1)],
@@ -1587,7 +1642,7 @@
         found = {}
         for chain in chains:
             got = [x.astype(F32) for x in chain.state[0]]
-            if chain.jobs != ("lat", "sm"):
+            if not chain.direct:
                 total = jnp.concatenate([got[0] + got[1], got[2] + got[3]], axis=0).astype(BF16)
             else:
                 total = sum(got).astype(BF16)

time: 341 us -> 330 us (0.968)
  Pallas kernels: 71.5 us -> 64.8 us
  waiting for transfers between devices: 85 us -> 79.6 us
    pallas_call x43 -> x40, Pallas kernels: 71.5 us -> 64.8 us  [call(): pl.pallas_call(wrapped, out_shape=[jax.ShapeDtypeStruct(shape, kind) for...]
    ppermute x108 -> x101, waiting for transfers between devices: 80.4 us -> 74.2 us  [flip(): lax.ppermute(x, axis, [(i, i ^ step) for i in range(lax.axis_size(axis))])]
    ppermute x108 -> x101, starting transfers between devices: 119 us -> 122 us  [flip(): lax.ppermute(x, axis, [(i, i ^ step) for i in range(lax.axis_size(axis))])]
  transfers between devices with their start and end apart: 139 -> 132, of which waited for: 64 -> 60; matrix products, arithmetic and copies ran while one was open for 0% -> 0% of each run, Pallas kernels for 11% -> 11%
where the time goes in v1:
time: 330 us
  starting transfers between devices  148 us (45%)
  waiting for transfers between devices  79.6 us (24%)
  Pallas kernels  64.8 us (20%)
  blocking collectives  35.2 us (11%)
    ppermute x101, starting transfers between devices, flip(): lax.ppermute(x, axis, [(i, i ^ step) for i in range(lax.axis_size(axis))])  122 us
    ppermute x101, waiting for transfers between devices, flip(): lax.ppermute(x, axis, [(i, i ^ step) for i in range(lax.axis_size(axis))])  74.2 us
    pallas_call x40, Pallas kernels, call(): pl.pallas_call(wrapped, out_shape=[jax.ShapeDtypeStruct(shape, kind) for...  64.8 us
    all_to_all x3, blocking collectives, exchange(): return lax.all_to_all(block, ALL_AXES, 0, 0)  35.2 us
    ppermute x3, starting transfers between devices, halo(): below = lax.ppermute(top, HA, [(i + 1, i) for i in range(count - 1)])  14.6 us
    ppermute x3, starting transfers between devices, halo(): above = lax.ppermute(bottom, HA, [(i, i + 1) for i in range(count - 1)])  9 us
  transfers between devices with their start and end apart: 132, of which 60 were waited for; matrix products, arithmetic and copies ran while one was open for 0% of the time, Pallas kernels for 11%

profile of v1, /device:TPU:0, one launch (start us, length us, event | category | flops | bytes accessed | tf_op | source)
XLA Modules:
  0.0 330.1 jit_solution(17559565545844079523)
XLA Ops:
  1.4 2.9 shard_map.271
  4.2 3.0 collective-permute-start.1
  9.2 2.9 collective-permute-done.2.refs_8_
  16.9 3.7 %collective-permute-start.8 = (f32[8,128]{1,0:T(8,128)S(1)}, f32[8,128]{1,0:T(8,128)S(1)}, u32[]{:S(2)}, u32[]{:S(2)}) collective-permute-start(f32[8,128]{1,0:T(8,128)S(1)} %fusion.10), channel_id=1, source_target_pairs={{0,24},{8,16},{16,8},{24,0},{1,25},{9,17},{17,9},{25,1},{2,26},{10... | collective-permute-start | bytes 12296 | tf_op jit(solution)/shard_map/ppermute | solution.py:1234
  21.4 2.7 shard_map.272
  25.1 2.5 shard_map.273
  28.2 2.4 collective-permute-start.12
  35.1 2.5 collective-permute-done.10
  38.8 2.7 collective-permute-start.18
  46.2 2.3 shard_map.274
  48.4 12.1 %all_to_all.15.refs_2_ = f32[32,8,128]{2,1,0:T(8,128)S(1)} all-to-all(f32[32,8,128]{2,1,0:T(8,128)S(1)} %get-tuple-element.238), channel_id=1, replica_groups=mesh['clip'=4,'ha'=4,'wa'=2] {'clip','ha','wa'}, dimensions={0} | all-to-all | bytes 262144 | tf_op jit(solution)/shard_map/all_to_all | solution.py:1206
  60.6 2.8 shard_map.275
  69.9 2.7 collective-permute-done.20
  75.7 2.6 collective-permute-start.26
  79.9 2.8 shard_map.276
  85.2 2.6 collective-permute-done.31.refs_5_
  90.3 3.0 collective-permute-done.30
  94.5 2.4 collective-permute-start.38
  101.8 2.3 shard_map.277
  104.1 10.5 %all_to_all.16.refs_2_ = f32[32,8,128]{2,1,0:T(8,128)S(1)} all-to-all(f32[32,8,128]{2,1,0:T(8,128)S(1)} %get-tuple-element.259), channel_id=1, replica_groups=mesh['clip'=4,'ha'=4,'wa'=2] {'clip','ha','wa'}, dimensions={0} | all-to-all | bytes 262144 | tf_op jit(solution)/shard_map/all_to_all | solution.py:1206
  115.8 12.6 %all_to_all.17.refs_2_ = f32[32,16,128]{2,1,0:T(8,128)S(1)} all-to-all(f32[32,16,128]{2,1,0:T(8,128)S(1)} %get-tuple-element.261), channel_id=1, replica_groups=mesh['clip'=4,'ha'=4,'wa'=2] {'clip','ha','wa'}, dimensions={0} | all-to-all | bytes 524288 | tf_op jit(solution)/shard_map/all_to_all | solution.py:1206
  128.4 3.0 shard_map.279
  140.5 2.3 collective-permute-start.44
  152.5 3.4 %collective-permute-start.55 = (bf16[64,768]{1,0:T(8,128)(2,1)S(1)}, bf16[64,768]{1,0:T(8,128)(2,1)S(1)}, u32[]{:S(2)}, u32[]{:S(2)}) collective-permute-start(bf16[64,768]{1,0:T(8,128)(2,1)S(1)} %get-tuple-element.283), channel_id=1, source_target_pairs={{0,2},{2,4},{4,6},{1,3},{3,5},{5,7},{8,10},{10,12},{12,14},{9,11},... | collective-permute-start | bytes 294920 | tf_op jit(solution)/shard_map/ppermute | solution.py:1215
  157.6 2.4 collective-permute-start.54
  164.5 2.6 collective-permute-start.64
  168.0 2.6 shard_map.282
  185.0 2.5 shard_map.285
  195.6 2.4 collective-permute-start.76
  204.1 2.4 shard_map.287
  209.9 2.2 collective-permute-start.78
  213.1 3.1 collective-permute-start.88
  216.2 11.7 %collective-permute-start.89 = (bf16[64,512]{1,0:T(8,128)(2,1)S(1)}, bf16[64,512]{1,0:T(8,128)(2,1)S(1)}, u32[]{:S(2)}, u32[]{:S(2)}) collective-permute-start(bf16[64,512]{1,0:T(8,128)(2,1)S(1)} %get-tuple-element.325), channel_id=1, source_target_pairs={{2,0},{4,2},{6,4},{3,1},{5,3},{7,5},{10,8},{12,10},{14,12},{11,9},... | collective-permute-start | bytes 196616 | tf_op jit(solution)/shard_map/ppermute | solution.py:1216
  228.1 3.0 collective-permute-start.87
  235.9 2.6 shard_map.290
  238.6 2.9 shard_map.292
  246.6 2.5 collective-permute-start.102
  254.2 2.6 collective-permute-start.99
  261.9 2.2 collective-permute-start.111
  264.7 2.2 collective-permute-start.110
  279.4 2.1 shard_map.297
  282.5 8.8 %collective-permute-done.119.refs_3_ = bf16[2,608,256]{2,1,0:T(8,128)(2,1)S(1)} collective-permute-done((bf16[2,608,256]{2,1,0:T(8,128)(2,1)S(1)}, bf16[2,608,256]{2,1,0:T(8,128)(2,1)S(1)}, u32[]{:S(2)}, u32[]{:S(2)}) %collective-permute-start.119) | collective-permute-done | bytes 622624 | tf_op jit(solution)/shard_map/ppermute | solution.py:1234
  304.9 2.7 collective-permute-start.127
  309.2 2.6 collective-permute-start.118
  313.0 3.1 collective-permute-done.127.refs_4_
  317.9 2.4 collective-permute-start.130
  323.3 2.2 collective-permute-done.124.refs_7_
  325.6 2.3 collective-permute-done.130.refs_10_
  (318 shorter events, 159.4 us)
Async XLA Ops:
  9.2 7.7 %collective-permute-start.4 = (f32[72,128]{1,0:T(8,128)S(1)}, f32[72,128]{1,0:T(8,128)S(1)}, u32[]{:S(2)}, u32[]{:S(2)}) collective-permute-start(f32[72,128]{1,0:T(8,128)S(1)} %collective-permute-done.1.refs_7_), channel_id=1, source_target_pairs={{0,1},{1,0},{2,3},{3,2},{4,5},{5,4},{6,7},{7,6},{8,9},{9,8},{10,11... | collective-permute-start | bytes 110600 | tf_op jit(solution)/shard_map/ppermute | solution.py:1210
  15.7 9.4 %collective-permute-start.9 = (bf16[256,128]{1,0:T(8,128)(2,1)S(1)}, bf16[256,128]{1,0:T(8,128)(2,1)S(1)}, u32[]{:S(2)}, u32[]{:S(2)}) collective-permute-start(bf16[256,128]{1,0:T(8,128)(2,1)S(1)} %get-tuple-element.227), channel_id=1, source_target_pairs={{0,1},{1,0},{2,3},{3,2},{4,5},{5,4},{6,7},{7,6},{8,9},{9,8},{10,11... | collective-permute-start | bytes 196616 | tf_op jit(solution)/shard_map/ppermute | solution.py:1210
  16.9 7.1 %collective-permute-start.8 = (f32[8,128]{1,0:T(8,128)S(1)}, f32[8,128]{1,0:T(8,128)S(1)}, u32[]{:S(2)}, u32[]{:S(2)}) collective-permute-start(f32[8,128]{1,0:T(8,128)S(1)} %fusion.10), channel_id=1, source_target_pairs={{0,24},{8,16},{16,8},{24,0},{1,25},{9,17},{17,9},{25,1},{2,26},{10... | collective-permute-start | bytes 12296 | tf_op jit(solution)/shard_map/ppermute | solution.py:1234
  32.1 6.7 %collective-permute-start.14 = (f32[152,128]{1,0:T(8,128)S(1)}, f32[152,128]{1,0:T(8,128)S(1)}, u32[]{:S(2)}, u32[]{:S(2)}) collective-permute-start(f32[152,128]{1,0:T(8,128)S(1)} %collective-permute-done.11.refs_5_), channel_id=1, source_target_pairs={{0,1},{1,0},{2,3},{3,2},{4,5},{5,4},{6,7},{7,6},{8,9},{9,8},{10,11... | collective-permute-start | bytes 233480 | tf_op jit(solution)/shard_map/ppermute | solution.py:1210
  87.8 6.7 %collective-permute-start.34 = (f32[152,128]{1,0:T(8,128)S(1)}, f32[152,128]{1,0:T(8,128)S(1)}, u32[]{:S(2)}, u32[]{:S(2)}) collective-permute-start(f32[152,128]{1,0:T(8,128)S(1)} %collective-permute-done.31.refs_5_), channel_id=1, source_target_pairs={{0,1},{1,0},{2,3},{3,2},{4,5},{5,4},{6,7},{7,6},{8,9},{9,8},{10,11... | collective-permute-start | bytes 233480 | tf_op jit(solution)/shard_map/ppermute | solution.py:1210
  148.4 9.2 %collective-permute-start.51 = (bf16[4,768,256]{2,1,0:T(8,128)(2,1)S(1)}, bf16[4,768,256]{2,1,0:T(8,128)(2,1)S(1)}, u32[]{:S(2)}, u32[]{:S(2)}) collective-permute-start(bf16[4,768,256]{2,1,0:T(8,128)(2,1)S(1)} %get-tuple-element.280), channel_id=1, source_target_pairs={{0,1},{1,0},{2,3},{3,2},{4,5},{5,4},{6,7},{7,6},{8,9},{9,8},{10,11... | collective-permute-start | bytes 4718600 | tf_op jit(solution)/shard_map/ppermute | solution.py:1234
  149.0 6.9 %collective-permute-start.50 = (f32[8,128]{1,0:T(8,128)S(1)}, f32[8,128]{1,0:T(8,128)S(1)}, u32[]{:S(2)}, u32[]{:S(2)}) collective-permute-start(f32[8,128]{1,0:T(8,128)S(1)} %add.298), channel_id=1, source_target_pairs={{0,6},{2,4},{4,2},{6,0},{1,7},{3,5},{5,3},{7,1},{8,14},{10,12},{12... | collective-permute-start | bytes 12296 | tf_op jit(solution)/shard_map/ppermute | solution.py:1234
  150.7 6.7 %collective-permute-start.49 = (f32[8,128]{1,0:T(8,128)S(1)}, f32[8,128]{1,0:T(8,128)S(1)}, u32[]{:S(2)}, u32[]{:S(2)}) collective-permute-start(f32[8,128]{1,0:T(8,128)S(1)} %add.298), channel_id=1, source_target_pairs={{0,4},{2,6},{4,0},{6,2},{1,5},{3,7},{5,1},{7,3},{8,12},{10,14},{12... | collective-permute-start | bytes 12296 | tf_op jit(solution)/shard_map/ppermute | solution.py:1234
  152.5 8.6 %collective-permute-start.55 = (bf16[64,768]{1,0:T(8,128)(2,1)S(1)}, bf16[64,768]{1,0:T(8,128)(2,1)S(1)}, u32[]{:S(2)}, u32[]{:S(2)}) collective-permute-start(bf16[64,768]{1,0:T(8,128)(2,1)S(1)} %get-tuple-element.283), channel_id=1, source_target_pairs={{0,2},{2,4},{4,6},{1,3},{3,5},{5,7},{8,10},{10,12},{12,14},{9,11},... | collective-permute-start | bytes 294920 | tf_op jit(solution)/shard_map/ppermute | solution.py:1215
  155.8 7.1 %collective-permute-start.56 = (bf16[64,768]{1,0:T(8,128)(2,1)S(1)}, bf16[64,768]{1,0:T(8,128)(2,1)S(1)}, u32[]{:S(2)}, u32[]{:S(2)}) collective-permute-start(bf16[64,768]{1,0:T(8,128)(2,1)S(1)} %get-tuple-element.284), channel_id=1, source_target_pairs={{2,0},{4,2},{6,4},{3,1},{5,3},{7,5},{10,8},{12,10},{14,12},{11,9},... | collective-permute-start | bytes 294920 | tf_op jit(solution)/shard_map/ppermute | solution.py:1216
  157.5 10.6 %collective-permute-start.57 = (bf16[256,768]{1,0:T(8,128)(2,1)S(1)}, bf16[256,768]{1,0:T(8,128)(2,1)S(1)}, u32[]{:S(2)}, u32[]{:S(2)}) collective-permute-start(bf16[256,768]{1,0:T(8,128)(2,1)S(1)} %get-tuple-element.285), channel_id=1, source_target_pairs={{0,1},{1,0},{2,3},{3,2},{4,5},{5,4},{6,7},{7,6},{8,9},{9,8},{10,11... | collective-permute-start | bytes 1179656 | tf_op jit(solution)/shard_map/ppermute | solution.py:1210
  161.1 6.0 %collective-permute-start.52 = (f32[8,128]{1,0:T(8,128)S(1)}, f32[8,128]{1,0:T(8,128)S(1)}, u32[]{:S(2)}, u32[]{:S(2)}) collective-permute-start(f32[8,128]{1,0:T(8,128)S(1)} %add_add_fusion.16), channel_id=1, source_target_pairs={{0,8},{8,0},{16,24},{24,16},{1,9},{9,1},{17,25},{25,17},{2,10},{10... | collective-permute-start | bytes 12296 | tf_op jit(solution)/shard_map/ppermute | solution.py:1234
  164.5 13.5 %collective-permute-start.64 = (bf16[2,384,256]{2,1,0:T(8,128)(2,1)S(1)}, bf16[2,384,256]{2,1,0:T(8,128)(2,1)S(1)}, u32[]{:S(2)}, u32[]{:S(2)}) collective-permute-start(bf16[2,384,256]{2,1,0:T(8,128)(2,1)S(1)} %get-tuple-element.289), channel_id=1, source_target_pairs={{0,2},{2,0},{4,6},{6,4},{1,3},{3,1},{5,7},{7,5},{8,10},{10,8},{12,... | collective-permute-start | bytes 1179656 | tf_op jit(solution)/shard_map/ppermute | solution.py:1234
  167.1 10.9 %collective-permute-start.65 = (bf16[2,384,256]{2,1,0:T(8,128)(2,1)S(1)}, bf16[2,384,256]{2,1,0:T(8,128)(2,1)S(1)}, u32[]{:S(2)}, u32[]{:S(2)}) collective-permute-start(bf16[2,384,256]{2,1,0:T(8,128)(2,1)S(1)} %get-tuple-element.290), channel_id=1, source_target_pairs={{0,4},{2,6},{4,0},{6,2},{1,5},{3,7},{5,1},{7,3},{8,12},{10,14},{12... | collective-permute-start | bytes 1179656 | tf_op jit(solution)/shard_map/ppermute | solution.py:1234
  189.4 6.2 %collective-permute-start.73 = (bf16[4,768,256]{2,1,0:T(8,128)(2,1)S(1)}, bf16[4,768,256]{2,1,0:T(8,128)(2,1)S(1)}, u32[]{:S(2)}, u32[]{:S(2)}) collective-permute-start(bf16[4,768,256]{2,1,0:T(8,128)(2,1)S(1)} %get-tuple-element.301), channel_id=1, source_target_pairs={{0,1},{1,0},{2,3},{3,2},{4,5},{5,4},{6,7},{7,6},{8,9},{9,8},{10,11... | collective-permute-start | bytes 4718600 | tf_op jit(solution)/shard_map/ppermute | solution.py:1234
  194.2 15.6 %collective-permute-start.81 = (bf16[384,256]{1,0:T(8,128)(2,1)S(1)}, bf16[384,256]{1,0:T(8,128)(2,1)S(1)}, u32[]{:S(2)}, u32[]{:S(2)}) collective-permute-start(bf16[384,256]{1,0:T(8,128)(2,1)S(1)} %get-tuple-element.314), channel_id=1, source_target_pairs={{0,4},{2,6},{4,0},{6,2},{1,5},{3,7},{5,1},{7,3},{8,12},{10,14},{12... | collective-permute-start | bytes 589832 | tf_op jit(solution)/shard_map/ppermute | solution.py:1234
  194.6 15.3 %collective-permute-start.82 = (bf16[384,256]{1,0:T(8,128)(2,1)S(1)}, bf16[384,256]{1,0:T(8,128)(2,1)S(1)}, u32[]{:S(2)}, u32[]{:S(2)}) collective-permute-start(bf16[384,256]{1,0:T(8,128)(2,1)S(1)} %get-tuple-element.315), channel_id=1, source_target_pairs={{0,2},{2,0},{4,6},{6,4},{1,3},{3,1},{5,7},{7,5},{8,10},{10,8},{12,... | collective-permute-start | bytes 589832 | tf_op jit(solution)/shard_map/ppermute | solution.py:1234
  201.4 26.7 %collective-permute-start.83 = (bf16[2,384,256]{2,1,0:T(8,128)(2,1)S(1)}, bf16[2,384,256]{2,1,0:T(8,128)(2,1)S(1)}, u32[]{:S(2)}, u32[]{:S(2)}) collective-permute-start(bf16[2,384,256]{2,1,0:T(8,128)(2,1)S(1)} %get-tuple-element.319), channel_id=1, source_target_pairs={{0,2},{2,0},{4,6},{6,4},{1,3},{3,1},{5,7},{7,5},{8,10},{10,8},{12,... | collective-permute-start | bytes 1179656 | tf_op jit(solution)/shard_map/ppermute | solution.py:1234
  202.9 25.2 %collective-permute-start.84 = (bf16[2,384,256]{2,1,0:T(8,128)(2,1)S(1)}, bf16[2,384,256]{2,1,0:T(8,128)(2,1)S(1)}, u32[]{:S(2)}, u32[]{:S(2)}) collective-permute-start(bf16[2,384,256]{2,1,0:T(8,128)(2,1)S(1)} %get-tuple-element.320), channel_id=1, source_target_pairs={{0,4},{2,6},{4,0},{6,2},{1,5},{3,7},{5,1},{7,3},{8,12},{10,14},{12... | collective-permute-start | bytes 1179656 | tf_op jit(solution)/shard_map/ppermute | solution.py:1234
  209.8 6.4 %collective-permute-start.79 = (f32[8,128]{1,0:T(8,128)S(1)}, f32[8,128]{1,0:T(8,128)S(1)}, u32[]{:S(2)}, u32[]{:S(2)}) collective-permute-start(f32[8,128]{1,0:T(8,128)S(1)} %add.319), channel_id=1, source_target_pairs={{0,16},{8,24},{16,0},{24,8},{1,17},{9,25},{17,1},{25,9},{2,18},{10... | collective-permute-start | bytes 12296 | tf_op jit(solution)/shard_map/ppermute | solution.py:1234
  209.9 18.0 %collective-permute-start.78 = (f32[8,128]{1,0:T(8,128)S(1)}, f32[8,128]{1,0:T(8,128)S(1)}, u32[]{:S(2)}, u32[]{:S(2)}) collective-permute-start(f32[8,128]{1,0:T(8,128)S(1)} %add.319), channel_id=1, source_target_pairs={{0,8},{8,0},{16,24},{24,16},{1,9},{9,1},{17,25},{25,17},{2,10},{10... | collective-permute-start | bytes 12296 | tf_op jit(solution)/shard_map/ppermute | solution.py:1234
  213.1 19.2 %collective-permute-start.88 = (bf16[64,512]{1,0:T(8,128)(2,1)S(1)}, bf16[64,512]{1,0:T(8,128)(2,1)S(1)}, u32[]{:S(2)}, u32[]{:S(2)}) collective-permute-start(bf16[64,512]{1,0:T(8,128)(2,1)S(1)} %get-tuple-element.324), channel_id=1, source_target_pairs={{0,2},{2,4},{4,6},{1,3},{3,5},{5,7},{8,10},{10,12},{12,14},{9,11},... | collective-permute-start | bytes 196616 | tf_op jit(solution)/shard_map/ppermute | solution.py:1215
  216.2 16.5 %collective-permute-start.89 = (bf16[64,512]{1,0:T(8,128)(2,1)S(1)}, bf16[64,512]{1,0:T(8,128)(2,1)S(1)}, u32[]{:S(2)}, u32[]{:S(2)}) collective-permute-start(bf16[64,512]{1,0:T(8,128)(2,1)S(1)} %get-tuple-element.325), channel_id=1, source_target_pairs={{2,0},{4,2},{6,4},{3,1},{5,3},{7,5},{10,8},{12,10},{14,12},{11,9},... | collective-permute-start | bytes 196616 | tf_op jit(solution)/shard_map/ppermute | solution.py:1216
  228.0 7.9 %collective-permute-start.90 = (bf16[256,512]{1,0:T(8,128)(2,1)S(1)}, bf16[256,512]{1,0:T(8,128)(2,1)S(1)}, u32[]{:S(2)}, u32[]{:S(2)}) collective-permute-start(bf16[256,512]{1,0:T(8,128)(2,1)S(1)} %get-tuple-element.326), channel_id=1, source_target_pairs={{0,1},{1,0},{2,3},{3,2},{4,5},{5,4},{6,7},{7,6},{8,9},{9,8},{10,11... | collective-permute-start | bytes 786440 | tf_op jit(solution)/shard_map/ppermute | solution.py:1210
  241.5 10.9 %collective-permute-start.98 = (bf16[4,1216,256]{2,1,0:T(8,128)(2,1)S(1)}, bf16[4,1216,256]{2,1,0:T(8,128)(2,1)S(1)}, u32[]{:S(2)}, u32[]{:S(2)}) collective-permute-start(bf16[4,1216,256]{2,1,0:T(8,128)(2,1)S(1)} %get-tuple-element.346), channel_id=1, source_target_pairs={{0,1},{1,0},{2,3},{3,2},{4,5},{5,4},{6,7},{7,6},{8,9},{9,8},{10,11... | collective-permute-start | bytes 7471112 | tf_op jit(solution)/shard_map/ppermute | solution.py:1234
  244.2 6.3 %collective-permute-start.94 = (f32[8,128]{1,0:T(8,128)S(1)}, f32[8,128]{1,0:T(8,128)S(1)}, u32[]{:S(2)}, u32[]{:S(2)}) collective-permute-start(f32[8,128]{1,0:T(8,128)S(1)} %add.326), channel_id=1, source_target_pairs={{0,2},{2,0},{4,6},{6,4},{1,3},{3,1},{5,7},{7,5},{8,10},{10,8},{12,... | collective-permute-start | bytes 12296 | tf_op jit(solution)/shard_map/ppermute | solution.py:1234
  246.3 6.1 %collective-permute-start.97 = (bf16[2,384,128]{2,1,0:T(8,128)(2,1)S(1)}, bf16[2,384,128]{2,1,0:T(8,128)(2,1)S(1)}, u32[]{:S(2)}, u32[]{:S(2)}) collective-permute-start(bf16[2,384,128]{2,1,0:T(8,128)(2,1)S(1)} %get-tuple-element.332), channel_id=1, source_target_pairs={{0,8},{8,0},{16,24},{24,16},{1,9},{9,1},{17,25},{25,17},{2,10},{10... | collective-permute-start | bytes 589832 | tf_op jit(solution)/shard_map/ppermute | solution.py:1234
  246.6 11.3 %collective-permute-start.102 = (bf16[64,256]{1,0:T(8,128)(2,1)S(1)}, bf16[64,256]{1,0:T(8,128)(2,1)S(1)}, u32[]{:S(2)}, u32[]{:S(2)}) collective-permute-start(bf16[64,256]{1,0:T(8,128)(2,1)S(1)} %get-tuple-element.349), channel_id=1, source_target_pairs={{0,2},{2,4},{4,6},{1,3},{3,5},{5,7},{8,10},{10,12},{12,14},{9,11},... | collective-permute-start | bytes 98312 | tf_op jit(solution)/shard_map/ppermute | solution.py:1215
  249.1 8.8 %collective-permute-start.103 = (bf16[64,256]{1,0:T(8,128)(2,1)S(1)}, bf16[64,256]{1,0:T(8,128)(2,1)S(1)}, u32[]{:S(2)}, u32[]{:S(2)}) collective-permute-start(bf16[64,256]{1,0:T(8,128)(2,1)S(1)} %get-tuple-element.350), channel_id=1, source_target_pairs={{2,0},{4,2},{6,4},{3,1},{5,3},{7,5},{10,8},{12,10},{14,12},{11,9},... | collective-permute-start | bytes 98312 | tf_op jit(solution)/shard_map/ppermute | solution.py:1216
  252.4 6.1 %collective-permute-start.101 = (f32[8,128]{1,0:T(8,128)S(1)}, f32[8,128]{1,0:T(8,128)S(1)}, u32[]{:S(2)}, u32[]{:S(2)}) collective-permute-start(f32[8,128]{1,0:T(8,128)S(1)} %add_add_fusion.10), channel_id=1, source_target_pairs={{0,24},{8,16},{16,8},{24,0},{1,25},{9,17},{17,9},{25,1},{2,26},{10... | collective-permute-start | bytes 12296 | tf_op jit(solution)/shard_map/ppermute | solution.py:1234
  261.9 9.5 %collective-permute-start.111 = (bf16[384,256]{1,0:T(8,128)(2,1)S(1)}, bf16[384,256]{1,0:T(8,128)(2,1)S(1)}, u32[]{:S(2)}, u32[]{:S(2)}) collective-permute-start(bf16[384,256]{1,0:T(8,128)(2,1)S(1)} %get-tuple-element.363), channel_id=1, source_target_pairs={{0,4},{2,6},{4,0},{6,2},{1,5},{3,7},{5,1},{7,3},{8,12},{10,14},{12... | collective-permute-start | bytes 589832 | tf_op jit(solution)/shard_map/ppermute | solution.py:1234
  264.2 7.2 %collective-permute-start.112 = (bf16[384,256]{1,0:T(8,128)(2,1)S(1)}, bf16[384,256]{1,0:T(8,128)(2,1)S(1)}, u32[]{:S(2)}, u32[]{:S(2)}) collective-permute-start(bf16[384,256]{1,0:T(8,128)(2,1)S(1)} %get-tuple-element.364), channel_id=1, source_target_pairs={{0,2},{2,0},{4,6},{6,4},{1,3},{3,1},{5,7},{7,5},{8,10},{10,8},{12,... | collective-permute-start | bytes 589832 | tf_op jit(solution)/shard_map/ppermute | solution.py:1234
  270.1 50.2 %collective-permute-start.116 = (bf16[384,128]{1,0:T(8,128)(2,1)S(1)}, bf16[384,128]{1,0:T(8,128)(2,1)S(1)}, u32[]{:S(2)}, u32[]{:S(2)}) collective-permute-start(bf16[384,128]{1,0:T(8,128)(2,1)S(1)} %get-tuple-element.381), channel_id=1, source_target_pairs={{0,16},{8,24},{16,0},{24,8},{1,17},{9,25},{17,1},{25,9},{2,18},{10... | collective-permute-start | bytes 294920 | tf_op jit(solution)/shard_map/ppermute | solution.py:1234
  278.1 13.2 %collective-permute-start.119 = (bf16[2,608,256]{2,1,0:T(8,128)(2,1)S(1)}, bf16[2,608,256]{2,1,0:T(8,128)(2,1)S(1)}, u32[]{:S(2)}, u32[]{:S(2)}) collective-permute-start(bf16[2,608,256]{2,1,0:T(8,128)(2,1)S(1)} %get-tuple-element.396), channel_id=1, source_target_pairs={{0,2},{2,0},{4,6},{6,4},{1,3},{3,1},{5,7},{7,5},{8,10},{10,8},{12,... | collective-permute-start | bytes 1867784 | tf_op jit(solution)/shard_map/ppermute | solution.py:1234
  278.6 12.8 %collective-permute-start.120 = (bf16[2,608,256]{2,1,0:T(8,128)(2,1)S(1)}, bf16[2,608,256]{2,1,0:T(8,128)(2,1)S(1)}, u32[]{:S(2)}, u32[]{:S(2)}) collective-permute-start(bf16[2,608,256]{2,1,0:T(8,128)(2,1)S(1)} %get-tuple-element.398), channel_id=1, source_target_pairs={{0,4},{2,6},{4,0},{6,2},{1,5},{3,7},{5,1},{7,3},{8,12},{10,14},{12... | collective-permute-start | bytes 1867784 | tf_op jit(solution)/shard_map/ppermute | solution.py:1234
  281.6 20.9 %collective-permute-start.125 = (bf16[4,640,256]{2,1,0:T(8,128)(2,1)S(1)}, bf16[4,640,256]{2,1,0:T(8,128)(2,1)S(1)}, u32[]{:S(2)}, u32[]{:S(2)}) collective-permute-start(bf16[4,640,256]{2,1,0:T(8,128)(2,1)S(1)} %get-tuple-element.375), channel_id=1, source_target_pairs={{0,1},{1,0},{2,3},{3,2},{4,5},{5,4},{6,7},{7,6},{8,9},{9,8},{10,11... | collective-permute-start | bytes 3932168 | tf_op jit(solution)/shard_map/ppermute | solution.py:1234
  292.3 7.0 %collective-permute-start.121 = (bf16[608,256]{1,0:T(8,128)(2,1)S(1)}, bf16[608,256]{1,0:T(8,128)(2,1)S(1)}, u32[]{:S(2)}, u32[]{:S(2)}) collective-permute-start(bf16[608,256]{1,0:T(8,128)(2,1)S(1)} %get-tuple-element.400), channel_id=1, source_target_pairs={{0,4},{2,6},{4,0},{6,2},{1,5},{3,7},{5,1},{7,3},{8,12},{10,14},{12... | collective-permute-start | bytes 933896 | tf_op jit(solution)/shard_map/ppermute | solution.py:1234
  292.9 6.9 %collective-permute-start.122 = (bf16[608,256]{1,0:T(8,128)(2,1)S(1)}, bf16[608,256]{1,0:T(8,128)(2,1)S(1)}, u32[]{:S(2)}, u32[]{:S(2)}) collective-permute-start(bf16[608,256]{1,0:T(8,128)(2,1)S(1)} %get-tuple-element.402), channel_id=1, source_target_pairs={{0,2},{2,0},{4,6},{6,4},{1,3},{3,1},{5,7},{7,5},{8,10},{10,8},{12,... | collective-permute-start | bytes 933896 | tf_op jit(solution)/shard_map/ppermute | solution.py:1234
  295.2 12.4 %collective-permute-start.117 = (bf16[2,384,128]{2,1,0:T(8,128)(2,1)S(1)}, bf16[2,384,128]{2,1,0:T(8,128)(2,1)S(1)}, u32[]{:S(2)}, u32[]{:S(2)}) collective-permute-start(bf16[2,384,128]{2,1,0:T(8,128)(2,1)S(1)} %get-tuple-element.388), channel_id=1, source_target_pairs={{0,8},{8,0},{16,24},{24,16},{1,9},{9,1},{17,25},{25,17},{2,10},{10... | collective-permute-start | bytes 589832 | tf_op jit(solution)/shard_map/ppermute | solution.py:1234
  300.7 8.5 %collective-permute-start.123 = (bf16[2,704,128]{2,1,0:T(8,128)(2,1)S(1)}, bf16[2,704,128]{2,1,0:T(8,128)(2,1)S(1)}, u32[]{:S(2)}, u32[]{:S(2)}) collective-permute-start(bf16[2,704,128]{2,1,0:T(8,128)(2,1)S(1)} %get-tuple-element.404), channel_id=1, source_target_pairs={{0,8},{8,0},{16,24},{24,16},{1,9},{9,1},{17,25},{25,17},{2,10},{10... | collective-permute-start | bytes 1081352 | tf_op jit(solution)/shard_map/ppermute | solution.py:1234
  303.4 9.1 %collective-permute-start.126 = (bf16[640,256]{1,0:T(8,128)(2,1)S(1)}, bf16[640,256]{1,0:T(8,128)(2,1)S(1)}, u32[]{:S(2)}, u32[]{:S(2)}) collective-permute-start(bf16[640,256]{1,0:T(8,128)(2,1)S(1)} %get-tuple-element.409), channel_id=1, source_target_pairs={{0,2},{2,0},{4,6},{6,4},{1,3},{3,1},{5,7},{7,5},{8,10},{10,8},{12,... | collective-permute-start | bytes 983048 | tf_op jit(solution)/shard_map/ppermute | solution.py:1234
  304.9 11.2 %collective-permute-start.127 = (bf16[640,256]{1,0:T(8,128)(2,1)S(1)}, bf16[640,256]{1,0:T(8,128)(2,1)S(1)}, u32[]{:S(2)}, u32[]{:S(2)}) collective-permute-start(bf16[640,256]{1,0:T(8,128)(2,1)S(1)} %get-tuple-element.410), channel_id=1, source_target_pairs={{0,4},{2,6},{4,0},{6,2},{1,5},{3,7},{5,1},{7,3},{8,12},{10,14},{12... | collective-permute-start | bytes 983048 | tf_op jit(solution)/shard_map/ppermute | solution.py:1234
  307.6 8.6 %collective-permute-start.128 = (bf16[640,256]{1,0:T(8,128)(2,1)S(1)}, bf16[640,256]{1,0:T(8,128)(2,1)S(1)}, u32[]{:S(2)}, u32[]{:S(2)}) collective-permute-start(bf16[640,256]{1,0:T(8,128)(2,1)S(1)} %get-tuple-element.411), channel_id=1, source_target_pairs={{0,6},{2,4},{4,2},{6,0},{1,7},{3,5},{5,3},{7,1},{8,14},{10,12},{12... | collective-permute-start | bytes 983048 | tf_op jit(solution)/shard_map/ppermute | solution.py:1234
  309.2 14.1 %collective-permute-start.118 = (bf16[384,128]{1,0:T(8,128)(2,1)S(1)}, bf16[384,128]{1,0:T(8,128)(2,1)S(1)}, u32[]{:S(2)}, u32[]{:S(2)}) collective-permute-start(bf16[384,128]{1,0:T(8,128)(2,1)S(1)} %get-tuple-element.390), channel_id=1, source_target_pairs={{0,16},{8,24},{16,0},{24,8},{1,17},{9,25},{17,1},{25,9},{2,18},{10... | collective-permute-start | bytes 294920 | tf_op jit(solution)/shard_map/ppermute | solution.py:1234
  312.5 13.1 %collective-permute-start.124 = (bf16[704,128]{1,0:T(8,128)(2,1)S(1)}, bf16[704,128]{1,0:T(8,128)(2,1)S(1)}, u32[]{:S(2)}, u32[]{:S(2)}) collective-permute-start(bf16[704,128]{1,0:T(8,128)(2,1)S(1)} %get-tuple-element.406), channel_id=1, source_target_pairs={{0,16},{8,24},{16,0},{24,8},{1,17},{9,25},{17,1},{25,9},{2,18},{10... | collective-permute-start | bytes 540680 | tf_op jit(solution)/shard_map/ppermute | solution.py:1234
  317.0 8.6 %collective-permute-start.129 = (bf16[416,128]{1,0:T(8,128)(2,1)S(1)}, bf16[416,128]{1,0:T(8,128)(2,1)S(1)}, u32[]{:S(2)}, u32[]{:S(2)}) collective-permute-start(bf16[416,128]{1,0:T(8,128)(2,1)S(1)} %get-tuple-element.413), channel_id=1, source_target_pairs={{0,8},{8,0},{16,24},{24,16},{1,9},{9,1},{17,25},{25,17},{2,10},{10... | collective-permute-start | bytes 319496 | tf_op jit(solution)/shard_map/ppermute | solution.py:1234
  317.9 10.0 %collective-permute-start.130 = (bf16[416,128]{1,0:T(8,128)(2,1)S(1)}, bf16[416,128]{1,0:T(8,128)(2,1)S(1)}, u32[]{:S(2)}, u32[]{:S(2)}) collective-permute-start(bf16[416,128]{1,0:T(8,128)(2,1)S(1)} %get-tuple-element.414), channel_id=1, source_target_pairs={{0,16},{8,24},{16,0},{24,8},{1,17},{9,25},{17,1},{25,9},{2,18},{10... | collective-permute-start | bytes 319496 | tf_op jit(solution)/shard_map/ppermute | solution.py:1234
  320.3 7.6 %collective-permute-start.131 = (bf16[416,128]{1,0:T(8,128)(2,1)S(1)}, bf16[416,128]{1,0:T(8,128)(2,1)S(1)}, u32[]{:S(2)}, u32[]{:S(2)}) collective-permute-start(bf16[416,128]{1,0:T(8,128)(2,1)S(1)} %get-tuple-element.415), channel_id=1, source_target_pairs={{0,24},{8,16},{16,8},{24,0},{1,25},{9,17},{17,9},{25,1},{2,26},{10... | collective-permute-start | bytes 319496 | tf_op jit(solution)/shard_map/ppermute | solution.py:1234
  (96 other events, 483.3 us)

commit v2 on v1

--- a/solution.py
+++ b/solution.py
@@ -1090,9 +1090,10 @@
 
 
 class Out:
-    def __init__(self, shape, kind):
+    def __init__(self, shape, kind, spare=0):
         self.shape = shape
         self.kind = kind
+        self.spare = spare
 
 
 def scalar_values(place, valid, frame, tiles):
@@ -1124,7 +1125,7 @@
     shapes = [(x.shape, x.kind) if isinstance(x, Out) else x for x in outs]
     inward = weights[: len(weights) - len(ahead)]
     buffers = [pltpu.VMEM(arrays[i].shape[1:] if layered[i] else arrays[i].shape, arrays[i].dtype) for i in inward]
-    buffers += [pltpu.VMEM(*shapes[i]) for i in results]
+    buffers += [pltpu.VMEM((outs[i].shape[0] + outs[i].spare,) + outs[i].shape[1:], outs[i].kind) for i in results]
     own = first + count + len(outs)
     copies = len(buffers) + len(ahead)
 
@@ -1150,7 +1151,8 @@
             later[-1].start()
         for n, i in enumerate(results):
             n += len(inward)
-            leaving.append(pltpu.make_async_copy(inner[n], refs[first + count + i], rest[-1].at[n]))
+            whole = inner[n].at[pl.ds(0, outs[i].shape[0])] if outs[i].spare else inner[n]
+            leaving.append(pltpu.make_async_copy(whole, refs[first + count + i], rest[-1].at[n]))
             refs[first + count + i] = inner[n]
         given = ()
         if mode is not None:
@@ -1636,7 +1638,7 @@
         parts = [x for chain in chains for x in chain.state[0]]
         turned = (1, 5)
         weights = [dims[:-2] + dims[:-3:-1] if i in turned else dims for i, dims in enumerate(weights)]
-        weights = call(bind(kernel_finish, tiles, plan), places, parts, [Out(dims, F32) for dims in weights])
+        weights = call(bind(kernel_finish, tiles, plan), places, parts, [Out(dims, F32, 1) for dims in weights])
         weights = [jnp.swapaxes(x, -1, -2) if i in turned else x for i, x in enumerate(weights)]
     else:
         found = {}

time: 330 us -> 330 us (level)
  no operation moved by 1% of the time
where the time goes in v2:
time: 330 us
  starting transfers between devices  148 us (45%)
  waiting for transfers between devices  79.6 us (24%)
  Pallas kernels  64.8 us (20%)
  blocking collectives  35.2 us (11%)
    ppermute x101, starting transfers between devices, flip(): lax.ppermute(x, axis, [(i, i ^ step) for i in range(lax.axis_size(axis))])  122 us
    ppermute x101, waiting for transfers between devices, flip(): lax.ppermute(x, axis, [(i, i ^ step) for i in range(lax.axis_size(axis))])  74.2 us
    pallas_call x40, Pallas kernels, call(): pl.pallas_call(wrapped, out_shape=[jax.ShapeDtypeStruct(shape, kind) for...  64.8 us
    all_to_all x3, blocking collectives, exchange(): return lax.all_to_all(block, ALL_AXES, 0, 0)  35.2 us
    ppermute x3, starting transfers between devices, halo(): below = lax.ppermute(top, HA, [(i + 1, i) for i in range(count - 1)])  14.6 us
    ppermute x3, starting transfers between devices, halo(): above = lax.ppermute(bottom, HA, [(i, i + 1) for i in range(count - 1)])  9 us
  transfers between devices with their start and end apart: 132, of which 60 were waited for; matrix products, arithmetic and copies ran while one was open for 0% of the time, Pallas kernels for 11%

profile of v2, /device:TPU:0, one launch (start us, length us, event | category | flops | bytes accessed | tf_op | source)
XLA Modules:
  0.0 330.1 jit_solution(1812993474311048815)
XLA Ops:
  1.4 2.9 shard_map.271
  4.2 3.0 collective-permute-start.1
  9.2 2.9 collective-permute-done.2.refs_8_
  16.9 3.7 %collective-permute-start.8 = (f32[8,128]{1,0:T(8,128)S(1)}, f32[8,128]{1,0:T(8,128)S(1)}, u32[]{:S(2)}, u32[]{:S(2)}) collective-permute-start(f32[8,128]{1,0:T(8,128)S(1)} %fusion.10), channel_id=1, source_target_pairs={{0,24},{8,16},{16,8},{24,0},{1,25},{9,17},{17,9},{25,1},{2,26},{10... | collective-permute-start | bytes 12296 | tf_op jit(solution)/shard_map/ppermute | solution.py:1236
  21.4 2.7 shard_map.272
  25.1 2.5 shard_map.273
  28.2 2.4 collective-permute-start.12
  35.1 2.5 collective-permute-done.10
  38.8 2.7 collective-permute-start.18
  46.2 2.3 shard_map.274
  48.4 12.1 %all_to_all.15.refs_2_ = f32[32,8,128]{2,1,0:T(8,128)S(1)} all-to-all(f32[32,8,128]{2,1,0:T(8,128)S(1)} %get-tuple-element.238), channel_id=1, replica_groups=mesh['clip'=4,'ha'=4,'wa'=2] {'clip','ha','wa'}, dimensions={0} | all-to-all | bytes 262144 | tf_op jit(solution)/shard_map/all_to_all | solution.py:1208
  60.6 2.8 shard_map.275
  69.9 2.7 collective-permute-done.20
  75.7 2.6 collective-permute-start.26
  79.9 2.8 shard_map.276
  85.2 2.6 collective-permute-done.31.refs_5_
  90.3 3.0 collective-permute-done.30
  94.5 2.4 collective-permute-start.38
  101.8 2.3 shard_map.277
  104.1 10.5 %all_to_all.16.refs_2_ = f32[32,8,128]{2,1,0:T(8,128)S(1)} all-to-all(f32[32,8,128]{2,1,0:T(8,128)S(1)} %get-tuple-element.259), channel_id=1, replica_groups=mesh['clip'=4,'ha'=4,'wa'=2] {'clip','ha','wa'}, dimensions={0} | all-to-all | bytes 262144 | tf_op jit(solution)/shard_map/all_to_all | solution.py:1208
  115.8 12.6 %all_to_all.17.refs_2_ = f32[32,16,128]{2,1,0:T(8,128)S(1)} all-to-all(f32[32,16,128]{2,1,0:T(8,128)S(1)} %get-tuple-element.261), channel_id=1, replica_groups=mesh['clip'=4,'ha'=4,'wa'=2] {'clip','ha','wa'}, dimensions={0} | all-to-all | bytes 524288 | tf_op jit(solution)/shard_map/all_to_all | solution.py:1208
  128.4 3.0 shard_map.279
  140.5 2.3 collective-permute-start.44
  152.5 3.4 %collective-permute-start.55 = (bf16[64,768]{1,0:T(8,128)(2,1)S(1)}, bf16[64,768]{1,0:T(8,128)(2,1)S(1)}, u32[]{:S(2)}, u32[]{:S(2)}) collective-permute-start(bf16[64,768]{1,0:T(8,128)(2,1)S(1)} %get-tuple-element.283), channel_id=1, source_target_pairs={{0,2},{2,4},{4,6},{1,3},{3,5},{5,7},{8,10},{10,12},{12,14},{9,11},... | collective-permute-start | bytes 294920 | tf_op jit(solution)/shard_map/ppermute | solution.py:1217
  157.6 2.4 collective-permute-start.54
  164.5 2.6 collective-permute-start.64
  168.0 2.6 shard_map.282
  185.0 2.5 shard_map.285
  195.6 2.4 collective-permute-start.76
  204.1 2.4 shard_map.287
  209.9 2.2 collective-permute-start.78
  213.1 3.1 collective-permute-start.88
  216.2 11.7 %collective-permute-start.89 = (bf16[64,512]{1,0:T(8,128)(2,1)S(1)}, bf16[64,512]{1,0:T(8,128)(2,1)S(1)}, u32[]{:S(2)}, u32[]{:S(2)}) collective-permute-start(bf16[64,512]{1,0:T(8,128)(2,1)S(1)} %get-tuple-element.325), channel_id=1, source_target_pairs={{2,0},{4,2},{6,4},{3,1},{5,3},{7,5},{10,8},{12,10},{14,12},{11,9},... | collective-permute-start | bytes 196616 | tf_op jit(solution)/shard_map/ppermute | solution.py:1218
  228.1 3.0 collective-permute-start.87
  235.9 2.6 shard_map.290
  238.6 2.9 shard_map.292
  246.6 2.5 collective-permute-start.102
  254.2 2.6 collective-permute-start.99
  261.9 2.2 collective-permute-start.111
  264.7 2.2 collective-permute-start.110
  279.4 2.1 shard_map.297
  282.5 8.8 %collective-permute-done.119.refs_3_ = bf16[2,608,256]{2,1,0:T(8,128)(2,1)S(1)} collective-permute-done((bf16[2,608,256]{2,1,0:T(8,128)(2,1)S(1)}, bf16[2,608,256]{2,1,0:T(8,128)(2,1)S(1)}, u32[]{:S(2)}, u32[]{:S(2)}) %collective-permute-start.119) | collective-permute-done | bytes 622624 | tf_op jit(solution)/shard_map/ppermute | solution.py:1236
  304.9 2.7 collective-permute-start.127
  309.2 2.6 collective-permute-start.118
  313.0 3.1 collective-permute-done.127.refs_4_
  317.9 2.4 collective-permute-start.130
  323.3 2.2 collective-permute-done.124.refs_7_
  325.6 2.3 collective-permute-done.130.refs_10_
  (318 shorter events, 159.4 us)
Async XLA Ops:
  9.2 7.7 %collective-permute-start.4 = (f32[72,128]{1,0:T(8,128)S(1)}, f32[72,128]{1,0:T(8,128)S(1)}, u32[]{:S(2)}, u32[]{:S(2)}) collective-permute-start(f32[72,128]{1,0:T(8,128)S(1)} %collective-permute-done.1.refs_7_), channel_id=1, source_target_pairs={{0,1},{1,0},{2,3},{3,2},{4,5},{5,4},{6,7},{7,6},{8,9},{9,8},{10,11... | collective-permute-start | bytes 110600 | tf_op jit(solution)/shard_map/ppermute | solution.py:1212
  15.7 9.4 %collective-permute-start.9 = (bf16[256,128]{1,0:T(8,128)(2,1)S(1)}, bf16[256,128]{1,0:T(8,128)(2,1)S(1)}, u32[]{:S(2)}, u32[]{:S(2)}) collective-permute-start(bf16[256,128]{1,0:T(8,128)(2,1)S(1)} %get-tuple-element.227), channel_id=1, source_target_pairs={{0,1},{1,0},{2,3},{3,2},{4,5},{5,4},{6,7},{7,6},{8,9},{9,8},{10,11... | collective-permute-start | bytes 196616 | tf_op jit(solution)/shard_map/ppermute | solution.py:1212
  16.9 7.1 %collective-permute-start.8 = (f32[8,128]{1,0:T(8,128)S(1)}, f32[8,128]{1,0:T(8,128)S(1)}, u32[]{:S(2)}, u32[]{:S(2)}) collective-permute-start(f32[8,128]{1,0:T(8,128)S(1)} %fusion.10), channel_id=1, source_target_pairs={{0,24},{8,16},{16,8},{24,0},{1,25},{9,17},{17,9},{25,1},{2,26},{10... | collective-permute-start | bytes 12296 | tf_op jit(solution)/shard_map/ppermute | solution.py:1236
  32.1 6.7 %collective-permute-start.14 = (f32[152,128]{1,0:T(8,128)S(1)}, f32[152,128]{1,0:T(8,128)S(1)}, u32[]{:S(2)}, u32[]{:S(2)}) collective-permute-start(f32[152,128]{1,0:T(8,128)S(1)} %collective-permute-done.11.refs_5_), channel_id=1, source_target_pairs={{0,1},{1,0},{2,3},{3,2},{4,5},{5,4},{6,7},{7,6},{8,9},{9,8},{10,11... | collective-permute-start | bytes 233480 | tf_op jit(solution)/shard_map/ppermute | solution.py:1212
  87.8 6.7 %collective-permute-start.34 = (f32[152,128]{1,0:T(8,128)S(1)}, f32[152,128]{1,0:T(8,128)S(1)}, u32[]{:S(2)}, u32[]{:S(2)}) collective-permute-start(f32[152,128]{1,0:T(8,128)S(1)} %collective-permute-done.31.refs_5_), channel_id=1, source_target_pairs={{0,1},{1,0},{2,3},{3,2},{4,5},{5,4},{6,7},{7,6},{8,9},{9,8},{10,11... | collective-permute-start | bytes 233480 | tf_op jit(solution)/shard_map/ppermute | solution.py:1212
  148.4 9.2 %collective-permute-start.51 = (bf16[4,768,256]{2,1,0:T(8,128)(2,1)S(1)}, bf16[4,768,256]{2,1,0:T(8,128)(2,1)S(1)}, u32[]{:S(2)}, u32[]{:S(2)}) collective-permute-start(bf16[4,768,256]{2,1,0:T(8,128)(2,1)S(1)} %get-tuple-element.280), channel_id=1, source_target_pairs={{0,1},{1,0},{2,3},{3,2},{4,5},{5,4},{6,7},{7,6},{8,9},{9,8},{10,11... | collective-permute-start | bytes 4718600 | tf_op jit(solution)/shard_map/ppermute | solution.py:1236
  149.0 6.9 %collective-permute-start.50 = (f32[8,128]{1,0:T(8,128)S(1)}, f32[8,128]{1,0:T(8,128)S(1)}, u32[]{:S(2)}, u32[]{:S(2)}) collective-permute-start(f32[8,128]{1,0:T(8,128)S(1)} %add.298), channel_id=1, source_target_pairs={{0,6},{2,4},{4,2},{6,0},{1,7},{3,5},{5,3},{7,1},{8,14},{10,12},{12... | collective-permute-start | bytes 12296 | tf_op jit(solution)/shard_map/ppermute | solution.py:1236
  150.7 6.7 %collective-permute-start.49 = (f32[8,128]{1,0:T(8,128)S(1)}, f32[8,128]{1,0:T(8,128)S(1)}, u32[]{:S(2)}, u32[]{:S(2)}) collective-permute-start(f32[8,128]{1,0:T(8,128)S(1)} %add.298), channel_id=1, source_target_pairs={{0,4},{2,6},{4,0},{6,2},{1,5},{3,7},{5,1},{7,3},{8,12},{10,14},{12... | collective-permute-start | bytes 12296 | tf_op jit(solution)/shard_map/ppermute | solution.py:1236
  152.5 8.6 %collective-permute-start.55 = (bf16[64,768]{1,0:T(8,128)(2,1)S(1)}, bf16[64,768]{1,0:T(8,128)(2,1)S(1)}, u32[]{:S(2)}, u32[]{:S(2)}) collective-permute-start(bf16[64,768]{1,0:T(8,128)(2,1)S(1)} %get-tuple-element.283), channel_id=1, source_target_pairs={{0,2},{2,4},{4,6},{1,3},{3,5},{5,7},{8,10},{10,12},{12,14},{9,11},... | collective-permute-start | bytes 294920 | tf_op jit(solution)/shard_map/ppermute | solution.py:1217
  155.8 7.1 %collective-permute-start.56 = (bf16[64,768]{1,0:T(8,128)(2,1)S(1)}, bf16[64,768]{1,0:T(8,128)(2,1)S(1)}, u32[]{:S(2)}, u32[]{:S(2)}) collective-permute-start(bf16[64,768]{1,0:T(8,128)(2,1)S(1)} %get-tuple-element.284), channel_id=1, source_target_pairs={{2,0},{4,2},{6,4},{3,1},{5,3},{7,5},{10,8},{12,10},{14,12},{11,9},... | collective-permute-start | bytes 294920 | tf_op jit(solution)/shard_map/ppermute | solution.py:1218
  157.5 10.6 %collective-permute-start.57 = (bf16[256,768]{1,0:T(8,128)(2,1)S(1)}, bf16[256,768]{1,0:T(8,128)(2,1)S(1)}, u32[]{:S(2)}, u32[]{:S(2)}) collective-permute-start(bf16[256,768]{1,0:T(8,128)(2,1)S(1)} %get-tuple-element.285), channel_id=1, source_target_pairs={{0,1},{1,0},{2,3},{3,2},{4,5},{5,4},{6,7},{7,6},{8,9},{9,8},{10,11... | collective-permute-start | bytes 1179656 | tf_op jit(solution)/shard_map/ppermute | solution.py:1212
  161.1 6.0 %collective-permute-start.52 = (f32[8,128]{1,0:T(8,128)S(1)}, f32[8,128]{1,0:T(8,128)S(1)}, u32[]{:S(2)}, u32[]{:S(2)}) collective-permute-start(f32[8,128]{1,0:T(8,128)S(1)} %add_add_fusion.16), channel_id=1, source_target_pairs={{0,8},{8,0},{16,24},{24,16},{1,9},{9,1},{17,25},{25,17},{2,10},{10... | collective-permute-start | bytes 12296 | tf_op jit(solution)/shard_map/ppermute | solution.py:1236
  164.5 13.5 %collective-permute-start.64 = (bf16[2,384,256]{2,1,0:T(8,128)(2,1)S(1)}, bf16[2,384,256]{2,1,0:T(8,128)(2,1)S(1)}, u32[]{:S(2)}, u32[]{:S(2)}) collective-permute-start(bf16[2,384,256]{2,1,0:T(8,128)(2,1)S(1)} %get-tuple-element.289), channel_id=1, source_target_pairs={{0,2},{2,0},{4,6},{6,4},{1,3},{3,1},{5,7},{7,5},{8,10},{10,8},{12,... | collective-permute-start | bytes 1179656 | tf_op jit(solution)/shard_map/ppermute | solution.py:1236
  167.1 10.9 %collective-permute-start.65 = (bf16[2,384,256]{2,1,0:T(8,128)(2,1)S(1)}, bf16[2,384,256]{2,1,0:T(8,128)(2,1)S(1)}, u32[]{:S(2)}, u32[]{:S(2)}) collective-permute-start(bf16[2,384,256]{2,1,0:T(8,128)(2,1)S(1)} %get-tuple-element.290), channel_id=1, source_target_pairs={{0,4},{2,6},{4,0},{6,2},{1,5},{3,7},{5,1},{7,3},{8,12},{10,14},{12... | collective-permute-start | bytes 1179656 | tf_op jit(solution)/shard_map/ppermute | solution.py:1236
  189.4 6.2 %collective-permute-start.73 = (bf16[4,768,256]{2,1,0:T(8,128)(2,1)S(1)}, bf16[4,768,256]{2,1,0:T(8,128)(2,1)S(1)}, u32[]{:S(2)}, u32[]{:S(2)}) collective-permute-start(bf16[4,768,256]{2,1,0:T(8,128)(2,1)S(1)} %get-tuple-element.301), channel_id=1, source_target_pairs={{0,1},{1,0},{2,3},{3,2},{4,5},{5,4},{6,7},{7,6},{8,9},{9,8},{10,11... | collective-permute-start | bytes 4718600 | tf_op jit(solution)/shard_map/ppermute | solution.py:1236
  194.2 15.6 %collective-permute-start.81 = (bf16[384,256]{1,0:T(8,128)(2,1)S(1)}, bf16[384,256]{1,0:T(8,128)(2,1)S(1)}, u32[]{:S(2)}, u32[]{:S(2)}) collective-permute-start(bf16[384,256]{1,0:T(8,128)(2,1)S(1)} %get-tuple-element.314), channel_id=1, source_target_pairs={{0,4},{2,6},{4,0},{6,2},{1,5},{3,7},{5,1},{7,3},{8,12},{10,14},{12... | collective-permute-start | bytes 589832 | tf_op jit(solution)/shard_map/ppermute | solution.py:1236
  194.6 15.3 %collective-permute-start.82 = (bf16[384,256]{1,0:T(8,128)(2,1)S(1)}, bf16[384,256]{1,0:T(8,128)(2,1)S(1)}, u32[]{:S(2)}, u32[]{:S(2)}) collective-permute-start(bf16[384,256]{1,0:T(8,128)(2,1)S(1)} %get-tuple-element.315), channel_id=1, source_target_pairs={{0,2},{2,0},{4,6},{6,4},{1,3},{3,1},{5,7},{7,5},{8,10},{10,8},{12,... | collective-permute-start | bytes 589832 | tf_op jit(solution)/shard_map/ppermute | solution.py:1236
  201.4 26.7 %collective-permute-start.83 = (bf16[2,384,256]{2,1,0:T(8,128)(2,1)S(1)}, bf16[2,384,256]{2,1,0:T(8,128)(2,1)S(1)}, u32[]{:S(2)}, u32[]{:S(2)}) collective-permute-start(bf16[2,384,256]{2,1,0:T(8,128)(2,1)S(1)} %get-tuple-element.319), channel_id=1, source_target_pairs={{0,2},{2,0},{4,6},{6,4},{1,3},{3,1},{5,7},{7,5},{8,10},{10,8},{12,... | collective-permute-start | bytes 1179656 | tf_op jit(solution)/shard_map/ppermute | solution.py:1236
  202.9 25.2 %collective-permute-start.84 = (bf16[2,384,256]{2,1,0:T(8,128)(2,1)S(1)}, bf16[2,384,256]{2,1,0:T(8,128)(2,1)S(1)}, u32[]{:S(2)}, u32[]{:S(2)}) collective-permute-start(bf16[2,384,256]{2,1,0:T(8,128)(2,1)S(1)} %get-tuple-element.320), channel_id=1, source_target_pairs={{0,4},{2,6},{4,0},{6,2},{1,5},{3,7},{5,1},{7,3},{8,12},{10,14},{12... | collective-permute-start | bytes 1179656 | tf_op jit(solution)/shard_map/ppermute | solution.py:1236
  209.8 6.4 %collective-permute-start.79 = (f32[8,128]{1,0:T(8,128)S(1)}, f32[8,128]{1,0:T(8,128)S(1)}, u32[]{:S(2)}, u32[]{:S(2)}) collective-permute-start(f32[8,128]{1,0:T(8,128)S(1)} %add.319), channel_id=1, source_target_pairs={{0,16},{8,24},{16,0},{24,8},{1,17},{9,25},{17,1},{25,9},{2,18},{10... | collective-permute-start | bytes 12296 | tf_op jit(solution)/shard_map/ppermute | solution.py:1236
  209.9 18.0 %collective-permute-start.78 = (f32[8,128]{1,0:T(8,128)S(1)}, f32[8,128]{1,0:T(8,128)S(1)}, u32[]{:S(2)}, u32[]{:S(2)}) collective-permute-start(f32[8,128]{1,0:T(8,128)S(1)} %add.319), channel_id=1, source_target_pairs={{0,8},{8,0},{16,24},{24,16},{1,9},{9,1},{17,25},{25,17},{2,10},{10... | collective-permute-start | bytes 12296 | tf_op jit(solution)/shard_map/ppermute | solution.py:1236
  213.1 19.2 %collective-permute-start.88 = (bf16[64,512]{1,0:T(8,128)(2,1)S(1)}, bf16[64,512]{1,0:T(8,128)(2,1)S(1)}, u32[]{:S(2)}, u32[]{:S(2)}) collective-permute-start(bf16[64,512]{1,0:T(8,128)(2,1)S(1)} %get-tuple-element.324), channel_id=1, source_target_pairs={{0,2},{2,4},{4,6},{1,3},{3,5},{5,7},{8,10},{10,12},{12,14},{9,11},... | collective-permute-start | bytes 196616 | tf_op jit(solution)/shard_map/ppermute | solution.py:1217
  216.2 16.5 %collective-permute-start.89 = (bf16[64,512]{1,0:T(8,128)(2,1)S(1)}, bf16[64,512]{1,0:T(8,128)(2,1)S(1)}, u32[]{:S(2)}, u32[]{:S(2)}) collective-permute-start(bf16[64,512]{1,0:T(8,128)(2,1)S(1)} %get-tuple-element.325), channel_id=1, source_target_pairs={{2,0},{4,2},{6,4},{3,1},{5,3},{7,5},{10,8},{12,10},{14,12},{11,9},... | collective-permute-start | bytes 196616 | tf_op jit(solution)/shard_map/ppermute | solution.py:1218
  228.0 7.9 %collective-permute-start.90 = (bf16[256,512]{1,0:T(8,128)(2,1)S(1)}, bf16[256,512]{1,0:T(8,128)(2,1)S(1)}, u32[]{:S(2)}, u32[]{:S(2)}) collective-permute-start(bf16[256,512]{1,0:T(8,128)(2,1)S(1)} %get-tuple-element.326), channel_id=1, source_target_pairs={{0,1},{1,0},{2,3},{3,2},{4,5},{5,4},{6,7},{7,6},{8,9},{9,8},{10,11... | collective-permute-start | bytes 786440 | tf_op jit(solution)/shard_map/ppermute | solution.py:1212
  241.5 10.9 %collective-permute-start.98 = (bf16[4,1216,256]{2,1,0:T(8,128)(2,1)S(1)}, bf16[4,1216,256]{2,1,0:T(8,128)(2,1)S(1)}, u32[]{:S(2)}, u32[]{:S(2)}) collective-permute-start(bf16[4,1216,256]{2,1,0:T(8,128)(2,1)S(1)} %get-tuple-element.346), channel_id=1, source_target_pairs={{0,1},{1,0},{2,3},{3,2},{4,5},{5,4},{6,7},{7,6},{8,9},{9,8},{10,11... | collective-permute-start | bytes 7471112 | tf_op jit(solution)/shard_map/ppermute | solution.py:1236
  244.2 6.3 %collective-permute-start.94 = (f32[8,128]{1,0:T(8,128)S(1)}, f32[8,128]{1,0:T(8,128)S(1)}, u32[]{:S(2)}, u32[]{:S(2)}) collective-permute-start(f32[8,128]{1,0:T(8,128)S(1)} %add.326), channel_id=1, source_target_pairs={{0,2},{2,0},{4,6},{6,4},{1,3},{3,1},{5,7},{7,5},{8,10},{10,8},{12,... | collective-permute-start | bytes 12296 | tf_op jit(solution)/shard_map/ppermute | solution.py:1236
  246.3 6.1 %collective-permute-start.97 = (bf16[2,384,128]{2,1,0:T(8,128)(2,1)S(1)}, bf16[2,384,128]{2,1,0:T(8,128)(2,1)S(1)}, u32[]{:S(2)}, u32[]{:S(2)}) collective-permute-start(bf16[2,384,128]{2,1,0:T(8,128)(2,1)S(1)} %get-tuple-element.332), channel_id=1, source_target_pairs={{0,8},{8,0},{16,24},{24,16},{1,9},{9,1},{17,25},{25,17},{2,10},{10... | collective-permute-start | bytes 589832 | tf_op jit(solution)/shard_map/ppermute | solution.py:1236
  246.6 11.3 %collective-permute-start.102 = (bf16[64,256]{1,0:T(8,128)(2,1)S(1)}, bf16[64,256]{1,0:T(8,128)(2,1)S(1)}, u32[]{:S(2)}, u32[]{:S(2)}) collective-permute-start(bf16[64,256]{1,0:T(8,128)(2,1)S(1)} %get-tuple-element.349), channel_id=1, source_target_pairs={{0,2},{2,4},{4,6},{1,3},{3,5},{5,7},{8,10},{10,12},{12,14},{9,11},... | collective-permute-start | bytes 98312 | tf_op jit(solution)/shard_map/ppermute | solution.py:1217
  249.1 8.8 %collective-permute-start.103 = (bf16[64,256]{1,0:T(8,128)(2,1)S(1)}, bf16[64,256]{1,0:T(8,128)(2,1)S(1)}, u32[]{:S(2)}, u32[]{:S(2)}) collective-permute-start(bf16[64,256]{1,0:T(8,128)(2,1)S(1)} %get-tuple-element.350), channel_id=1, source_target_pairs={{2,0},{4,2},{6,4},{3,1},{5,3},{7,5},{10,8},{12,10},{14,12},{11,9},... | collective-permute-start | bytes 98312 | tf_op jit(solution)/shard_map/ppermute | solution.py:1218
  252.4 6.1 %collective-permute-start.101 = (f32[8,128]{1,0:T(8,128)S(1)}, f32[8,128]{1,0:T(8,128)S(1)}, u32[]{:S(2)}, u32[]{:S(2)}) collective-permute-start(f32[8,128]{1,0:T(8,128)S(1)} %add_add_fusion.10), channel_id=1, source_target_pairs={{0,24},{8,16},{16,8},{24,0},{1,25},{9,17},{17,9},{25,1},{2,26},{10... | collective-permute-start | bytes 12296 | tf_op jit(solution)/shard_map/ppermute | solution.py:1236
  261.9 9.5 %collective-permute-start.111 = (bf16[384,256]{1,0:T(8,128)(2,1)S(1)}, bf16[384,256]{1,0:T(8,128)(2,1)S(1)}, u32[]{:S(2)}, u32[]{:S(2)}) collective-permute-start(bf16[384,256]{1,0:T(8,128)(2,1)S(1)} %get-tuple-element.363), channel_id=1, source_target_pairs={{0,4},{2,6},{4,0},{6,2},{1,5},{3,7},{5,1},{7,3},{8,12},{10,14},{12... | collective-permute-start | bytes 589832 | tf_op jit(solution)/shard_map/ppermute | solution.py:1236
  264.2 7.2 %collective-permute-start.112 = (bf16[384,256]{1,0:T(8,128)(2,1)S(1)}, bf16[384,256]{1,0:T(8,128)(2,1)S(1)}, u32[]{:S(2)}, u32[]{:S(2)}) collective-permute-start(bf16[384,256]{1,0:T(8,128)(2,1)S(1)} %get-tuple-element.364), channel_id=1, source_target_pairs={{0,2},{2,0},{4,6},{6,4},{1,3},{3,1},{5,7},{7,5},{8,10},{10,8},{12,... | collective-permute-start | bytes 589832 | tf_op jit(solution)/shard_map/ppermute | solution.py:1236
  270.1 50.2 %collective-permute-start.116 = (bf16[384,128]{1,0:T(8,128)(2,1)S(1)}, bf16[384,128]{1,0:T(8,128)(2,1)S(1)}, u32[]{:S(2)}, u32[]{:S(2)}) collective-permute-start(bf16[384,128]{1,0:T(8,128)(2,1)S(1)} %get-tuple-element.381), channel_id=1, source_target_pairs={{0,16},{8,24},{16,0},{24,8},{1,17},{9,25},{17,1},{25,9},{2,18},{10... | collective-permute-start | bytes 294920 | tf_op jit(solution)/shard_map/ppermute | solution.py:1236
  278.1 13.2 %collective-permute-start.119 = (bf16[2,608,256]{2,1,0:T(8,128)(2,1)S(1)}, bf16[2,608,256]{2,1,0:T(8,128)(2,1)S(1)}, u32[]{:S(2)}, u32[]{:S(2)}) collective-permute-start(bf16[2,608,256]{2,1,0:T(8,128)(2,1)S(1)} %get-tuple-element.396), channel_id=1, source_target_pairs={{0,2},{2,0},{4,6},{6,4},{1,3},{3,1},{5,7},{7,5},{8,10},{10,8},{12,... | collective-permute-start | bytes 1867784 | tf_op jit(solution)/shard_map/ppermute | solution.py:1236
  278.6 12.8 %collective-permute-start.120 = (bf16[2,608,256]{2,1,0:T(8,128)(2,1)S(1)}, bf16[2,608,256]{2,1,0:T(8,128)(2,1)S(1)}, u32[]{:S(2)}, u32[]{:S(2)}) collective-permute-start(bf16[2,608,256]{2,1,0:T(8,128)(2,1)S(1)} %get-tuple-element.398), channel_id=1, source_target_pairs={{0,4},{2,6},{4,0},{6,2},{1,5},{3,7},{5,1},{7,3},{8,12},{10,14},{12... | collective-permute-start | bytes 1867784 | tf_op jit(solution)/shard_map/ppermute | solution.py:1236
  281.6 20.9 %collective-permute-start.125 = (bf16[4,640,256]{2,1,0:T(8,128)(2,1)S(1)}, bf16[4,640,256]{2,1,0:T(8,128)(2,1)S(1)}, u32[]{:S(2)}, u32[]{:S(2)}) collective-permute-start(bf16[4,640,256]{2,1,0:T(8,128)(2,1)S(1)} %get-tuple-element.375), channel_id=1, source_target_pairs={{0,1},{1,0},{2,3},{3,2},{4,5},{5,4},{6,7},{7,6},{8,9},{9,8},{10,11... | collective-permute-start | bytes 3932168 | tf_op jit(solution)/shard_map/ppermute | solution.py:1236
  292.3 7.0 %collective-permute-start.121 = (bf16[608,256]{1,0:T(8,128)(2,1)S(1)}, bf16[608,256]{1,0:T(8,128)(2,1)S(1)}, u32[]{:S(2)}, u32[]{:S(2)}) collective-permute-start(bf16[608,256]{1,0:T(8,128)(2,1)S(1)} %get-tuple-element.400), channel_id=1, source_target_pairs={{0,4},{2,6},{4,0},{6,2},{1,5},{3,7},{5,1},{7,3},{8,12},{10,14},{12... | collective-permute-start | bytes 933896 | tf_op jit(solution)/shard_map/ppermute | solution.py:1236
  292.9 6.9 %collective-permute-start.122 = (bf16[608,256]{1,0:T(8,128)(2,1)S(1)}, bf16[608,256]{1,0:T(8,128)(2,1)S(1)}, u32[]{:S(2)}, u32[]{:S(2)}) collective-permute-start(bf16[608,256]{1,0:T(8,128)(2,1)S(1)} %get-tuple-element.402), channel_id=1, source_target_pairs={{0,2},{2,0},{4,6},{6,4},{1,3},{3,1},{5,7},{7,5},{8,10},{10,8},{12,... | collective-permute-start | bytes 933896 | tf_op jit(solution)/shard_map/ppermute | solution.py:1236
  295.2 12.4 %collective-permute-start.117 = (bf16[2,384,128]{2,1,0:T(8,128)(2,1)S(1)}, bf16[2,384,128]{2,1,0:T(8,128)(2,1)S(1)}, u32[]{:S(2)}, u32[]{:S(2)}) collective-permute-start(bf16[2,384,128]{2,1,0:T(8,128)(2,1)S(1)} %get-tuple-element.388), channel_id=1, source_target_pairs={{0,8},{8,0},{16,24},{24,16},{1,9},{9,1},{17,25},{25,17},{2,10},{10... | collective-permute-start | bytes 589832 | tf_op jit(solution)/shard_map/ppermute | solution.py:1236
  300.7 8.5 %collective-permute-start.123 = (bf16[2,704,128]{2,1,0:T(8,128)(2,1)S(1)}, bf16[2,704,128]{2,1,0:T(8,128)(2,1)S(1)}, u32[]{:S(2)}, u32[]{:S(2)}) collective-permute-start(bf16[2,704,128]{2,1,0:T(8,128)(2,1)S(1)} %get-tuple-element.404), channel_id=1, source_target_pairs={{0,8},{8,0},{16,24},{24,16},{1,9},{9,1},{17,25},{25,17},{2,10},{10... | collective-permute-start | bytes 1081352 | tf_op jit(solution)/shard_map/ppermute | solution.py:1236
  303.4 9.1 %collective-permute-start.126 = (bf16[640,256]{1,0:T(8,128)(2,1)S(1)}, bf16[640,256]{1,0:T(8,128)(2,1)S(1)}, u32[]{:S(2)}, u32[]{:S(2)}) collective-permute-start(bf16[640,256]{1,0:T(8,128)(2,1)S(1)} %get-tuple-element.409), channel_id=1, source_target_pairs={{0,2},{2,0},{4,6},{6,4},{1,3},{3,1},{5,7},{7,5},{8,10},{10,8},{12,... | collective-permute-start | bytes 983048 | tf_op jit(solution)/shard_map/ppermute | solution.py:1236
  304.9 11.2 %collective-permute-start.127 = (bf16[640,256]{1,0:T(8,128)(2,1)S(1)}, bf16[640,256]{1,0:T(8,128)(2,1)S(1)}, u32[]{:S(2)}, u32[]{:S(2)}) collective-permute-start(bf16[640,256]{1,0:T(8,128)(2,1)S(1)} %get-tuple-element.410), channel_id=1, source_target_pairs={{0,4},{2,6},{4,0},{6,2},{1,5},{3,7},{5,1},{7,3},{8,12},{10,14},{12... | collective-permute-start | bytes 983048 | tf_op jit(solution)/shard_map/ppermute | solution.py:1236
  307.6 8.6 %collective-permute-start.128 = (bf16[640,256]{1,0:T(8,128)(2,1)S(1)}, bf16[640,256]{1,0:T(8,128)(2,1)S(1)}, u32[]{:S(2)}, u32[]{:S(2)}) collective-permute-start(bf16[640,256]{1,0:T(8,128)(2,1)S(1)} %get-tuple-element.411), channel_id=1, source_target_pairs={{0,6},{2,4},{4,2},{6,0},{1,7},{3,5},{5,3},{7,1},{8,14},{10,12},{12... | collective-permute-start | bytes 983048 | tf_op jit(solution)/shard_map/ppermute | solution.py:1236
  309.2 14.1 %collective-permute-start.118 = (bf16[384,128]{1,0:T(8,128)(2,1)S(1)}, bf16[384,128]{1,0:T(8,128)(2,1)S(1)}, u32[]{:S(2)}, u32[]{:S(2)}) collective-permute-start(bf16[384,128]{1,0:T(8,128)(2,1)S(1)} %get-tuple-element.390), channel_id=1, source_target_pairs={{0,16},{8,24},{16,0},{24,8},{1,17},{9,25},{17,1},{25,9},{2,18},{10... | collective-permute-start | bytes 294920 | tf_op jit(solution)/shard_map/ppermute | solution.py:1236
  312.5 13.1 %collective-permute-start.124 = (bf16[704,128]{1,0:T(8,128)(2,1)S(1)}, bf16[704,128]{1,0:T(8,128)(2,1)S(1)}, u32[]{:S(2)}, u32[]{:S(2)}) collective-permute-start(bf16[704,128]{1,0:T(8,128)(2,1)S(1)} %get-tuple-element.406), channel_id=1, source_target_pairs={{0,16},{8,24},{16,0},{24,8},{1,17},{9,25},{17,1},{25,9},{2,18},{10... | collective-permute-start | bytes 540680 | tf_op jit(solution)/shard_map/ppermute | solution.py:1236
  317.0 8.6 %collective-permute-start.129 = (bf16[416,128]{1,0:T(8,128)(2,1)S(1)}, bf16[416,128]{1,0:T(8,128)(2,1)S(1)}, u32[]{:S(2)}, u32[]{:S(2)}) collective-permute-start(bf16[416,128]{1,0:T(8,128)(2,1)S(1)} %get-tuple-element.413), channel_id=1, source_target_pairs={{0,8},{8,0},{16,24},{24,16},{1,9},{9,1},{17,25},{25,17},{2,10},{10... | collective-permute-start | bytes 319496 | tf_op jit(solution)/shard_map/ppermute | solution.py:1236
  317.9 10.0 %collective-permute-start.130 = (bf16[416,128]{1,0:T(8,128)(2,1)S(1)}, bf16[416,128]{1,0:T(8,128)(2,1)S(1)}, u32[]{:S(2)}, u32[]{:S(2)}) collective-permute-start(bf16[416,128]{1,0:T(8,128)(2,1)S(1)} %get-tuple-element.414), channel_id=1, source_target_pairs={{0,16},{8,24},{16,0},{24,8},{1,17},{9,25},{17,1},{25,9},{2,18},{10... | collective-permute-start | bytes 319496 | tf_op jit(solution)/shard_map/ppermute | solution.py:1236
  320.3 7.6 %collective-permute-start.131 = (bf16[416,128]{1,0:T(8,128)(2,1)S(1)}, bf16[416,128]{1,0:T(8,128)(2,1)S(1)}, u32[]{:S(2)}, u32[]{:S(2)}) collective-permute-start(bf16[416,128]{1,0:T(8,128)(2,1)S(1)} %get-tuple-element.415), channel_id=1, source_target_pairs={{0,24},{8,16},{16,8},{24,0},{1,25},{9,17},{17,9},{25,1},{2,26},{10... | collective-permute-start | bytes 319496 | tf_op jit(solution)/shard_map/ppermute | solution.py:1236
  (96 other events, 483.3 us)
